TPU v7x, 32 devices: a whole 2x2x4 slice. The times are simulated.
32 devices in a mesh: dp: 8 (over z, x), tensor: 4 (over y, core).
Axes of the slice: x: 2, y: 2, z: 4, core: 2. Of those that a mesh axis runs over, the one named last changes fastest.
Arguments:
- hidden: bfloat16 [1024, 28672], P('dp', 'tensor'), may hold values from -6 to 6
- out_grad: bfloat16 [1024, 8192], P('dp'), may hold values from -6 to 6
- prev_hidden: bfloat16 [1024, 28672], P('dp', 'tensor'), may hold values from -6 to 6
- prev_grad: bfloat16 [1024, 8192], P('dp'), may hold values from -6 to 6
- prev_basis: float32 [28672, 32], P('tensor'), may hold values from -6 to 6
- warm_start: float32 [8192, 32], replicated, may hold values from -0.17 to 0.17
Outputs:
- new_basis: float32 [28672, 32], P('tensor')
- new_factor: float32 [8192, 32], P('dp')
All inputs are finite; a program needn't handle non-finite values.
Results may differ from a plain program's by a relative error of at most 0.007.
Values sent between devices are 32-bit elements; how exact they have to be, the bound alone decides.
No kernel may reach another device: no remote copies, remote signals or barrier semaphores. Data moves between devices by JAX's collectives and lax.ppermute only.
A program may use at most 64 MiB of HBM per device.

v0:
```python
import jax
import jax.numpy as jnp
from jax import lax
from jax.sharding import PartitionSpec as P

FF = 28672


def orthonormal(rows_in, gram_matrix, norm_scale):
    lower = jnp.linalg.cholesky(gram_matrix)
    return norm_scale * jax.scipy.linalg.solve_triangular(lower, rows_in.T, lower=True).T


def on_device(hidden, out_grad, prev_hidden, prev_grad, prev_basis, warm_start):
    highest = lax.Precision.HIGHEST
    replicas = lax.axis_size("dp")
    norm_scale = jnp.sqrt(jnp.float32(FF))
    warm_low = warm_start.astype(jnp.bfloat16)
    projected = jnp.dot(out_grad, warm_low, preferred_element_type=jnp.float32).astype(jnp.bfloat16)
    projected_prev = jnp.dot(prev_grad, warm_low, preferred_element_type=jnp.float32).astype(
        jnp.bfloat16
    )
    coupling = jnp.dot(warm_start.T, warm_start, precision=highest)
    summed = jnp.einsum("tf,tr->fr", hidden, projected, preferred_element_type=jnp.float32)
    summed = summed + jnp.einsum(
        "tf,tr->fr", prev_hidden, projected_prev, preferred_element_type=jnp.float32
    )
    local_p = (summed - jnp.dot(prev_basis, coupling, precision=highest)) / replicas
    p_mean = lax.psum(local_p, "dp")
    gram_matrix = lax.psum(jnp.dot(p_mean.T, p_mean, precision=highest), "tensor")
    new_basis = orthonormal(p_mean, gram_matrix, norm_scale)
    basis_low = new_basis.astype(jnp.bfloat16)
    pulled = jnp.dot(hidden, basis_low, preferred_element_type=jnp.float32).astype(jnp.bfloat16)
    pulled_prev = jnp.dot(prev_hidden, basis_low, preferred_element_type=jnp.float32).astype(
        jnp.bfloat16
    )
    cross_basis = jnp.dot(prev_basis.T, new_basis, precision=highest)
    summed_q = jnp.einsum("td,tr->dr", out_grad, pulled, preferred_element_type=jnp.float32)
    summed_q = summed_q + jnp.einsum(
        "td,tr->dr", prev_grad, pulled_prev, preferred_element_type=jnp.float32
    )
    local_q = (summed_q - jnp.dot(warm_start, cross_basis, precision=highest)) / replicas
    row_count = warm_start.shape[0] // replicas
    summed_all = lax.psum(local_q, ("dp", "tensor"))
    owned_rows = lax.dynamic_slice_in_dim(
        summed_all, lax.axis_index("dp") * row_count, row_count, 0
    )
    return (new_basis, owned_rows / norm_scale)


def solution(mesh):
    return jax.shard_map(
        on_device,
        mesh=mesh,
        in_specs=(
            P("dp", "tensor"),
            P("dp", None),
            P("dp", "tensor"),
            P("dp", None),
            P("tensor", None),
            P(),
        ),
        out_specs=(P("tensor", None), P("dp", None)),
        check_vma=False,
    )
```

profile of v0, /device:TPU:0, one launch (start us, length us, event | category | flops | bytes accessed | tf_op | source)
XLA Modules:
  0.0 273.8 jit_solution(12528383104815905478)
XLA Ops:
  7.2 0.0 all-reduce.3.cloned.1.call-start
  7.2 2.7 fusion.18
  9.9 3.9 %fusion.5 = f32[32,7168]{1,0:T(8,128)} fusion(bf16[128,7168]{1,0:T(8,128)(2,1)} %param.6, bf16[128,8192]{1,0:T(8,128)(2,1)S(1)} %copy-done, f32[8192,32]{0,1:T(8,128)S(1)} %copy-done.1), kind=kOutput, calls=%fused_computation.11 | convolution fusion | flops 126095360 | bytes 5898240 | tf_op jit(solution)/shard_map/tf,tr->fr/dot_general | solution.py:24
  13.9 4.8 %convolution_add_fusion.1 = f32[32,7168]{1,0:T(8,128)} fusion(f32[32,7168]{1,0:T(8,128)} %fusion.5, bf16[128,7168]{1,0:T(8,128)(2,1)} %param.8, bf16[128,8192]{1,0:T(8,128)(2,1)} %param.9, f32[8192,32]{0,1:T(8,128)S(1)} %copy-done.1), kind=kOutput, calls=%fused_computation.7 | convolution fusion | flops 126324736 | bytes 6815744 | tf_op jit(solution)/shard_map/tf,tr->fr/dot_general | solution.py:25
  18.7 3.3 %fusion.4 = f32[7168,32]{0,1:T(8,128)} fusion(f32[32,7168]{1,0:T(8,128)} %convolution_add_fusion.1, f32[32,32]{1,0:T(8,128)S(1)} %fusion.18, f32[7168,32]{0,1:T(8,128)} %param.10), kind=kOutput, calls=%fused_computation.8 | convolution fusion | flops 88539136 | bytes 2756608 | tf_op jit(solution)/shard_map/dot_general | solution.py:28
  22.0 0.0 all-reduce.3.cloned.1.call-update
  22.0 0.0 all-reduce.5.cloned.1.call-start
  22.1 79.2 %all-reduce.3.cloned.1.call-done = f32[7168,32]{0,1:T(8,128)} async-done(((f32[7168,32]{0,1:T(8,128)}), f32[7168,32]{0,1:T(8,128)}) %all-reduce.3.cloned.1.call-update) | async-done | bytes 917520 | tf_op jit(solution)/shard_map/psum | solution.py:29
  101.2 2.3 fusion.19
  103.6 10.1 %psum.22 = f32[32,32]{0,1:T(8,128)S(1)} all-reduce(f32[32,32]{0,1:T(8,128)S(1)} %fusion.19), channel_id=1, replica_groups=mesh['dp'=8,'tensor'=4] {'tensor'}, use_global_device_ids=true, to_apply=%region_1.0 | all-reduce | flops 1024 | bytes 8192 | tf_op jit(solution)/shard_map/psum | solution.py:30
  113.7 0.1 copy.9
  113.8 2.9 %cholesky.16 = f32[32,32]{1,0:T(8,128)S(1)} custom-call(f32[32,32]{1,0:T(8,128)S(1)} %fusion.17), custom_call_target="Cholesky" | custom-call | tf_op jit(solution)/shard_map/jit(cholesky)/cholesky | solution.py:10
  116.7 0.6 compare_reduce_fusion
  117.4 0.7 fusion.15
  118.0 2.4 custom-call.7
  120.5 2.2 convolution_multiply_fusion
  122.7 0.9 copy-done.2
  123.6 0.9 fusion.20
  124.5 4.3 %fusion.6 = f32[32,8192]{1,0:T(8,128)} fusion(bf16[128,8192]{1,0:T(8,128)(2,1)S(1)} %copy-done, bf16[128,7168]{1,0:T(8,128)(2,1)} %param.6, f32[7168,32]{0,1:T(8,128)} %copy-done.2), kind=kOutput, calls=%fused_computation.14 | convolution fusion | flops 126062592 | bytes 5898240 | tf_op jit(solution)/shard_map/td,tr->dr/dot_general | solution.py:38
  128.8 2.1 fusion.21
  130.8 5.5 %fusion.2 = f32[8192,32]{0,1:T(8,128)} fusion(f32[32,8192]{1,0:T(8,128)} %fusion.21, f32[32,8192]{1,0:T(8,128)} %fusion.6, bf16[128,8192]{1,0:T(8,128)(2,1)} %param.9, bf16[128,7168]{1,0:T(8,128)(2,1)} %param.8, f32[7168,32]{0,1:T(8,128)} %copy-done.2), kind=kOutput, calls=%fused_computation.3 | convolution fusion | flops 126849024 | bytes 7995392 | tf_op jit(solution)/shard_map/td,tr->dr/dot_general | solution.py:39
  136.3 0.0 all-reduce.5.cloned.1.call-update
  136.4 129.0 %all-reduce.5.cloned.1.call-done = f32[8192,32]{0,1:T(8,128)} async-done(((f32[8192,32]{0,1:T(8,128)}), f32[8192,32]{0,1:T(8,128)}) %all-reduce.5.cloned.1.call-update) | async-done | bytes 1048592 | tf_op jit(solution)/shard_map/psum | solution.py:44
  265.4 1.6 dynamic-slice_multiply_fusion
  (9 shorter events, 0.1 us)
Async XLA Ops:
  7.2 2.7 %copy-start = (bf16[128,8192]{1,0:T(8,128)(2,1)S(1)}, bf16[128,8192]{1,0:T(8,128)(2,1)}, u32[]{:S(2)}) copy-start(bf16[128,8192]{1,0:T(8,128)(2,1)} %param.7) | copy-start | bytes 6291460
  7.2 2.7 copy-start.1
  7.2 94.0 %all-reduce.3.cloned.1.call-start = ((), (), s32[]{:S(2)}) async-start(), calls=%async_computation | async-start | bytes 1835008 | tf_op jit(solution)/shard_map/psum | solution.py:29
  22.0 243.3 %all-reduce.5.cloned.1.call-start = ((), (), s32[]{:S(2)}) async-start(), calls=%async_computation.1 | async-start | bytes 2097152 | tf_op jit(solution)/shard_map/psum | solution.py:44
  120.5 3.1 %copy-start.3 = (f32[7168,32]{0,1:T(8,128)S(1)}, f32[7168,32]{0,1:T(8,128)}, u32[]{:S(2)}) copy-start(f32[7168,32]{0,1:T(8,128)} %param.10) | copy-start | bytes 2752516
  122.7 0.9 copy-start.2
Sparse Core Ops, SparseCore 0:
  22.1 79.0 all-reduce.2
  136.5 128.8 all-reduce.4
where the time goes:
time: 274 us
  waiting for transfers between devices  208 us (76%)
  matrix products  32 us (12%)
  between operations  14.1 us (5%)
  blocking collectives  10.1 us (4%)
  other arithmetic  8.26 us (3%)
    psum x1, waiting for transfers between devices, on_device(): summed_all = lax.psum(local_q, ('dp', 'tensor'))  129 us
    psum x1, waiting for transfers between devices, on_device(): p_mean = lax.psum(local_p, 'dp')  79.2 us
    psum x1, blocking collectives, on_device(): lax.psum(jnp.dot(p_mean.T, p_mean, precision=highest), 'tensor')  10.1 us
    dot_general x1, matrix products, on_device(): jnp.einsum('td,tr->dr', prev_grad, pulled_prev, preferred_element_type=jn...  5.52 us
  transfers between devices with their start and end apart: 2, of which 2 were waited for; matrix products, arithmetic and copies ran while one was open for 0% of the time, Pallas kernels for 0%

commit v1 on v0

v1 whole, which is shorter than its diff:
```python
import functools

import jax
import jax.numpy as jnp
from jax import lax
from jax.experimental import pallas as pl
from jax.experimental.pallas import tpu as pltpu
from jax.sharding import PartitionSpec as P

F32 = jnp.float32
BF16 = jnp.bfloat16
SQUARE = 4
NT = (((1,), (1,)), ((), ()))
NN = (((1,), (0,)), ((), ()))
VMEM_SPEC = pl.BlockSpec(memory_space=pltpu.VMEM)
ANY_SPEC = pl.BlockSpec(memory_space=pl.ANY)


def orthonormal(rows_in, gram_matrix, norm_scale):
    lower = jnp.linalg.cholesky(gram_matrix)
    return norm_scale * jax.scipy.linalg.solve_triangular(lower, rows_in.T, lower=True).T


def plain_on_device(hidden, out_grad, prev_hidden, prev_grad, prev_basis, warm_start, *, norm_scale):
    highest = lax.Precision.HIGHEST
    replicas = lax.axis_size("dp")
    warm_low = warm_start.astype(BF16)
    projected = jnp.dot(out_grad, warm_low, preferred_element_type=F32).astype(BF16)
    projected_prev = jnp.dot(prev_grad, warm_low, preferred_element_type=F32).astype(BF16)
    coupling = jnp.dot(warm_start.T, warm_start, precision=highest)
    summed = jnp.einsum("tf,tr->fr", hidden, projected, preferred_element_type=F32)
    summed = summed + jnp.einsum(
        "tf,tr->fr", prev_hidden, projected_prev, preferred_element_type=F32
    )
    local_p = (summed - jnp.dot(prev_basis, coupling, precision=highest)) / replicas
    p_mean = lax.psum(local_p, "dp")
    gram_matrix = lax.psum(jnp.dot(p_mean.T, p_mean, precision=highest), "tensor")
    new_basis = orthonormal(p_mean, gram_matrix, norm_scale)
    basis_low = new_basis.astype(BF16)
    pulled = jnp.dot(hidden, basis_low, preferred_element_type=F32).astype(BF16)
    pulled_prev = jnp.dot(prev_hidden, basis_low, preferred_element_type=F32).astype(BF16)
    cross_basis = jnp.dot(prev_basis.T, new_basis, precision=highest)
    summed_q = jnp.einsum("td,tr->dr", out_grad, pulled, preferred_element_type=F32)
    summed_q = summed_q + jnp.einsum(
        "td,tr->dr", prev_grad, pulled_prev, preferred_element_type=F32
    )
    local_q = (summed_q - jnp.dot(warm_start, cross_basis, precision=highest)) / replicas
    row_count = warm_start.shape[0] // replicas
    summed_all = lax.psum(local_q, ("dp", "tensor"))
    owned_rows = lax.dynamic_slice_in_dim(
        summed_all, lax.axis_index("dp") * row_count, row_count, 0
    )
    return (new_basis, owned_rows / norm_scale)


def split(x, terms):
    parts = []
    for i in range(terms):
        part = x.astype(BF16)
        parts.append(part)
        if i + 1 < terms:
            x = x - part.astype(F32)
    return parts


def dot(a, b, dims, precision=None):
    return lax.dot_general(a, b, dims, preferred_element_type=F32, precision=precision)


def chunks(extent, count):
    step = extent // count
    return [pl.ds(i * step, step) for i in range(count)]


def left_factor_kernel(w_ref, o_ref, o2_ref, h_ref, h2_ref, *refs):
    pieces, (wv, ov, hv, sem) = refs[:SQUARE], refs[SQUARE:]
    q = lax.axis_index("dp") % SQUARE
    rows = wv.shape[0] // SQUARE
    tokens = o_ref.shape[0]
    o_cuts, h_cuts = chunks(o_ref.shape[1], 4), chunks(h_ref.shape[1], 4)
    copies = []
    for m in range(SQUARE):
        copies.append(
            pltpu.make_async_copy(
                w_ref.at[pl.ds((q ^ m) * rows, rows), :], wv.at[pl.ds(m * rows, rows), :], sem.at[m]
            )
        )
    for i, cut in enumerate(o_cuts):
        for j, ref in enumerate((o_ref, o2_ref)):
            copies.append(
                pltpu.make_async_copy(
                    ref.at[:, cut], ov.at[pl.ds(j * tokens, tokens), cut], sem.at[4 + 2 * i + j]
                )
            )
    for i, cut in enumerate(h_cuts):
        for j, ref in enumerate((h_ref, h2_ref)):
            copies.append(
                pltpu.make_async_copy(
                    ref.at[:, cut], hv.at[pl.ds(j * tokens, tokens), cut], sem.at[12 + 2 * i + j]
                )
            )
    for copy in copies:
        copy.start()
    for copy in copies[:4]:
        copy.wait()
    projected = jnp.zeros((wv.shape[0], 2 * tokens), F32)
    for i, cut in enumerate(o_cuts):
        copies[4 + 2 * i].wait()
        copies[5 + 2 * i].wait()
        projected += dot(wv[:, cut].astype(BF16), ov[:, cut], NT)
    projected = projected.astype(BF16)
    for i, cut in enumerate(h_cuts):
        copies[12 + 2 * i].wait()
        copies[13 + 2 * i].wait()
        summed = dot(projected, hv[:, cut], NN)
        for m in range(SQUARE):
            pieces[m][:, cut] = summed[m * rows : (m + 1) * rows]


def feedback_kernel(w_ref, b_ref, out_ref, c_ref):
    q = lax.axis_index("dp") % SQUARE
    rows = out_ref.shape[0]
    rank = w_ref.shape[0]
    total = jnp.zeros((3 * rank, 3 * rank), F32)
    for cut in chunks(w_ref.shape[1], 4):
        stacked = jnp.concatenate(split(w_ref[:, cut], 3), axis=0)
        total += dot(stacked, stacked, NT)
    total = total[:rank] + total[rank : 2 * rank] + total[2 * rank :]
    c_ref[...] = total[:, :rank] + total[:, rank : 2 * rank] + total[:, 2 * rank :]
    own = c_ref[pl.ds(q * rows, rows), :]
    for cut in chunks(b_ref.shape[1], 4):
        out_ref[:, cut] = dot(own, b_ref[:, cut], NN, lax.Precision.HIGHEST)


def pull_kernel(s0, s1, s2, s3, h_ref, h2_ref, keep_ref, send_ref, v_ref):
    q = lax.axis_index("dp") % SQUARE
    core = lax.axis_index("tensor") % 2
    tokens = h_ref.shape[0]
    rows, half = s0.shape[0], keep_ref.shape[0]
    rank = SQUARE * rows
    now = jnp.zeros((2 * rank, tokens), F32)
    prev = jnp.zeros((2 * rank, tokens), F32)
    for cut in chunks(h_ref.shape[1], 4):
        p = jnp.concatenate([s[:, cut] for s in (s0, s1, s2, s3)], axis=0)
        stacked = jnp.concatenate(split(p, 2), axis=0)
        now += dot(stacked, h_ref[:, cut], NT)
        prev += dot(stacked, h2_ref[:, cut], NT)
    now = now[:rank] + now[rank:]
    prev = prev[:rank] + prev[rank:]
    for m in range(SQUARE):
        place = pl.ds((q ^ m) * rows, rows)
        v_ref[place, :tokens] = now[m * rows : (m + 1) * rows]
        v_ref[place, tokens:] = prev[m * rows : (m + 1) * rows]
    keep_ref[...] = v_ref[pl.ds(core * half, half), :]
    send_ref[...] = v_ref[pl.ds((1 - core) * half, half), :]


def push_kernel(keep_ref, got_ref, o_ref, o2_ref, *outs):
    me = lax.axis_index("dp")
    tokens = o_ref.shape[0]
    half, width = outs[0].shape[1:]
    v = jnp.concatenate(split(keep_ref[...] + got_ref[...], 2), axis=0)
    for m in range(SQUARE):
        for z in range(2):
            cut = pl.ds(pl.multiple_of((me ^ m ^ (SQUARE * z)) * width, width), width)
            both = dot(v[:, :tokens], o_ref[:, cut], NN) + dot(v[:, tokens:], o2_ref[:, cut], NN)
            outs[m][z] = both[:half] + both[half:]


def gram_kernel(s0, s1, s2, s3, b_ref, out_ref, p_ref):
    q = lax.axis_index("dp") % SQUARE
    rows = s0.shape[0]
    rank = SQUARE * rows
    for m, s in enumerate((s0, s1, s2, s3)):
        p_ref[pl.ds((q ^ m) * rows, rows), :] = s[...]
    total = jnp.zeros((3 * rank, 6 * rank), F32)
    for cut in chunks(b_ref.shape[1], 4):
        p = split(p_ref[:, cut], 3)
        b = split(b_ref[:, cut], 3)
        total += dot(jnp.concatenate(p, axis=0), jnp.concatenate(p + b, axis=0), NT)
    total = total[:rank] + total[rank : 2 * rank] + total[2 * rank :]
    gram = total[:, :rank] + total[:, rank : 2 * rank] + total[:, 2 * rank : 3 * rank]
    cross = total[:, 3 * rank : 4 * rank] + total[:, 4 * rank : 5 * rank] + total[:, 5 * rank :]
    out_ref[...] = jnp.zeros_like(out_ref)
    out_ref[:, :rank] = gram
    out_ref[:, rank : 2 * rank] = cross


def cholesky_kernel(in_ref, out_ref):
    rank = in_ref.shape[0]
    shape = in_ref.shape
    row = lax.broadcasted_iota(jnp.int32, shape, 0)
    lane = lax.broadcasted_iota(jnp.int32, shape, 1)
    a = jnp.where(lane == row + 2 * rank, 1.0, in_ref[...])
    for k in range(rank):
        pivot = a[k : k + 1, k : k + 1]
        scale = 1.0 / jnp.sqrt(pivot)
        top = a[k : k + 1, :] * scale
        below = jnp.where(row[:, :1] > k, a[:, k : k + 1] * scale, 0.0)
        a = jnp.where(row == k, top, a - below * top)
    out_ref[...] = a


def basis_kernel(s0, s1, s2, s3, l_ref, out_ref, p_ref, *, norm_scale):
    q = lax.axis_index("dp") % SQUARE
    rows = s0.shape[0]
    rank = SQUARE * rows
    inverse = l_ref[:, 2 * rank : 3 * rank] * norm_scale
    for m, s in enumerate((s0, s1, s2, s3)):
        p_ref[pl.ds((q ^ m) * rows, rows), :] = s[...]
    for cut in chunks(out_ref.shape[1], 4):
        out_ref[:, cut] = dot(inverse, p_ref[:, cut], NN, lax.Precision.HIGHEST)


def factor_kernel(t_ref, u_ref, l_ref, w_ref, out_ref, z_ref, wv, sem, *, replicas):
    core = lax.axis_index("tensor") % 2
    half, width = t_ref.shape
    rank = 2 * half
    start = pl.multiple_of(lax.axis_index("dp") * width, width)
    copy = pltpu.make_async_copy(w_ref.at[:, pl.ds(start, width)], wv, sem)
    copy.start()
    z_ref[pl.ds(core * half, half), :] = t_ref[...] * (1.0 / replicas)
    z_ref[pl.ds((1 - core) * half, half), :] = u_ref[...] * (1.0 / replicas)
    highest = lax.Precision.HIGHEST
    out = dot(l_ref[:, 2 * rank : 3 * rank], z_ref[...], NN, highest)
    copy.wait()
    out_ref[...] = out - dot(l_ref[:, rank : 2 * rank], wv[...], NN, highest)


def call(kernel, outs, specs, scratch=(), flops=0, moved=0):
    return pl.pallas_call(
        kernel,
        out_shape=[jax.ShapeDtypeStruct(shape, F32) for shape in outs],
        in_specs=specs,
        out_specs=[VMEM_SPEC] * len(outs),
        scratch_shapes=scratch,
        compiler_params=pltpu.CompilerParams(vmem_limit_bytes=32 << 20),
        cost_estimate=pl.CostEstimate(flops=flops, bytes_accessed=moved, transcendentals=0),
    )


def swap_dp(x, m):
    n = lax.axis_size("dp")
    return lax.ppermute(x, "dp", [(i, i ^ m) for i in range(n)])


def swap_tensor(x, m):
    n = lax.axis_size("tensor")
    return lax.ppermute(x, "tensor", [(i, i ^ m) for i in range(n)])


def swap_both(x, md, mt):
    n, k = lax.axis_size("dp"), lax.axis_size("tensor")
    pairs = [(i * k + t, (i ^ md) * k + (t ^ mt)) for i in range(n) for t in range(k)]
    return lax.ppermute(x, ("dp", "tensor"), pairs)


def on_device(hidden, out_grad, prev_hidden, prev_grad, prev_basis, warm_start, *, norm_scale):
    replicas = lax.axis_size("dp")
    tokens, units = hidden.shape
    width = out_grad.shape[1]
    rank = warm_start.shape[1]
    rows, half, owned = rank // SQUARE, rank // 2, width // replicas
    w, b = warm_start.T, prev_basis.T
    piece = (rows, units)

    terms = call(
        left_factor_kernel,
        [piece] * SQUARE,
        [ANY_SPEC] * 5,
        [
            pltpu.VMEM((rank, width), F32),
            pltpu.VMEM((2 * tokens, width), BF16),
            pltpu.VMEM((2 * tokens, units), BF16),
            pltpu.SemaphoreType.DMA((20,)),
        ],
        flops=4 * tokens * rank * (units + width),
        moved=4 * tokens * (units + width) + 4 * rank * (units + width),
    )(w, out_grad, prev_grad, hidden, prev_hidden)
    got = [swap_dp(terms[m], m) for m in range(1, SQUARE)]
    (feedback,) = call(
        feedback_kernel,
        [piece],
        [VMEM_SPEC] * 2,
        [pltpu.VMEM((rank, rank), F32)],
        flops=2 * rank * rank * (units + width),
        moved=4 * rank * (units + width),
    )(w, b)
    summed = terms[0] + got[0] + got[1] + got[2]
    own = (summed + swap_dp(summed, SQUARE)) * (1.0 / replicas) - feedback
    p = [own] + [swap_dp(own, m) for m in range(1, SQUARE)]

    keep, send = call(
        pull_kernel,
        [(half, 2 * tokens)] * 2,
        [VMEM_SPEC] * 6,
        [pltpu.VMEM((rank, 2 * tokens), F32)],
        flops=8 * tokens * rank * units,
        moved=4 * tokens * units + 4 * rank * units,
    )(*p, hidden, prev_hidden)
    other = swap_tensor(send, 1)
    (gram,) = call(
        gram_kernel,
        [(rank, 128)],
        [VMEM_SPEC] * 5,
        [pltpu.VMEM((rank, units), F32)],
        flops=4 * rank * rank * units,
        moved=8 * rank * units,
    )(*p, b)
    parts = call(
        push_kernel,
        [(2, half, owned)] * SQUARE,
        [VMEM_SPEC] * 4,
        flops=8 * tokens * half * width,
        moved=4 * tokens * width + 4 * half * width,
    )(keep, other, out_grad, prev_grad)
    came = [swap_dp(parts[m], m) for m in range(1, SQUARE)]

    gram = gram + swap_tensor(gram, 1)
    gram = gram + swap_tensor(gram, 2)
    (solved,) = call(
        cholesky_kernel, [(rank, 128)], [VMEM_SPEC], flops=rank**3, moved=8 * rank * 128
    )(gram)
    (basis,) = call(
        functools.partial(basis_kernel, norm_scale=norm_scale),
        [(rank, units)],
        [VMEM_SPEC] * 5,
        [pltpu.VMEM((rank, units), F32)],
        flops=2 * rank * rank * units,
        moved=8 * rank * units,
    )(*p, solved)

    near = parts[0][0] + came[0][0] + came[1][0] + came[2][0]
    far = parts[0][1] + came[0][1] + came[1][1] + came[2][1]
    mine = near + swap_both(far, SQUARE, 0) + swap_both(near, 0, 2) + swap_both(far, SQUARE, 2)
    (factor,) = call(
        functools.partial(factor_kernel, replicas=replicas),
        [(rank, owned)],
        [VMEM_SPEC] * 3 + [ANY_SPEC],
        [pltpu.VMEM((rank, owned), F32), pltpu.VMEM((rank, owned), F32), pltpu.SemaphoreType.DMA],
        flops=4 * rank * rank * owned,
        moved=12 * rank * owned,
    )(mine, swap_tensor(mine, 1), solved, w)
    return (basis.T, factor.T)


def fits(mesh, dp=8, tensor=4):
    return mesh.shape["dp"] == dp and mesh.shape["tensor"] == tensor


def solution(mesh):
    def whole(hidden, out_grad, prev_hidden, prev_grad, prev_basis, warm_start):
        norm_scale = float(prev_basis.shape[0]) ** 0.5
        body = on_device if fits(mesh) else plain_on_device
        return jax.shard_map(
            functools.partial(body, norm_scale=norm_scale),
            mesh=mesh,
            in_specs=(
                P("dp", "tensor"),
                P("dp", None),
                P("dp", "tensor"),
                P("dp", None),
                P("tensor", None),
                P(),
            ),
            out_specs=(P("tensor", None), P("dp", None)),
            check_vma=False,
        )(hidden, out_grad, prev_hidden, prev_grad, prev_basis, warm_start)

    return whole
```

time: 274 us -> 87.9 us (0.32)
  waiting for transfers between devices: 208 us -> 42 us
  matrix products: 32 us -> 0 us
  starting transfers between devices: 0.08 us -> 21.4 us
  Pallas kernels: 0 us -> 15.9 us
  between operations: 14.1 us -> 0.73 us
  blocking collectives: 10.1 us -> 0 us
  other arithmetic: 8.26 us -> 0.13 us
  local copies, waits for them, and re-layouts: 1.01 us -> 7.43 us
    psum x2 -> x0, waiting for transfers between devices: 208 us -> none  [the longest x1 129 us: on_device(): summed_all = lax.psum(local_q, ('dp', 'tensor'))]
    ppermute x0 -> x17, waiting for transfers between devices: none -> 42 us  [the longest x10 32.7 us: swap_dp(): return lax.ppermute(x, 'dp', [(i, i ^ m) for i in range(n)])]
    dot_general x9 -> x0, matrix products: 29.8 us -> none  [the longest x1 5.52 us: on_device(): jnp.einsum('td,tr->dr', prev_grad, pulled_prev, preferred_element_type=jn...]
    ppermute x0 -> x17, starting transfers between devices: none -> 21.4 us  [the longest x10 14.5 us: swap_dp(): return lax.ppermute(x, 'dp', [(i, i ^ m) for i in range(n)])]
    pallas_call x0 -> x8, Pallas kernels: none -> 15.9 us  [the longest x1 4.38 us: on_device(): call(left_factor_kernel, [piece] * SQUARE, [ANY_SPEC] * 5, [pltpu.VMEM((r...]
    psum x1 -> x0, blocking collectives: 10.1 us -> none  [on_device(): lax.psum(jnp.dot(p_mean.T, p_mean, precision=highest), 'tensor')]
    another operation x5 -> x0, other arithmetic: 6.68 us -> none  [the longest x3 3.59 us: orthonormal(): lower = jnp.linalg.cholesky(gram_matrix)]
    unnamed x8 -> x22, local copies, waits for them, and re-layouts: 0.93 us -> 7.43 us
  transfers between devices with their start and end apart: 2 -> 17, of which waited for: 2 -> 15; matrix products, arithmetic and copies ran while one was open for 0% -> 0% of each run, Pallas kernels for 0% -> 9%
where the time goes in v1:
time: 87.9 us; the launch traced here: 87.6 us
  waiting for transfers between devices  42 us (48%)
  starting transfers between devices  21.4 us (24%)
  Pallas kernels  15.9 us (18%)
  local copies, waits for them, and re-layouts  7.43 us (8%)
    ppermute x10, waiting for transfers between devices, swap_dp(): return lax.ppermute(x, 'dp', [(i, i ^ m) for i in range(n)])  32.7 us
    ppermute x10, starting transfers between devices, swap_dp(): return lax.ppermute(x, 'dp', [(i, i ^ m) for i in range(n)])  14.5 us
    unnamed x22, local copies, waits for them, and re-layouts  7.43 us
    ppermute x3, waiting for transfers between devices, swap_both(): return lax.ppermute(x, ('dp', 'tensor'), pairs)  5.1 us
    ppermute x3, starting transfers between devices, swap_both(): return lax.ppermute(x, ('dp', 'tensor'), pairs)  4.76 us
    pallas_call x1, Pallas kernels, on_device(): call(left_factor_kernel, [piece] * SQUARE, [ANY_SPEC] * 5, [pltpu.VMEM((r...  4.38 us
    ppermute x4, waiting for transfers between devices, swap_tensor(): return lax.ppermute(x, 'tensor', [(i, i ^ m) for i in range(n)])  4.23 us
    pallas_call x1, Pallas kernels, on_device(): call(cholesky_kernel, [(rank, 128)], [VMEM_SPEC], flops=rank ** 3, moved=...  3.01 us
  transfers between devices with their start and end apart: 17, of which 15 were waited for; matrix products, arithmetic and copies ran while one was open for 0% of the time, Pallas kernels for 9%

profile of v1, /device:TPU:0, one launch (start us, length us, event | category | flops | bytes accessed | tf_op | source)
XLA Modules:
  0.0 87.6 jit_solution(17983299178113731203)
XLA Ops:
  1.9 1.6 %copy-done.2 = bf16[128,8192]{1,0:T(8,128)(2,1)S(1)} copy-done((bf16[128,8192]{1,0:T(8,128)(2,1)S(1)}, bf16[128,8192]{1,0:T(8,128)(2,1)}, u32[]{:S(2)}) %copy-start.2) | copy-done | bytes 2097176
  3.5 1.6 %copy-done.4 = bf16[128,8192]{1,0:T(8,128)(2,1)S(1)} copy-done((bf16[128,8192]{1,0:T(8,128)(2,1)S(1)}, bf16[128,8192]{1,0:T(8,128)(2,1)}, u32[]{:S(2)}) %copy-start.4) | copy-done | bytes 2097176
  8.0 4.4 %shard_map.77 = (f32[8,7168]{1,0:T(8,128)S(1)}, f32[8,7168]{1,0:T(8,128)S(1)}, f32[8,7168]{1,0:T(8,128)S(1)}, f32[8,7168]{1,0:T(8,128)S(1)}) custom-call(f32[32,8192]{1,0:T(8,128)S(1)} %bitcast.8, bf16[128,8192]{1,0:T(8,128)(2,1)S(1)} %copy-done.2, bf16[128,8192]{1,0:T(8,128)(2,1)S(1)} %copy-done.4, bf16[128,7168]{1,0:T(8,128)(2,1)S(1)} %copy-done.6, ...), custom_call_target="tpu_custom_call" | custom-call | flops 251658240 | bytes 9830400 | tf_op jit(solution)/shard_map/pallas_call | solution.py:267
  12.4 3.0 %collective-permute-start = (f32[8,7168]{1,0:T(8,128)S(1)}, f32[8,7168]{1,0:T(8,128)S(1)}, u32[]{:S(2)}, u32[]{:S(2)}) collective-permute-start(f32[8,7168]{1,0:T(8,128)S(1)} %get-tuple-element.13), channel_id=1, source_target_pairs={{0,4},{4,0},{8,12},{12,8},{16,20},{20,16},{24,28},{28,24},{1,5},{5... | collective-permute-start | bytes 688136 | tf_op jit(solution)/shard_map/ppermute | solution.py:244
  15.4 1.6 %collective-permute-start.1 = (f32[8,7168]{1,0:T(8,128)S(1)}, f32[8,7168]{1,0:T(8,128)S(1)}, u32[]{:S(2)}, u32[]{:S(2)}) collective-permute-start(f32[8,7168]{1,0:T(8,128)S(1)} %get-tuple-element.14), channel_id=1, source_target_pairs={{0,8},{4,12},{8,0},{12,4},{16,24},{20,28},{24,16},{28,20},{1,9},{5... | collective-permute-start | bytes 688136 | tf_op jit(solution)/shard_map/ppermute | solution.py:244
  17.0 4.0 %collective-permute-done = f32[8,7168]{1,0:T(8,128)S(1)} collective-permute-done((f32[8,7168]{1,0:T(8,128)S(1)}, f32[8,7168]{1,0:T(8,128)S(1)}, u32[]{:S(2)}, u32[]{:S(2)}) %collective-permute-start) | collective-permute-done | bytes 229408 | tf_op jit(solution)/shard_map/ppermute | solution.py:244
  21.0 2.9 %collective-permute-done.1 = f32[8,7168]{1,0:T(8,128)S(1)} collective-permute-done((f32[8,7168]{1,0:T(8,128)S(1)}, f32[8,7168]{1,0:T(8,128)S(1)}, u32[]{:S(2)}, u32[]{:S(2)}) %collective-permute-start.1) | collective-permute-done | bytes 229408 | tf_op jit(solution)/shard_map/ppermute | solution.py:244
  24.0 3.3 %collective-permute-done.2 = f32[8,7168]{1,0:T(8,128)S(1)} collective-permute-done((f32[8,7168]{1,0:T(8,128)S(1)}, f32[8,7168]{1,0:T(8,128)S(1)}, u32[]{:S(2)}, u32[]{:S(2)}) %collective-permute-start.2) | collective-permute-done | bytes 229408 | tf_op jit(solution)/shard_map/ppermute | solution.py:244
  27.3 2.8 %collective-permute-start.3 = (f32[8,7168]{1,0:T(8,128)S(1)}, f32[8,7168]{1,0:T(8,128)S(1)}, u32[]{:S(2)}, u32[]{:S(2)}) collective-permute-start(f32[8,7168]{1,0:T(8,128)S(1)} %add_add_fusion), channel_id=1, source_target_pairs={{0,16},{4,20},{8,24},{12,28},{16,0},{20,4},{24,8},{28,12},{1,17},{... | collective-permute-start | bytes 688136 | tf_op jit(solution)/shard_map/ppermute | solution.py:244
  30.1 2.0 %shard_map.78 = f32[8,7168]{1,0:T(8,128)S(1)} custom-call(f32[32,8192]{1,0:T(8,128)S(1)} %bitcast.9, f32[32,7168]{1,0:T(8,128)S(1)} %bitcast.11), custom_call_target="tpu_custom_call" | custom-call | flops 31457280 | bytes 1966080 | tf_op jit(solution)/shard_map/pallas_call | solution.py:281
  32.1 7.5 %collective-permute-done.3 = f32[8,7168]{1,0:T(8,128)S(1)} collective-permute-done((f32[8,7168]{1,0:T(8,128)S(1)}, f32[8,7168]{1,0:T(8,128)S(1)}, u32[]{:S(2)}, u32[]{:S(2)}) %collective-permute-start.3) | collective-permute-done | bytes 229408 | tf_op jit(solution)/shard_map/ppermute | solution.py:244
  43.2 6.0 %collective-permute-done.6.s3 = f32[8,7168]{1,0:T(8,128)S(1)} collective-permute-done((f32[8,7168]{1,0:T(8,128)S(1)}, f32[8,7168]{1,0:T(8,128)S(1)}, u32[]{:S(2)}, u32[]{:S(2)}) %collective-permute-start.6) | collective-permute-done | bytes 229408 | tf_op jit(solution)/shard_map/ppermute | solution.py:244
  49.2 2.7 %collective-permute-done.5.s2 = f32[8,7168]{1,0:T(8,128)S(1)} collective-permute-done((f32[8,7168]{1,0:T(8,128)S(1)}, f32[8,7168]{1,0:T(8,128)S(1)}, u32[]{:S(2)}, u32[]{:S(2)}) %collective-permute-start.5) | collective-permute-done | bytes 229408 | tf_op jit(solution)/shard_map/ppermute | solution.py:244
  56.7 1.8 %collective-permute-start.11 = (f32[2,16,1024]{2,1,0:T(8,128)S(1)}, f32[2,16,1024]{2,1,0:T(8,128)S(1)}, u32[]{:S(2)}, u32[]{:S(2)}) collective-permute-start(f32[2,16,1024]{2,1,0:T(8,128)S(1)} %get-tuple-element.20), channel_id=1, source_target_pairs={{0,8},{4,12},{8,0},{12,4},{16,24},{20,28},{24,16},{28,20},{1,9},{5... | collective-permute-start | bytes 393224 | tf_op jit(solution)/shard_map/ppermute | solution.py:244
  59.0 2.1 %collective-permute-done.10 = f32[2,16,1024]{2,1,0:T(8,128)S(1)} collective-permute-done((f32[2,16,1024]{2,1,0:T(8,128)S(1)}, f32[2,16,1024]{2,1,0:T(8,128)S(1)}, u32[]{:S(2)}, u32[]{:S(2)}) %collective-permute-start.10) | collective-permute-done | bytes 131104 | tf_op jit(solution)/shard_map/ppermute | solution.py:244
  61.0 2.0 %collective-permute-done.11 = f32[2,16,1024]{2,1,0:T(8,128)S(1)} collective-permute-done((f32[2,16,1024]{2,1,0:T(8,128)S(1)}, f32[2,16,1024]{2,1,0:T(8,128)S(1)}, u32[]{:S(2)}, u32[]{:S(2)}) %collective-permute-start.11) | collective-permute-done | bytes 131104 | tf_op jit(solution)/shard_map/ppermute | solution.py:244
  63.1 2.0 %collective-permute-done.12 = f32[2,16,1024]{2,1,0:T(8,128)S(1)} collective-permute-done((f32[2,16,1024]{2,1,0:T(8,128)S(1)}, f32[2,16,1024]{2,1,0:T(8,128)S(1)}, u32[]{:S(2)}, u32[]{:S(2)}) %collective-permute-start.12) | collective-permute-done | bytes 131104 | tf_op jit(solution)/shard_map/ppermute | solution.py:244
  66.5 3.3 %collective-permute-start.15 = (f32[16,1024]{1,0:T(8,128)S(1)}, f32[16,1024]{1,0:T(8,128)S(1)}, u32[]{:S(2)}, u32[]{:S(2)}) collective-permute-start(f32[16,1024]{1,0:T(8,128)S(1)} %get-tuple-element.23), channel_id=1, source_target_pairs={{0,18},{1,19},{2,16},{3,17},{4,22},{5,23},{6,20},{7,21},{8,26},{9,... | collective-permute-start | bytes 196616 | tf_op jit(solution)/shard_map/ppermute | solution.py:255
  69.8 2.7 %collective-permute-done.15 = f32[16,1024]{1,0:T(8,128)S(1)} collective-permute-done((f32[16,1024]{1,0:T(8,128)S(1)}, f32[16,1024]{1,0:T(8,128)S(1)}, u32[]{:S(2)}, u32[]{:S(2)}) %collective-permute-start.15) | collective-permute-done | bytes 65568 | tf_op jit(solution)/shard_map/ppermute | solution.py:255
  72.5 2.4 %collective-permute-done.13 = f32[16,1024]{1,0:T(8,128)S(1)} collective-permute-done((f32[16,1024]{1,0:T(8,128)S(1)}, f32[16,1024]{1,0:T(8,128)S(1)}, u32[]{:S(2)}, u32[]{:S(2)}) %collective-permute-start.13) | collective-permute-done | bytes 65568 | tf_op jit(solution)/shard_map/ppermute | solution.py:255
  77.7 1.5 %collective-permute-start.8 = (f32[32,128]{1,0:T(8,128)S(1)}, f32[32,128]{1,0:T(8,128)S(1)}, u32[]{:S(2)}, u32[]{:S(2)}) collective-permute-start(f32[32,128]{1,0:T(8,128)S(1)} %add.59), channel_id=1, source_target_pairs={{0,2},{1,3},{2,0},{3,1},{4,6},{5,7},{6,4},{7,5},{8,10},{9,11},{10,... | collective-permute-start | bytes 49160 | tf_op jit(solution)/shard_map/ppermute | solution.py:249
  79.2 2.2 %collective-permute-done.8 = f32[32,128]{1,0:T(8,128)S(1)} collective-permute-done((f32[32,128]{1,0:T(8,128)S(1)}, f32[32,128]{1,0:T(8,128)S(1)}, u32[]{:S(2)}, u32[]{:S(2)}) %collective-permute-start.8) | collective-permute-done | bytes 16416 | tf_op jit(solution)/shard_map/ppermute | solution.py:249
  81.4 3.0 %shard_map.80.l_ref = f32[32,128]{1,0:T(8,128)S(1)} custom-call(f32[32,128]{1,0:T(8,128)S(1)} %add.60.in_ref), custom_call_target="tpu_custom_call" | custom-call | flops 32768 | bytes 32768 | tf_op jit(solution)/shard_map/pallas_call | solution.py:321
  84.4 1.9 %shard_map.81 = f32[32,7168]{1,0:T(8,128)} custom-call(f32[8,7168]{1,0:T(8,128)S(1)} %multiply_subtract_fusion.s0, f32[8,7168]{1,0:T(8,128)S(1)} %collective-permute-done.4.s1, f32[8,7168]{1,0:T(8,128)S(1)} %collective-permute-done.5.s2, f32[8,7168]{1,0:T(8,128)S(1)} %collective-permute-done.6.s3, f32[32,128]{1,0:T(8,128)S(1)} %shard_map.80.l_ref), custom_call_target="tpu_custom_call" | custom-call | flops 14680064 | bytes 1835008 | tf_op jit(solution)/shard_map/pallas_call | solution.py:324
  (46 shorter events, 18.7 us)
Async XLA Ops:
  1.9 1.6 %copy-start.2 = (bf16[128,8192]{1,0:T(8,128)(2,1)S(1)}, bf16[128,8192]{1,0:T(8,128)(2,1)}, u32[]{:S(2)}) copy-start(bf16[128,8192]{1,0:T(8,128)(2,1)} %o_ref.3) | copy-start | bytes 6291460
  8.0 22.1 %copy-start.10 = (f32[7168,32]{0,1:T(8,128)S(1)}, f32[7168,32]{0,1:T(8,128)}, u32[]{:S(2)}) copy-start(f32[7168,32]{0,1:T(8,128)} %param.10) | copy-start | bytes 2752516
  12.4 8.6 %collective-permute-start = (f32[8,7168]{1,0:T(8,128)S(1)}, f32[8,7168]{1,0:T(8,128)S(1)}, u32[]{:S(2)}, u32[]{:S(2)}) collective-permute-start(f32[8,7168]{1,0:T(8,128)S(1)} %get-tuple-element.13), channel_id=1, source_target_pairs={{0,4},{4,0},{8,12},{12,8},{16,20},{20,16},{24,28},{28,24},{1,5},{5... | collective-permute-start | bytes 688136 | tf_op jit(solution)/shard_map/ppermute | solution.py:244
  15.4 8.5 %collective-permute-start.1 = (f32[8,7168]{1,0:T(8,128)S(1)}, f32[8,7168]{1,0:T(8,128)S(1)}, u32[]{:S(2)}, u32[]{:S(2)}) collective-permute-start(f32[8,7168]{1,0:T(8,128)S(1)} %get-tuple-element.14), channel_id=1, source_target_pairs={{0,8},{4,12},{8,0},{12,4},{16,24},{20,28},{24,16},{28,20},{1,9},{5... | collective-permute-start | bytes 688136 | tf_op jit(solution)/shard_map/ppermute | solution.py:244
  17.0 10.2 %collective-permute-start.2 = (f32[8,7168]{1,0:T(8,128)S(1)}, f32[8,7168]{1,0:T(8,128)S(1)}, u32[]{:S(2)}, u32[]{:S(2)}) collective-permute-start(f32[8,7168]{1,0:T(8,128)S(1)} %get-tuple-element.15), channel_id=1, source_target_pairs={{0,12},{4,8},{8,4},{12,0},{16,28},{20,24},{24,20},{28,16},{1,13},{... | collective-permute-start | bytes 688136 | tf_op jit(solution)/shard_map/ppermute | solution.py:244
  27.2 24.9 %copy-start.7 = (bf16[128,7168]{1,0:T(8,128)(2,1)S(1)}, bf16[128,7168]{1,0:T(8,128)(2,1)}, u32[]{:S(2)}) copy-start(bf16[128,7168]{1,0:T(8,128)(2,1)} %h_ref.3) | copy-start | bytes 5505028
  27.2 24.9 %copy-start.9 = (bf16[128,7168]{1,0:T(8,128)(2,1)S(1)}, bf16[128,7168]{1,0:T(8,128)(2,1)}, u32[]{:S(2)}) copy-start(bf16[128,7168]{1,0:T(8,128)(2,1)} %h2_ref.3) | copy-start | bytes 5505028
  27.3 12.4 %collective-permute-start.3 = (f32[8,7168]{1,0:T(8,128)S(1)}, f32[8,7168]{1,0:T(8,128)S(1)}, u32[]{:S(2)}, u32[]{:S(2)}) collective-permute-start(f32[8,7168]{1,0:T(8,128)S(1)} %add_add_fusion), channel_id=1, source_target_pairs={{0,16},{4,20},{8,24},{12,28},{16,0},{20,4},{24,8},{28,12},{1,17},{... | collective-permute-start | bytes 688136 | tf_op jit(solution)/shard_map/ppermute | solution.py:244
  39.7 15.1 %copy-start.3 = (bf16[128,8192]{1,0:T(8,128)(2,1)S(1)}, bf16[128,8192]{1,0:T(8,128)(2,1)}, u32[]{:S(2)}) copy-start(bf16[128,8192]{1,0:T(8,128)(2,1)} %o_ref.3) | copy-start | bytes 6291460
  39.7 15.1 %copy-start.5 = (bf16[128,8192]{1,0:T(8,128)(2,1)S(1)}, bf16[128,8192]{1,0:T(8,128)(2,1)}, u32[]{:S(2)}) copy-start(bf16[128,8192]{1,0:T(8,128)(2,1)} %o2_ref.3) | copy-start | bytes 6291460
  39.7 9.5 %collective-permute-start.6 = (f32[8,7168]{1,0:T(8,128)S(1)}, f32[8,7168]{1,0:T(8,128)S(1)}, u32[]{:S(2)}, u32[]{:S(2)}) collective-permute-start(f32[8,7168]{1,0:T(8,128)S(1)} %multiply_subtract_fusion.s0), channel_id=1, source_target_pairs={{0,12},{4,8},{8,4},{12,0},{16,28},{20,24},{24,20},{28,16},{1,13},{... | collective-permute-start | bytes 688136 | tf_op jit(solution)/shard_map/ppermute | solution.py:244
  41.2 10.7 %collective-permute-start.5 = (f32[8,7168]{1,0:T(8,128)S(1)}, f32[8,7168]{1,0:T(8,128)S(1)}, u32[]{:S(2)}, u32[]{:S(2)}) collective-permute-start(f32[8,7168]{1,0:T(8,128)S(1)} %multiply_subtract_fusion.s0), channel_id=1, source_target_pairs={{0,8},{4,12},{8,0},{12,4},{16,24},{20,28},{24,16},{28,20},{1,9},{5... | collective-permute-start | bytes 688136 | tf_op jit(solution)/shard_map/ppermute | solution.py:244
  42.6 9.6 %collective-permute-start.4 = (f32[8,7168]{1,0:T(8,128)S(1)}, f32[8,7168]{1,0:T(8,128)S(1)}, u32[]{:S(2)}, u32[]{:S(2)}) collective-permute-start(f32[8,7168]{1,0:T(8,128)S(1)} %multiply_subtract_fusion.s0), channel_id=1, source_target_pairs={{0,4},{4,0},{8,12},{12,8},{16,20},{20,16},{24,28},{28,24},{1,5},{5... | collective-permute-start | bytes 688136 | tf_op jit(solution)/shard_map/ppermute | solution.py:244
  53.5 1.2 %collective-permute-start.9 = (f32[16,256]{1,0:T(8,128)S(1)}, f32[16,256]{1,0:T(8,128)S(1)}, u32[]{:S(2)}, u32[]{:S(2)}) collective-permute-start(f32[16,256]{1,0:T(8,128)S(1)} %get-tuple-element.17), channel_id=1, source_target_pairs={{0,1},{1,0},{2,3},{3,2},{4,5},{5,4},{6,7},{7,6},{8,9},{9,8},{10,11... | collective-permute-start | bytes 49160 | tf_op jit(solution)/shard_map/ppermute | solution.py:249
  55.5 5.6 %collective-permute-start.10 = (f32[2,16,1024]{2,1,0:T(8,128)S(1)}, f32[2,16,1024]{2,1,0:T(8,128)S(1)}, u32[]{:S(2)}, u32[]{:S(2)}) collective-permute-start(f32[2,16,1024]{2,1,0:T(8,128)S(1)} %get-tuple-element.19), channel_id=1, source_target_pairs={{0,4},{4,0},{8,12},{12,8},{16,20},{20,16},{24,28},{28,24},{1,5},{5... | collective-permute-start | bytes 393224 | tf_op jit(solution)/shard_map/ppermute | solution.py:244
  56.7 6.4 %collective-permute-start.11 = (f32[2,16,1024]{2,1,0:T(8,128)S(1)}, f32[2,16,1024]{2,1,0:T(8,128)S(1)}, u32[]{:S(2)}, u32[]{:S(2)}) collective-permute-start(f32[2,16,1024]{2,1,0:T(8,128)S(1)} %get-tuple-element.20), channel_id=1, source_target_pairs={{0,8},{4,12},{8,0},{12,4},{16,24},{20,28},{24,16},{28,20},{1,9},{5... | collective-permute-start | bytes 393224 | tf_op jit(solution)/shard_map/ppermute | solution.py:244
  58.4 6.6 %collective-permute-start.12 = (f32[2,16,1024]{2,1,0:T(8,128)S(1)}, f32[2,16,1024]{2,1,0:T(8,128)S(1)}, u32[]{:S(2)}, u32[]{:S(2)}) collective-permute-start(f32[2,16,1024]{2,1,0:T(8,128)S(1)} %get-tuple-element.21), channel_id=1, source_target_pairs={{0,12},{4,8},{8,4},{12,0},{16,28},{20,24},{24,20},{28,16},{1,13},{... | collective-permute-start | bytes 393224 | tf_op jit(solution)/shard_map/ppermute | solution.py:244
  65.1 21.2 %copy-start.1 = (f32[8192,32]{0,1:T(8,128)S(1)}, f32[8192,32]{0,1:T(8,128)}, u32[]{:S(2)}) copy-start(f32[8192,32]{0,1:T(8,128)} %param.11) | copy-start | bytes 3145732
  65.1 4.8 %collective-permute-start.14 = (f32[16,1024]{1,0:T(8,128)S(1)}, f32[16,1024]{1,0:T(8,128)S(1)}, u32[]{:S(2)}, u32[]{:S(2)}) collective-permute-start(f32[16,1024]{1,0:T(8,128)S(1)} %get-tuple-element.22), channel_id=1, source_target_pairs={{0,2},{1,3},{2,0},{3,1},{4,6},{5,7},{6,4},{7,5},{8,10},{9,11},{10,... | collective-permute-start | bytes 196616 | tf_op jit(solution)/shard_map/ppermute | solution.py:255
  66.5 6.1 %collective-permute-start.15 = (f32[16,1024]{1,0:T(8,128)S(1)}, f32[16,1024]{1,0:T(8,128)S(1)}, u32[]{:S(2)}, u32[]{:S(2)}) collective-permute-start(f32[16,1024]{1,0:T(8,128)S(1)} %get-tuple-element.23), channel_id=1, source_target_pairs={{0,18},{1,19},{2,16},{3,17},{4,22},{5,23},{6,20},{7,21},{8,26},{9,... | collective-permute-start | bytes 196616 | tf_op jit(solution)/shard_map/ppermute | solution.py:255
  69.8 5.2 %collective-permute-start.13 = (f32[16,1024]{1,0:T(8,128)S(1)}, f32[16,1024]{1,0:T(8,128)S(1)}, u32[]{:S(2)}, u32[]{:S(2)}) collective-permute-start(f32[16,1024]{1,0:T(8,128)S(1)} %get-tuple-element.23), channel_id=1, source_target_pairs={{0,16},{1,17},{2,18},{3,19},{4,20},{5,21},{6,22},{7,23},{8,24},{9,... | collective-permute-start | bytes 196616 | tf_op jit(solution)/shard_map/ppermute | solution.py:255
  75.0 11.3 %collective-permute-start.16 = (f32[16,1024]{1,0:T(8,128)S(1)}, f32[16,1024]{1,0:T(8,128)S(1)}, u32[]{:S(2)}, u32[]{:S(2)}) collective-permute-start(f32[16,1024]{1,0:T(8,128)S(1)} %add_add_fusion.1.t_ref), channel_id=1, source_target_pairs={{0,1},{1,0},{2,3},{3,2},{4,5},{5,4},{6,7},{7,6},{8,9},{9,8},{10,11... | collective-permute-start | bytes 196616 | tf_op jit(solution)/shard_map/ppermute | solution.py:249
  76.3 1.4 %collective-permute-start.7 = (f32[32,128]{1,0:T(8,128)S(1)}, f32[32,128]{1,0:T(8,128)S(1)}, u32[]{:S(2)}, u32[]{:S(2)}) collective-permute-start(f32[32,128]{1,0:T(8,128)S(1)} %shard_map.79), channel_id=1, source_target_pairs={{0,1},{1,0},{2,3},{3,2},{4,5},{5,4},{6,7},{7,6},{8,9},{9,8},{10,11... | collective-permute-start | bytes 49160 | tf_op jit(solution)/shard_map/ppermute | solution.py:249
  77.7 3.7 %collective-permute-start.8 = (f32[32,128]{1,0:T(8,128)S(1)}, f32[32,128]{1,0:T(8,128)S(1)}, u32[]{:S(2)}, u32[]{:S(2)}) collective-permute-start(f32[32,128]{1,0:T(8,128)S(1)} %add.59), channel_id=1, source_target_pairs={{0,2},{1,3},{2,0},{3,1},{4,6},{5,7},{6,4},{7,5},{8,10},{9,11},{10,... | collective-permute-start | bytes 49160 | tf_op jit(solution)/shard_map/ppermute | solution.py:249
  (4 other events, 5.8 us)

commit v2 on v1

--- a/solution.py
+++ b/solution.py
@@ -14,6 +14,7 @@
 NN = (((1,), (0,)), ((), ()))
 VMEM_SPEC = pl.BlockSpec(memory_space=pltpu.VMEM)
 ANY_SPEC = pl.BlockSpec(memory_space=pl.ANY)
+HBM_SPEC = pl.BlockSpec(memory_space=pltpu.HBM)
 
 
 def orthonormal(rows_in, gram_matrix, norm_scale):
@@ -155,7 +156,7 @@
     send_ref[...] = v_ref[pl.ds((1 - core) * half, half), :]
 
 
-def push_kernel(keep_ref, got_ref, o_ref, o2_ref, *outs):
+def push_kernel(keep_ref, got_ref, o_ref, o2_ref, after_ref, *outs):
     me = lax.axis_index("dp")
     tokens = o_ref.shape[0]
     half, width = outs[0].shape[1:]
@@ -201,40 +202,48 @@
     out_ref[...] = a
 
 
-def basis_kernel(s0, s1, s2, s3, l_ref, out_ref, p_ref, *, norm_scale):
+def near_far_kernel(a_ref, b_ref, c_ref, d_ref, after_ref, near_ref, far_ref):
+    near_ref[...] = a_ref[0] + b_ref[0] + c_ref[0] + d_ref[0]
+    far_ref[...] = a_ref[1] + b_ref[1] + c_ref[1] + d_ref[1]
+
+
+def total_kernel(a_ref, b_ref, c_ref, d_ref, after_ref, out_ref):
+    out_ref[...] = a_ref[...] + b_ref[...] + c_ref[...] + d_ref[...]
+
+
+def basis_kernel(s0, s1, s2, s3, l_ref, w_ref, out_ref, fix_ref, p_ref, *, norm_scale):
     q = lax.axis_index("dp") % SQUARE
     rows = s0.shape[0]
     rank = SQUARE * rows
+    width = fix_ref.shape[1]
+    highest = lax.Precision.HIGHEST
     inverse = l_ref[:, 2 * rank : 3 * rank] * norm_scale
     for m, s in enumerate((s0, s1, s2, s3)):
         p_ref[pl.ds((q ^ m) * rows, rows), :] = s[...]
     for cut in chunks(out_ref.shape[1], 4):
-        out_ref[:, cut] = dot(inverse, p_ref[:, cut], NN, lax.Precision.HIGHEST)
-
-
-def factor_kernel(t_ref, u_ref, l_ref, w_ref, out_ref, z_ref, wv, sem, *, replicas):
+        out_ref[:, cut] = dot(inverse, p_ref[:, cut], NN, highest)
+    own = pl.ds(pl.multiple_of(lax.axis_index("dp") * width, width), width)
+    fix_ref[...] = dot(l_ref[:, rank : 2 * rank], w_ref[:, own], NN, highest)
+
+
+def factor_kernel(t_ref, u_ref, l_ref, fix_ref, out_ref, z_ref, *, replicas):
     core = lax.axis_index("tensor") % 2
-    half, width = t_ref.shape
+    half = t_ref.shape[0]
     rank = 2 * half
-    start = pl.multiple_of(lax.axis_index("dp") * width, width)
-    copy = pltpu.make_async_copy(w_ref.at[:, pl.ds(start, width)], wv, sem)
-    copy.start()
-    z_ref[pl.ds(core * half, half), :] = t_ref[...] * (1.0 / replicas)
-    z_ref[pl.ds((1 - core) * half, half), :] = u_ref[...] * (1.0 / replicas)
-    highest = lax.Precision.HIGHEST
-    out = dot(l_ref[:, 2 * rank : 3 * rank], z_ref[...], NN, highest)
-    copy.wait()
-    out_ref[...] = out - dot(l_ref[:, rank : 2 * rank], wv[...], NN, highest)
-
-
-def call(kernel, outs, specs, scratch=(), flops=0, moved=0):
+    z_ref[pl.ds(core * half, half), :] = t_ref[...]
+    z_ref[pl.ds((1 - core) * half, half), :] = u_ref[...]
+    inverse = l_ref[:, 2 * rank : 3 * rank] * (1.0 / replicas)
+    out_ref[...] = dot(inverse, z_ref[...], NN, lax.Precision.HIGHEST) - fix_ref[...]
+
+
+def call(kernel, outs, specs, scratch=(), flops=0, moved=0, vmem=32 << 20):
     return pl.pallas_call(
         kernel,
         out_shape=[jax.ShapeDtypeStruct(shape, F32) for shape in outs],
         in_specs=specs,
         out_specs=[VMEM_SPEC] * len(outs),
         scratch_shapes=scratch,
-        compiler_params=pltpu.CompilerParams(vmem_limit_bytes=32 << 20),
+        compiler_params=pltpu.CompilerParams(vmem_limit_bytes=vmem),
         cost_estimate=pl.CostEstimate(flops=flops, bytes_accessed=moved, transcendentals=0),
     )
 
@@ -267,7 +276,7 @@
     terms = call(
         left_factor_kernel,
         [piece] * SQUARE,
-        [ANY_SPEC] * 5,
+        [HBM_SPEC] * 5,
         [
             pltpu.VMEM((rank, width), F32),
             pltpu.VMEM((2 * tokens, width), BF16),
@@ -276,6 +285,7 @@
         ],
         flops=4 * tokens * rank * (units + width),
         moved=4 * tokens * (units + width) + 4 * rank * (units + width),
+        vmem=60 << 20,
     )(w, out_grad, prev_grad, hidden, prev_hidden)
     got = [swap_dp(terms[m], m) for m in range(1, SQUARE)]
     (feedback,) = call(
@@ -310,10 +320,10 @@
     parts = call(
         push_kernel,
         [(2, half, owned)] * SQUARE,
-        [VMEM_SPEC] * 4,
+        [VMEM_SPEC] * 4 + [ANY_SPEC],
         flops=8 * tokens * half * width,
         moved=4 * tokens * width + 4 * half * width,
-    )(keep, other, out_grad, prev_grad)
+    )(keep, other, out_grad, prev_grad, gram)
     came = [swap_dp(parts[m], m) for m in range(1, SQUARE)]
 
     gram = gram + swap_tensor(gram, 1)
@@ -321,26 +331,41 @@
     (solved,) = call(
         cholesky_kernel, [(rank, 128)], [VMEM_SPEC], flops=rank**3, moved=8 * rank * 128
     )(gram)
-    (basis,) = call(
+    near, far = call(
+        near_far_kernel,
+        [(half, owned)] * 2,
+        [VMEM_SPEC] * 4 + [ANY_SPEC],
+        flops=6 * half * owned,
+        moved=40 * half * owned,
+    )(parts[0], *came, solved)
+    basis, fix = call(
         functools.partial(basis_kernel, norm_scale=norm_scale),
-        [(rank, units)],
-        [VMEM_SPEC] * 5,
+        [(rank, units), (rank, owned)],
+        [VMEM_SPEC] * 6,
         [pltpu.VMEM((rank, units), F32)],
         flops=2 * rank * rank * units,
         moved=8 * rank * units,
-    )(*p, solved)
-
-    near = parts[0][0] + came[0][0] + came[1][0] + came[2][0]
-    far = parts[0][1] + came[0][1] + came[1][1] + came[2][1]
-    mine = near + swap_both(far, SQUARE, 0) + swap_both(near, 0, 2) + swap_both(far, SQUARE, 2)
+    )(*p, solved, w)
+    far_far, near_up, far_up = (
+        swap_both(far, SQUARE, 2),
+        swap_both(near, 0, 2),
+        swap_both(far, SQUARE, 0),
+    )
+    (mine,) = call(
+        total_kernel,
+        [(half, owned)],
+        [VMEM_SPEC] * 4 + [ANY_SPEC],
+        flops=3 * half * owned,
+        moved=20 * half * owned,
+    )(near, far_far, near_up, far_up, fix)
     (factor,) = call(
         functools.partial(factor_kernel, replicas=replicas),
         [(rank, owned)],
-        [VMEM_SPEC] * 3 + [ANY_SPEC],
-        [pltpu.VMEM((rank, owned), F32), pltpu.VMEM((rank, owned), F32), pltpu.SemaphoreType.DMA],
-        flops=4 * rank * rank * owned,
+        [VMEM_SPEC] * 4,
+        [pltpu.VMEM((rank, owned), F32)],
+        flops=2 * rank * rank * owned,
         moved=12 * rank * owned,
-    )(mine, swap_tensor(mine, 1), solved, w)
+    )(mine, swap_tensor(mine, 1), solved, fix)
     return (basis.T, factor.T)
 
 

time: 87.9 us -> 76.3 us (0.87)
  local copies, waits for them, and re-layouts: 7.43 us -> 0.03 us
  waiting for transfers between devices: 42 us -> 35.9 us
  Pallas kernels: 15.9 us -> 17.7 us
  other arithmetic: 0.13 us -> 1.18 us
    unnamed x22 -> x12, local copies, waits for them, and re-layouts: 7.43 us -> 0.03 us
    ppermute x10, waiting for transfers between devices: 32.7 us -> 26.8 us  [swap_dp(): return lax.ppermute(x, 'dp', [(i, i ^ m) for i in range(n)])]
    pallas_call x2 -> x4, Pallas kernels: 5.06 us -> 7.2 us  [the longest x1 6.46 us: on_device(): call(left_factor_kernel, [piece] * SQUARE, [HBM_SPEC] * 5, [pltpu.VMEM((r...]
    add x1, other arithmetic: 0.04 us -> 1.13 us  [on_device(): summed = terms[0] + got[0] + got[1] + got[2]]
    ppermute x3, waiting for transfers between devices: 5.1 us -> 4.2 us  [swap_both(): return lax.ppermute(x, ('dp', 'tensor'), pairs)]
  transfers between devices with their start and end apart: 17 -> 17, of which waited for: 15 -> 12; matrix products, arithmetic and copies ran while one was open for 0% -> 0% of each run, Pallas kernels for 9% -> 11%
where the time goes in v2:
time: 76.3 us; the launch traced here: 76.2 us
  waiting for transfers between devices  35.9 us (47%)
  starting transfers between devices  20.6 us (27%)
  Pallas kernels  17.7 us (23%)
  other arithmetic  1.18 us (2%)
    ppermute x10, waiting for transfers between devices, swap_dp(): return lax.ppermute(x, 'dp', [(i, i ^ m) for i in range(n)])  26.8 us
    ppermute x10, starting transfers between devices, swap_dp(): return lax.ppermute(x, 'dp', [(i, i ^ m) for i in range(n)])  14.5 us
    pallas_call x1, Pallas kernels, on_device(): call(left_factor_kernel, [piece] * SQUARE, [HBM_SPEC] * 5, [pltpu.VMEM((r...  6.46 us
    ppermute x4, waiting for transfers between devices, swap_tensor(): return lax.ppermute(x, 'tensor', [(i, i ^ m) for i in range(n)])  4.86 us
    ppermute x3, starting transfers between devices, swap_both(): return lax.ppermute(x, ('dp', 'tensor'), pairs)  4.71 us
    ppermute x3, waiting for transfers between devices, swap_both(): return lax.ppermute(x, ('dp', 'tensor'), pairs)  4.2 us
    pallas_call x1, Pallas kernels, on_device(): call(cholesky_kernel, [(rank, 128)], [VMEM_SPEC], flops=rank ** 3, moved=...  3.01 us
    pallas_call x1, Pallas kernels, on_device(): call(feedback_kernel, [piece], [VMEM_SPEC] * 2, [pltpu.VMEM((rank, rank),...  2.04 us
  transfers between devices with their start and end apart: 17, of which 12 were waited for; matrix products, arithmetic and copies ran while one was open for 0% of the time, Pallas kernels for 11%

profile of v2, /device:TPU:0, one launch (start us, length us, event | category | flops | bytes accessed | tf_op | source)
XLA Modules:
  0.0 76.2 jit_solution(18370684385158214595)
XLA Ops:
  0.6 6.5 %shard_map.77 = (f32[8,7168]{1,0:T(8,128)}, f32[8,7168]{1,0:T(8,128)}, f32[8,7168]{1,0:T(8,128)}, f32[8,7168]{1,0:T(8,128)}) custom-call(f32[32,8192]{1,0:T(8,128)} %bitcast.4, bf16[128,8192]{1,0:T(8,128)(2,1)} %o_ref.3, bf16[128,8192]{1,0:T(8,128)(2,1)} %o2_ref.3, bf16[128,7168]{1,0:T(8,128)(2,1)} %h_ref.3, bf16[128,7168]{1,0:T(8,128)(2,1)} %h2_ref.3), custom_call_target="tpu_custom_call" | custom-call | flops 251658240 | bytes 9830400 | tf_op jit(solution)/shard_map/pallas_call | solution.py:276
  7.1 3.0 %collective-permute-start = (f32[8,7168]{1,0:T(8,128)}, f32[8,7168]{1,0:T(8,128)S(1)}, u32[]{:S(2)}, u32[]{:S(2)}) collective-permute-start(f32[8,7168]{1,0:T(8,128)} %get-tuple-element.17), channel_id=1, source_target_pairs={{0,4},{4,0},{8,12},{12,8},{16,20},{20,16},{24,28},{28,24},{1,5},{5... | collective-permute-start | bytes 688136 | tf_op jit(solution)/shard_map/ppermute | solution.py:253
  10.1 1.6 %collective-permute-start.1 = (f32[8,7168]{1,0:T(8,128)}, f32[8,7168]{1,0:T(8,128)S(1)}, u32[]{:S(2)}, u32[]{:S(2)}) collective-permute-start(f32[8,7168]{1,0:T(8,128)} %get-tuple-element.18), channel_id=1, source_target_pairs={{0,8},{4,12},{8,0},{12,4},{16,24},{20,28},{24,16},{28,20},{1,9},{5... | collective-permute-start | bytes 688136 | tf_op jit(solution)/shard_map/ppermute | solution.py:253
  11.7 4.2 %collective-permute-done = f32[8,7168]{1,0:T(8,128)S(1)} collective-permute-done((f32[8,7168]{1,0:T(8,128)}, f32[8,7168]{1,0:T(8,128)S(1)}, u32[]{:S(2)}, u32[]{:S(2)}) %collective-permute-start) | collective-permute-done | bytes 229408 | tf_op jit(solution)/shard_map/ppermute | solution.py:253
  15.9 2.9 %collective-permute-done.1 = f32[8,7168]{1,0:T(8,128)S(1)} collective-permute-done((f32[8,7168]{1,0:T(8,128)}, f32[8,7168]{1,0:T(8,128)S(1)}, u32[]{:S(2)}, u32[]{:S(2)}) %collective-permute-start.1) | collective-permute-done | bytes 229408 | tf_op jit(solution)/shard_map/ppermute | solution.py:253
  18.9 3.3 %collective-permute-done.2 = f32[8,7168]{1,0:T(8,128)S(1)} collective-permute-done((f32[8,7168]{1,0:T(8,128)}, f32[8,7168]{1,0:T(8,128)S(1)}, u32[]{:S(2)}, u32[]{:S(2)}) %collective-permute-start.2) | collective-permute-done | bytes 229408 | tf_op jit(solution)/shard_map/ppermute | solution.py:253
  23.3 2.8 %collective-permute-start.3 = (f32[8,7168]{1,0:T(8,128)S(1)}, f32[8,7168]{1,0:T(8,128)S(1)}, u32[]{:S(2)}, u32[]{:S(2)}) collective-permute-start(f32[8,7168]{1,0:T(8,128)S(1)} %add_add_fusion), channel_id=1, source_target_pairs={{0,16},{4,20},{8,24},{12,28},{16,0},{20,4},{24,8},{28,12},{1,17},{... | collective-permute-start | bytes 688136 | tf_op jit(solution)/shard_map/ppermute | solution.py:253
  26.1 2.0 %shard_map.78 = f32[8,7168]{1,0:T(8,128)S(1)} custom-call(f32[32,8192]{1,0:T(8,128)S(1)} %bitcast.5, f32[32,7168]{1,0:T(8,128)S(1)} %bitcast.7), custom_call_target="tpu_custom_call" | custom-call | flops 31457280 | bytes 1966080 | tf_op jit(solution)/shard_map/pallas_call | solution.py:291
  28.1 7.5 %collective-permute-done.3 = f32[8,7168]{1,0:T(8,128)S(1)} collective-permute-done((f32[8,7168]{1,0:T(8,128)S(1)}, f32[8,7168]{1,0:T(8,128)S(1)}, u32[]{:S(2)}, u32[]{:S(2)}) %collective-permute-start.3) | collective-permute-done | bytes 229408 | tf_op jit(solution)/shard_map/ppermute | solution.py:253
  35.7 1.5 %collective-permute-start.6 = (f32[8,7168]{1,0:T(8,128)S(1)}, f32[8,7168]{1,0:T(8,128)S(1)}, u32[]{:S(2)}, u32[]{:S(2)}) collective-permute-start(f32[8,7168]{1,0:T(8,128)S(1)} %multiply_subtract_fusion.s0), channel_id=1, source_target_pairs={{0,12},{4,8},{8,4},{12,0},{16,28},{20,24},{24,20},{28,16},{1,13},{... | collective-permute-start | bytes 688136 | tf_op jit(solution)/shard_map/ppermute | solution.py:253
  37.2 1.4 %collective-permute-start.5 = (f32[8,7168]{1,0:T(8,128)S(1)}, f32[8,7168]{1,0:T(8,128)S(1)}, u32[]{:S(2)}, u32[]{:S(2)}) collective-permute-start(f32[8,7168]{1,0:T(8,128)S(1)} %multiply_subtract_fusion.s0), channel_id=1, source_target_pairs={{0,8},{4,12},{8,0},{12,4},{16,24},{20,28},{24,16},{28,20},{1,9},{5... | collective-permute-start | bytes 688136 | tf_op jit(solution)/shard_map/ppermute | solution.py:253
  39.2 6.0 %collective-permute-done.6.s3 = f32[8,7168]{1,0:T(8,128)S(1)} collective-permute-done((f32[8,7168]{1,0:T(8,128)S(1)}, f32[8,7168]{1,0:T(8,128)S(1)}, u32[]{:S(2)}, u32[]{:S(2)}) %collective-permute-start.6) | collective-permute-done | bytes 229408 | tf_op jit(solution)/shard_map/ppermute | solution.py:253
  45.2 2.7 %collective-permute-done.5.s2 = f32[8,7168]{1,0:T(8,128)S(1)} collective-permute-done((f32[8,7168]{1,0:T(8,128)S(1)}, f32[8,7168]{1,0:T(8,128)S(1)}, u32[]{:S(2)}, u32[]{:S(2)}) %collective-permute-start.5) | collective-permute-done | bytes 229408 | tf_op jit(solution)/shard_map/ppermute | solution.py:253
  48.2 1.4 %shard_map.82 = (f32[16,256]{1,0:T(8,128)S(1)}, f32[16,256]{1,0:T(8,128)S(1)}) custom-call(f32[8,7168]{1,0:T(8,128)S(1)} %multiply_subtract_fusion.s0, f32[8,7168]{1,0:T(8,128)S(1)} %collective-permute-done.4.s1, f32[8,7168]{1,0:T(8,128)S(1)} %collective-permute-done.5.s2, f32[8,7168]{1,0:T(8,128)S(1)} %collective-permute-done.6.s3, ...), custom_call_target="tpu_custom_call" | custom-call | flops 234881024 | bytes 4587520 | tf_op jit(solution)/shard_map/pallas_call | solution.py:303
  49.6 1.3 %shard_map.79.after_ref = f32[32,128]{1,0:T(8,128)S(1)} custom-call(f32[8,7168]{1,0:T(8,128)S(1)} %multiply_subtract_fusion.s0, f32[8,7168]{1,0:T(8,128)S(1)} %collective-permute-done.4.s1, f32[8,7168]{1,0:T(8,128)S(1)} %collective-permute-done.5.s2, f32[8,7168]{1,0:T(8,128)S(1)} %collective-permute-done.6.s3, f32[32,7168]{1,0:T(8,128)S(1)} %bitcast.8), custom_call_target="tpu_custom_call" | custom-call | flops 29360128 | bytes 1835008 | tf_op jit(solution)/shard_map/pallas_call | solution.py:312
  52.8 1.8 %collective-permute-start.11 = (f32[2,16,1024]{2,1,0:T(8,128)S(1)}, f32[2,16,1024]{2,1,0:T(8,128)S(1)}, u32[]{:S(2)}, u32[]{:S(2)}) collective-permute-start(f32[2,16,1024]{2,1,0:T(8,128)S(1)} %get-tuple-element.25), channel_id=1, source_target_pairs={{0,8},{4,12},{8,0},{12,4},{16,24},{20,28},{24,16},{28,20},{1,9},{5... | collective-permute-start | bytes 393224 | tf_op jit(solution)/shard_map/ppermute | solution.py:253
  56.3 1.3 %collective-permute-start.8 = (f32[32,128]{1,0:T(8,128)S(1)}, f32[32,128]{1,0:T(8,128)S(1)}, u32[]{:S(2)}, u32[]{:S(2)}) collective-permute-start(f32[32,128]{1,0:T(8,128)S(1)} %add.22), channel_id=1, source_target_pairs={{0,2},{1,3},{2,0},{3,1},{4,6},{5,7},{6,4},{7,5},{8,10},{9,11},{10,... | collective-permute-start | bytes 49160 | tf_op jit(solution)/shard_map/ppermute | solution.py:258
  57.6 2.4 %collective-permute-done.8 = f32[32,128]{1,0:T(8,128)S(1)} collective-permute-done((f32[32,128]{1,0:T(8,128)S(1)}, f32[32,128]{1,0:T(8,128)S(1)}, u32[]{:S(2)}, u32[]{:S(2)}) %collective-permute-start.8) | collective-permute-done | bytes 16416 | tf_op jit(solution)/shard_map/ppermute | solution.py:258
  60.0 3.0 %shard_map.80.l_ref.after_ref = f32[32,128]{1,0:T(8,128)S(1)} custom-call(f32[32,128]{1,0:T(8,128)S(1)} %add.23.in_ref), custom_call_target="tpu_custom_call" | custom-call | flops 32768 | bytes 32768 | tf_op jit(solution)/shard_map/pallas_call | solution.py:331
  63.1 1.4 %collective-permute-start.14 = (f32[16,1024]{1,0:T(8,128)S(1)}, f32[16,1024]{1,0:T(8,128)S(1)}, u32[]{:S(2)}, u32[]{:S(2)}) collective-permute-start(f32[16,1024]{1,0:T(8,128)S(1)} %get-tuple-element.27.a_ref), channel_id=1, source_target_pairs={{0,2},{1,3},{2,0},{3,1},{4,6},{5,7},{6,4},{7,5},{8,10},{9,11},{10,... | collective-permute-start | bytes 196616 | tf_op jit(solution)/shard_map/ppermute | solution.py:264
  64.5 3.3 %collective-permute-start.15 = (f32[16,1024]{1,0:T(8,128)S(1)}, f32[16,1024]{1,0:T(8,128)S(1)}, u32[]{:S(2)}, u32[]{:S(2)}) collective-permute-start(f32[16,1024]{1,0:T(8,128)S(1)} %get-tuple-element.28), channel_id=1, source_target_pairs={{0,16},{1,17},{2,18},{3,19},{4,20},{5,21},{6,22},{7,23},{8,24},{9,... | collective-permute-start | bytes 196616 | tf_op jit(solution)/shard_map/ppermute | solution.py:264
  67.8 1.9 %shard_map.81 = (f32[32,7168]{1,0:T(8,128)}, f32[32,1024]{1,0:T(8,128)S(1)}) custom-call(f32[8,7168]{1,0:T(8,128)S(1)} %multiply_subtract_fusion.s0, f32[8,7168]{1,0:T(8,128)S(1)} %collective-permute-done.4.s1, f32[8,7168]{1,0:T(8,128)S(1)} %collective-permute-done.5.s2, f32[8,7168]{1,0:T(8,128)S(1)} %collective-permute-done.6.s3, ...), custom_call_target="tpu_custom_call" | custom-call | flops 14680064 | bytes 1835008 | tf_op jit(solution)/shard_map/pallas_call | solution.py:341
  69.7 2.5 %collective-permute-done.15.d_ref = f32[16,1024]{1,0:T(8,128)S(1)} collective-permute-done((f32[16,1024]{1,0:T(8,128)S(1)}, f32[16,1024]{1,0:T(8,128)S(1)}, u32[]{:S(2)}, u32[]{:S(2)}) %collective-permute-start.15) | collective-permute-done | bytes 65568 | tf_op jit(solution)/shard_map/ppermute | solution.py:264
  72.2 1.7 %collective-permute-done.13.b_ref = f32[16,1024]{1,0:T(8,128)S(1)} collective-permute-done((f32[16,1024]{1,0:T(8,128)S(1)}, f32[16,1024]{1,0:T(8,128)S(1)}, u32[]{:S(2)}, u32[]{:S(2)}) %collective-permute-start.13) | collective-permute-done | bytes 65568 | tf_op jit(solution)/shard_map/ppermute | solution.py:264
  (36 shorter events, 8.1 us)
Async XLA Ops:
  0.6 25.5 %copy-start = (f32[8192,32]{0,1:T(8,128)S(1)}, f32[8192,32]{0,1:T(8,128)}, u32[]{:S(2)}) copy-start(f32[8192,32]{0,1:T(8,128)} %param.11) | copy-start | bytes 3145732
  0.6 25.4 %copy-start.5 = (f32[7168,32]{0,1:T(8,128)S(1)}, f32[7168,32]{0,1:T(8,128)}, u32[]{:S(2)}) copy-start(f32[7168,32]{0,1:T(8,128)} %param.10) | copy-start | bytes 2752516
  7.1 8.8 %collective-permute-start = (f32[8,7168]{1,0:T(8,128)}, f32[8,7168]{1,0:T(8,128)S(1)}, u32[]{:S(2)}, u32[]{:S(2)}) collective-permute-start(f32[8,7168]{1,0:T(8,128)} %get-tuple-element.17), channel_id=1, source_target_pairs={{0,4},{4,0},{8,12},{12,8},{16,20},{20,16},{24,28},{28,24},{1,5},{5... | collective-permute-start | bytes 688136 | tf_op jit(solution)/shard_map/ppermute | solution.py:253
  10.1 8.7 %collective-permute-start.1 = (f32[8,7168]{1,0:T(8,128)}, f32[8,7168]{1,0:T(8,128)S(1)}, u32[]{:S(2)}, u32[]{:S(2)}) collective-permute-start(f32[8,7168]{1,0:T(8,128)} %get-tuple-element.18), channel_id=1, source_target_pairs={{0,8},{4,12},{8,0},{12,4},{16,24},{20,28},{24,16},{28,20},{1,9},{5... | collective-permute-start | bytes 688136 | tf_op jit(solution)/shard_map/ppermute | solution.py:253
  11.7 10.4 %collective-permute-start.2 = (f32[8,7168]{1,0:T(8,128)}, f32[8,7168]{1,0:T(8,128)S(1)}, u32[]{:S(2)}, u32[]{:S(2)}) collective-permute-start(f32[8,7168]{1,0:T(8,128)} %get-tuple-element.19), channel_id=1, source_target_pairs={{0,12},{4,8},{8,4},{12,0},{16,28},{20,24},{24,20},{28,16},{1,13},{... | collective-permute-start | bytes 688136 | tf_op jit(solution)/shard_map/ppermute | solution.py:253
  22.1 26.0 %copy-start.3 = (bf16[128,7168]{1,0:T(8,128)(2,1)S(1)}, bf16[128,7168]{1,0:T(8,128)(2,1)}, u32[]{:S(2)}) copy-start(bf16[128,7168]{1,0:T(8,128)(2,1)} %h_ref.3) | copy-start | bytes 5505028
  22.1 26.0 %copy-start.4 = (bf16[128,7168]{1,0:T(8,128)(2,1)S(1)}, bf16[128,7168]{1,0:T(8,128)(2,1)}, u32[]{:S(2)}) copy-start(bf16[128,7168]{1,0:T(8,128)(2,1)} %h2_ref.3) | copy-start | bytes 5505028
  23.3 12.4 %collective-permute-start.3 = (f32[8,7168]{1,0:T(8,128)S(1)}, f32[8,7168]{1,0:T(8,128)S(1)}, u32[]{:S(2)}, u32[]{:S(2)}) collective-permute-start(f32[8,7168]{1,0:T(8,128)S(1)} %add_add_fusion), channel_id=1, source_target_pairs={{0,16},{4,20},{8,24},{12,28},{16,0},{20,4},{24,8},{28,12},{1,17},{... | collective-permute-start | bytes 688136 | tf_op jit(solution)/shard_map/ppermute | solution.py:253
  35.6 15.2 %copy-start.1 = (bf16[128,8192]{1,0:T(8,128)(2,1)S(1)}, bf16[128,8192]{1,0:T(8,128)(2,1)}, u32[]{:S(2)}) copy-start(bf16[128,8192]{1,0:T(8,128)(2,1)} %o_ref.3) | copy-start | bytes 6291460
  35.7 15.2 %copy-start.2 = (bf16[128,8192]{1,0:T(8,128)(2,1)S(1)}, bf16[128,8192]{1,0:T(8,128)(2,1)}, u32[]{:S(2)}) copy-start(bf16[128,8192]{1,0:T(8,128)(2,1)} %o2_ref.3) | copy-start | bytes 6291460
  35.7 9.5 %collective-permute-start.6 = (f32[8,7168]{1,0:T(8,128)S(1)}, f32[8,7168]{1,0:T(8,128)S(1)}, u32[]{:S(2)}, u32[]{:S(2)}) collective-permute-start(f32[8,7168]{1,0:T(8,128)S(1)} %multiply_subtract_fusion.s0), channel_id=1, source_target_pairs={{0,12},{4,8},{8,4},{12,0},{16,28},{20,24},{24,20},{28,16},{1,13},{... | collective-permute-start | bytes 688136 | tf_op jit(solution)/shard_map/ppermute | solution.py:253
  37.2 10.7 %collective-permute-start.5 = (f32[8,7168]{1,0:T(8,128)S(1)}, f32[8,7168]{1,0:T(8,128)S(1)}, u32[]{:S(2)}, u32[]{:S(2)}) collective-permute-start(f32[8,7168]{1,0:T(8,128)S(1)} %multiply_subtract_fusion.s0), channel_id=1, source_target_pairs={{0,8},{4,12},{8,0},{12,4},{16,24},{20,28},{24,16},{28,20},{1,9},{5... | collective-permute-start | bytes 688136 | tf_op jit(solution)/shard_map/ppermute | solution.py:253
  38.5 9.6 %collective-permute-start.4 = (f32[8,7168]{1,0:T(8,128)S(1)}, f32[8,7168]{1,0:T(8,128)S(1)}, u32[]{:S(2)}, u32[]{:S(2)}) collective-permute-start(f32[8,7168]{1,0:T(8,128)S(1)} %multiply_subtract_fusion.s0), channel_id=1, source_target_pairs={{0,4},{4,0},{8,12},{12,8},{16,20},{20,16},{24,28},{28,24},{1,5},{5... | collective-permute-start | bytes 688136 | tf_op jit(solution)/shard_map/ppermute | solution.py:253
  49.5 1.3 %collective-permute-start.9 = (f32[16,256]{1,0:T(8,128)S(1)}, f32[16,256]{1,0:T(8,128)S(1)}, u32[]{:S(2)}, u32[]{:S(2)}) collective-permute-start(f32[16,256]{1,0:T(8,128)S(1)} %get-tuple-element.22), channel_id=1, source_target_pairs={{0,1},{1,0},{2,3},{3,2},{4,5},{5,4},{6,7},{7,6},{8,9},{9,8},{10,11... | collective-permute-start | bytes 49160 | tf_op jit(solution)/shard_map/ppermute | solution.py:258
  51.6 11.5 %collective-permute-start.10 = (f32[2,16,1024]{2,1,0:T(8,128)S(1)}, f32[2,16,1024]{2,1,0:T(8,128)S(1)}, u32[]{:S(2)}, u32[]{:S(2)}) collective-permute-start(f32[2,16,1024]{2,1,0:T(8,128)S(1)} %get-tuple-element.24), channel_id=1, source_target_pairs={{0,4},{4,0},{8,12},{12,8},{16,20},{20,16},{24,28},{28,24},{1,5},{5... | collective-permute-start | bytes 393224 | tf_op jit(solution)/shard_map/ppermute | solution.py:253
  52.8 10.3 %collective-permute-start.11 = (f32[2,16,1024]{2,1,0:T(8,128)S(1)}, f32[2,16,1024]{2,1,0:T(8,128)S(1)}, u32[]{:S(2)}, u32[]{:S(2)}) collective-permute-start(f32[2,16,1024]{2,1,0:T(8,128)S(1)} %get-tuple-element.25), channel_id=1, source_target_pairs={{0,8},{4,12},{8,0},{12,4},{16,24},{20,28},{24,16},{28,20},{1,9},{5... | collective-permute-start | bytes 393224 | tf_op jit(solution)/shard_map/ppermute | solution.py:253
  54.5 8.5 %collective-permute-start.12 = (f32[2,16,1024]{2,1,0:T(8,128)S(1)}, f32[2,16,1024]{2,1,0:T(8,128)S(1)}, u32[]{:S(2)}, u32[]{:S(2)}) collective-permute-start(f32[2,16,1024]{2,1,0:T(8,128)S(1)} %get-tuple-element.26), channel_id=1, source_target_pairs={{0,12},{4,8},{8,4},{12,0},{16,28},{20,24},{24,20},{28,16},{1,13},{... | collective-permute-start | bytes 393224 | tf_op jit(solution)/shard_map/ppermute | solution.py:253
  55.1 1.2 %collective-permute-start.7 = (f32[32,128]{1,0:T(8,128)S(1)}, f32[32,128]{1,0:T(8,128)S(1)}, u32[]{:S(2)}, u32[]{:S(2)}) collective-permute-start(f32[32,128]{1,0:T(8,128)S(1)} %shard_map.79.after_ref), channel_id=1, source_target_pairs={{0,1},{1,0},{2,3},{3,2},{4,5},{5,4},{6,7},{7,6},{8,9},{9,8},{10,11... | collective-permute-start | bytes 49160 | tf_op jit(solution)/shard_map/ppermute | solution.py:258
  56.3 3.7 %collective-permute-start.8 = (f32[32,128]{1,0:T(8,128)S(1)}, f32[32,128]{1,0:T(8,128)S(1)}, u32[]{:S(2)}, u32[]{:S(2)}) collective-permute-start(f32[32,128]{1,0:T(8,128)S(1)} %add.22), channel_id=1, source_target_pairs={{0,2},{1,3},{2,0},{3,1},{4,6},{5,7},{6,4},{7,5},{8,10},{9,11},{10,... | collective-permute-start | bytes 49160 | tf_op jit(solution)/shard_map/ppermute | solution.py:258
  63.1 6.6 %collective-permute-start.14 = (f32[16,1024]{1,0:T(8,128)S(1)}, f32[16,1024]{1,0:T(8,128)S(1)}, u32[]{:S(2)}, u32[]{:S(2)}) collective-permute-start(f32[16,1024]{1,0:T(8,128)S(1)} %get-tuple-element.27.a_ref), channel_id=1, source_target_pairs={{0,2},{1,3},{2,0},{3,1},{4,6},{5,7},{6,4},{7,5},{8,10},{9,11},{10,... | collective-permute-start | bytes 196616 | tf_op jit(solution)/shard_map/ppermute | solution.py:264
  64.5 7.7 %collective-permute-start.15 = (f32[16,1024]{1,0:T(8,128)S(1)}, f32[16,1024]{1,0:T(8,128)S(1)}, u32[]{:S(2)}, u32[]{:S(2)}) collective-permute-start(f32[16,1024]{1,0:T(8,128)S(1)} %get-tuple-element.28), channel_id=1, source_target_pairs={{0,16},{1,17},{2,18},{3,19},{4,20},{5,21},{6,22},{7,23},{8,24},{9,... | collective-permute-start | bytes 196616 | tf_op jit(solution)/shard_map/ppermute | solution.py:264
  67.8 6.1 %collective-permute-start.13 = (f32[16,1024]{1,0:T(8,128)S(1)}, f32[16,1024]{1,0:T(8,128)S(1)}, u32[]{:S(2)}, u32[]{:S(2)}) collective-permute-start(f32[16,1024]{1,0:T(8,128)S(1)} %get-tuple-element.28), channel_id=1, source_target_pairs={{0,18},{1,19},{2,16},{3,17},{4,22},{5,23},{6,20},{7,21},{8,26},{9,... | collective-permute-start | bytes 196616 | tf_op jit(solution)/shard_map/ppermute | solution.py:264
  73.9 1.3 %collective-permute-start.16 = (f32[16,1024]{1,0:T(8,128)S(1)}, f32[16,1024]{1,0:T(8,128)S(1)}, u32[]{:S(2)}, u32[]{:S(2)}) collective-permute-start(f32[16,1024]{1,0:T(8,128)S(1)} %shard_map.85.t_ref), channel_id=1, source_target_pairs={{0,1},{1,0},{2,3},{3,2},{4,5},{5,4},{6,7},{7,6},{8,9},{9,8},{10,11... | collective-permute-start | bytes 196616 | tf_op jit(solution)/shard_map/ppermute | solution.py:258

commit v3 on v2

--- a/solution.py
+++ b/solution.py
@@ -73,12 +73,18 @@
     return [pl.ds(i * step, step) for i in range(count)]
 
 
-def left_factor_kernel(w_ref, o_ref, o2_ref, h_ref, h2_ref, *refs):
-    pieces, (wv, ov, hv, sem) = refs[:SQUARE], refs[SQUARE:]
+def store_pieces(pieces, cut, summed):
+    rows = pieces[0].shape[0]
+    for m, piece in enumerate(pieces):
+        piece[:, cut] = summed[m * rows : (m + 1) * rows]
+
+
+def first_term_kernel(w_ref, o_ref, o2_ref, h_ref, h2_ref, *refs):
+    pieces, y_ref, (wv, ov, hv, sem) = refs[:SQUARE], refs[SQUARE], refs[SQUARE + 1 :]
     q = lax.axis_index("dp") % SQUARE
     rows = wv.shape[0] // SQUARE
     tokens = o_ref.shape[0]
-    o_cuts, h_cuts = chunks(o_ref.shape[1], 4), chunks(h_ref.shape[1], 4)
+    o_cuts, h_cuts = chunks(o_ref.shape[1], 4), chunks(hv.shape[1], 2)
     copies = []
     for m in range(SQUARE):
         copies.append(
@@ -110,12 +116,35 @@
         copies[5 + 2 * i].wait()
         projected += dot(wv[:, cut].astype(BF16), ov[:, cut], NT)
     projected = projected.astype(BF16)
+    y_ref[...] = projected.astype(F32)
     for i, cut in enumerate(h_cuts):
         copies[12 + 2 * i].wait()
         copies[13 + 2 * i].wait()
-        summed = dot(projected, hv[:, cut], NN)
-        for m in range(SQUARE):
-            pieces[m][:, cut] = summed[m * rows : (m + 1) * rows]
+        store_pieces(pieces, cut, dot(projected, hv[:, cut], NN))
+
+
+def second_term_kernel(y_ref, h_ref, h2_ref, *refs):
+    pieces, (hv, sem) = refs[:SQUARE], refs[SQUARE:]
+    tokens, units = h_ref.shape
+    first = units - hv.shape[1]
+    cuts = chunks(hv.shape[1], 2)
+    copies = []
+    for i, cut in enumerate(cuts):
+        for j, ref in enumerate((h_ref, h2_ref)):
+            copies.append(
+                pltpu.make_async_copy(
+                    ref.at[:, pl.ds(first + cut.start, cut.size)],
+                    hv.at[pl.ds(j * tokens, tokens), cut],
+                    sem.at[2 * i + j],
+                )
+            )
+    for copy in copies:
+        copy.start()
+    projected = y_ref[...].astype(BF16)
+    for i, cut in enumerate(cuts):
+        copies[2 * i].wait()
+        copies[2 * i + 1].wait()
+        store_pieces(pieces, cut, dot(projected, hv[:, cut], NN))
 
 
 def feedback_kernel(w_ref, b_ref, out_ref, c_ref):
@@ -133,58 +162,81 @@
         out_ref[:, cut] = dot(own, b_ref[:, cut], NN, lax.Precision.HIGHEST)
 
 
-def pull_kernel(s0, s1, s2, s3, h_ref, h2_ref, keep_ref, send_ref, v_ref):
+def pulled_rows(pieces, h_ref, h2_ref, cuts):
+    rank, tokens = SQUARE * pieces[0].shape[0], h_ref.shape[0]
+    now = jnp.zeros((2 * rank, tokens), F32)
+    prev = jnp.zeros((2 * rank, tokens), F32)
+    for cut, units in cuts:
+        p = jnp.concatenate([s[:, cut] for s in pieces], axis=0)
+        stacked = jnp.concatenate(split(p, 2), axis=0)
+        now += dot(stacked, h_ref[:, units], NT)
+        prev += dot(stacked, h2_ref[:, units], NT)
+    both = jnp.concatenate([now, prev], axis=1)
+    return both[:rank] + both[rank:]
+
+
+def cuts_of(pieces, first, count):
+    cuts = chunks(pieces[0].shape[1], count)
+    return [(cut, pl.ds(first + cut.start, cut.size)) for cut in cuts]
+
+
+def first_pull_kernel(s0, s1, s2, s3, h_ref, h2_ref, b_ref, v_ref, g_ref, p_ref):
+    pieces = (s0, s1, s2, s3)
+    cuts = cuts_of(pieces, 0, 2)
+    v_ref[...] = pulled_rows(pieces, h_ref, h2_ref, cuts)
+    g_ref[...] = gram_terms(pieces, b_ref, p_ref, cuts)
+
+
+def pull_kernel(s0, s1, s2, s3, first_ref, h_ref, h2_ref, keep_ref, send_ref, v_ref):
     q = lax.axis_index("dp") % SQUARE
     core = lax.axis_index("tensor") % 2
-    tokens = h_ref.shape[0]
+    pieces = (s0, s1, s2, s3)
     rows, half = s0.shape[0], keep_ref.shape[0]
-    rank = SQUARE * rows
-    now = jnp.zeros((2 * rank, tokens), F32)
-    prev = jnp.zeros((2 * rank, tokens), F32)
-    for cut in chunks(h_ref.shape[1], 4):
-        p = jnp.concatenate([s[:, cut] for s in (s0, s1, s2, s3)], axis=0)
-        stacked = jnp.concatenate(split(p, 2), axis=0)
-        now += dot(stacked, h_ref[:, cut], NT)
-        prev += dot(stacked, h2_ref[:, cut], NT)
-    now = now[:rank] + now[rank:]
-    prev = prev[:rank] + prev[rank:]
+    first = h_ref.shape[1] - s0.shape[1]
+    both = first_ref[...] + pulled_rows(pieces, h_ref, h2_ref, cuts_of(pieces, first, 2))
     for m in range(SQUARE):
-        place = pl.ds((q ^ m) * rows, rows)
-        v_ref[place, :tokens] = now[m * rows : (m + 1) * rows]
-        v_ref[place, tokens:] = prev[m * rows : (m + 1) * rows]
+        v_ref[pl.ds((q ^ m) * rows, rows), :] = both[m * rows : (m + 1) * rows]
     keep_ref[...] = v_ref[pl.ds(core * half, half), :]
     send_ref[...] = v_ref[pl.ds((1 - core) * half, half), :]
 
 
-def push_kernel(keep_ref, got_ref, o_ref, o2_ref, after_ref, *outs):
+def ordered(pieces, p_ref):
+    q = lax.axis_index("dp") % SQUARE
+    rows = pieces[0].shape[0]
+    for m, s in enumerate(pieces):
+        p_ref[pl.ds((q ^ m) * rows, rows), :] = s[...]
+
+
+def gram_terms(pieces, b_ref, p_ref, cuts):
+    ordered(pieces, p_ref)
+    rank = SQUARE * pieces[0].shape[0]
+    total = jnp.zeros((3 * rank, 6 * rank), F32)
+    for cut, units in cuts:
+        p = split(p_ref[:, cut], 3)
+        b = split(b_ref[:, units], 3)
+        total += dot(jnp.concatenate(p, axis=0), jnp.concatenate(p + b, axis=0), NT)
+    total = total[:rank] + total[rank : 2 * rank] + total[2 * rank :]
+    gram = total[:, :rank] + total[:, rank : 2 * rank] + total[:, 2 * rank : 3 * rank]
+    cross = total[:, 3 * rank : 4 * rank] + total[:, 4 * rank : 5 * rank] + total[:, 5 * rank :]
+    return jnp.concatenate([gram, cross, jnp.zeros((rank, 128 - 2 * rank), F32)], axis=1)
+
+
+def gram_kernel(s0, s1, s2, s3, b_ref, first_ref, out_ref, p_ref):
+    pieces = (s0, s1, s2, s3)
+    first = b_ref.shape[1] - s0.shape[1]
+    out_ref[...] = first_ref[...] + gram_terms(pieces, b_ref, p_ref, cuts_of(pieces, first, 2))
+
+
+def push_kernel(mine_ref, got_ref, o_ref, o2_ref, after_ref, *outs):
     me = lax.axis_index("dp")
     tokens = o_ref.shape[0]
     half, width = outs[0].shape[1:]
-    v = jnp.concatenate(split(keep_ref[...] + got_ref[...], 2), axis=0)
+    v = jnp.concatenate(split(mine_ref[...] + got_ref[...], 2), axis=0)
     for m in range(SQUARE):
         for z in range(2):
             cut = pl.ds(pl.multiple_of((me ^ m ^ (SQUARE * z)) * width, width), width)
             both = dot(v[:, :tokens], o_ref[:, cut], NN) + dot(v[:, tokens:], o2_ref[:, cut], NN)
             outs[m][z] = both[:half] + both[half:]
-
-
-def gram_kernel(s0, s1, s2, s3, b_ref, out_ref, p_ref):
-    q = lax.axis_index("dp") % SQUARE
-    rows = s0.shape[0]
-    rank = SQUARE * rows
-    for m, s in enumerate((s0, s1, s2, s3)):
-        p_ref[pl.ds((q ^ m) * rows, rows), :] = s[...]
-    total = jnp.zeros((3 * rank, 6 * rank), F32)
-    for cut in chunks(b_ref.shape[1], 4):
-        p = split(p_ref[:, cut], 3)
-        b = split(b_ref[:, cut], 3)
-        total += dot(jnp.concatenate(p, axis=0), jnp.concatenate(p + b, axis=0), NT)
-    total = total[:rank] + total[rank : 2 * rank] + total[2 * rank :]
-    gram = total[:, :rank] + total[:, rank : 2 * rank] + total[:, 2 * rank : 3 * rank]
-    cross = total[:, 3 * rank : 4 * rank] + total[:, 4 * rank : 5 * rank] + total[:, 5 * rank :]
-    out_ref[...] = jnp.zeros_like(out_ref)
-    out_ref[:, :rank] = gram
-    out_ref[:, rank : 2 * rank] = cross
 
 
 def cholesky_kernel(in_ref, out_ref):
@@ -207,21 +259,21 @@
     far_ref[...] = a_ref[1] + b_ref[1] + c_ref[1] + d_ref[1]
 
 
-def total_kernel(a_ref, b_ref, c_ref, d_ref, after_ref, out_ref):
-    out_ref[...] = a_ref[...] + b_ref[...] + c_ref[...] + d_ref[...]
-
-
-def basis_kernel(s0, s1, s2, s3, l_ref, w_ref, out_ref, fix_ref, p_ref, *, norm_scale):
-    q = lax.axis_index("dp") % SQUARE
-    rows = s0.shape[0]
-    rank = SQUARE * rows
+def total_kernel(a_ref, b_ref, after_ref, out_ref):
+    out_ref[...] = a_ref[...] + b_ref[...]
+
+
+def basis_kernel(u0, u1, u2, u3, s0, s1, s2, s3, l_ref, w_ref, out_ref, fix_ref, p_ref, r_ref, *, norm_scale):
+    rank = l_ref.shape[0]
     width = fix_ref.shape[1]
     highest = lax.Precision.HIGHEST
     inverse = l_ref[:, 2 * rank : 3 * rank] * norm_scale
-    for m, s in enumerate((s0, s1, s2, s3)):
-        p_ref[pl.ds((q ^ m) * rows, rows), :] = s[...]
-    for cut in chunks(out_ref.shape[1], 4):
-        out_ref[:, cut] = dot(inverse, p_ref[:, cut], NN, highest)
+    first = 0
+    for pieces, ref in (((u0, u1, u2, u3), p_ref), ((s0, s1, s2, s3), r_ref)):
+        ordered(pieces, ref)
+        for cut, units in cuts_of(pieces, first, 2):
+            out_ref[:, units] = dot(inverse, ref[:, cut], NN, highest)
+        first += ref.shape[1]
     own = pl.ds(pl.multiple_of(lax.axis_index("dp") * width, width), width)
     fix_ref[...] = dot(l_ref[:, rank : 2 * rank], w_ref[:, own], NN, highest)
 
@@ -248,6 +300,10 @@
     )
 
 
+def in_hbm(x):
+    return pltpu.with_memory_space_constraint(x, pltpu.HBM)
+
+
 def swap_dp(x, m):
     n = lax.axis_size("dp")
     return lax.ppermute(x, "dp", [(i, i ^ m) for i in range(n)])
@@ -256,12 +312,6 @@
 def swap_tensor(x, m):
     n = lax.axis_size("tensor")
     return lax.ppermute(x, "tensor", [(i, i ^ m) for i in range(n)])
-
-
-def swap_both(x, md, mt):
-    n, k = lax.axis_size("dp"), lax.axis_size("tensor")
-    pairs = [(i * k + t, (i ^ md) * k + (t ^ mt)) for i in range(n) for t in range(k)]
-    return lax.ppermute(x, ("dp", "tensor"), pairs)
 
 
 def on_device(hidden, out_grad, prev_hidden, prev_grad, prev_basis, warm_start, *, norm_scale):
@@ -271,62 +321,91 @@
     rank = warm_start.shape[1]
     rows, half, owned = rank // SQUARE, rank // 2, width // replicas
     w, b = warm_start.T, prev_basis.T
-    piece = (rows, units)
-
-    terms = call(
-        left_factor_kernel,
-        [piece] * SQUARE,
+    first = units // 256 * 128
+    rest = units - first
+
+    *terms, projected = call(
+        first_term_kernel,
+        [(rows, first)] * SQUARE + [(rank, 2 * tokens)],
         [HBM_SPEC] * 5,
         [
             pltpu.VMEM((rank, width), F32),
             pltpu.VMEM((2 * tokens, width), BF16),
-            pltpu.VMEM((2 * tokens, units), BF16),
-            pltpu.SemaphoreType.DMA((20,)),
+            pltpu.VMEM((2 * tokens, first), BF16),
+            pltpu.SemaphoreType.DMA((16,)),
         ],
-        flops=4 * tokens * rank * (units + width),
-        moved=4 * tokens * (units + width) + 4 * rank * (units + width),
-        vmem=60 << 20,
-    )(w, out_grad, prev_grad, hidden, prev_hidden)
-    got = [swap_dp(terms[m], m) for m in range(1, SQUARE)]
+        flops=4 * tokens * rank * (first + width),
+        moved=4 * tokens * (first + width) + 4 * rank * (first + width),
+    )(*[in_hbm(x) for x in (w, out_grad, prev_grad, hidden, prev_hidden)])
+    late_terms = call(
+        second_term_kernel,
+        [(rows, rest)] * SQUARE,
+        [VMEM_SPEC] + [HBM_SPEC] * 2,
+        [pltpu.VMEM((2 * tokens, rest), BF16), pltpu.SemaphoreType.DMA((4,))],
+        flops=4 * tokens * rank * rest,
+        moved=4 * tokens * rest + 4 * rank * rest,
+    )(projected, in_hbm(hidden), in_hbm(prev_hidden))
     (feedback,) = call(
         feedback_kernel,
-        [piece],
+        [(rows, units)],
         [VMEM_SPEC] * 2,
         [pltpu.VMEM((rank, rank), F32)],
         flops=2 * rank * rank * (units + width),
         moved=4 * rank * (units + width),
     )(w, b)
-    summed = terms[0] + got[0] + got[1] + got[2]
-    own = (summed + swap_dp(summed, SQUARE)) * (1.0 / replicas) - feedback
-    p = [own] + [swap_dp(own, m) for m in range(1, SQUARE)]
-
+
+    def swap_square(x):
+        return [swap_dp(x[m], m) for m in range(1, SQUARE)]
+
+    def mean(summed, came, correction):
+        return (summed + came) * (1.0 / replicas) - correction
+
+    early = terms[0] + sum(swap_square(terms))
+    early_came = swap_dp(early, SQUARE)
+    late = late_terms[0] + sum(swap_square(late_terms))
+    late_came = swap_dp(late, SQUARE)
+    early_own = mean(early, early_came, feedback[:, :first])
+    early_p = [early_own] + swap_square([early_own] * SQUARE)
+    late_own = mean(late, late_came, feedback[:, first:])
+    late_p = [late_own] + swap_square([late_own] * SQUARE)
+
+    early_v, early_gram = call(
+        first_pull_kernel,
+        [(rank, 2 * tokens), (rank, 128)],
+        [VMEM_SPEC] * 7,
+        [pltpu.VMEM((rank, first), F32)],
+        flops=8 * tokens * rank * first,
+        moved=4 * tokens * first + 4 * rank * first,
+    )(*early_p, hidden, prev_hidden, b)
     keep, send = call(
         pull_kernel,
         [(half, 2 * tokens)] * 2,
-        [VMEM_SPEC] * 6,
+        [VMEM_SPEC] * 7,
         [pltpu.VMEM((rank, 2 * tokens), F32)],
-        flops=8 * tokens * rank * units,
-        moved=4 * tokens * units + 4 * rank * units,
-    )(*p, hidden, prev_hidden)
+        flops=8 * tokens * rank * rest,
+        moved=4 * tokens * rest + 4 * rank * rest,
+    )(*late_p, early_v, hidden, prev_hidden)
     other = swap_tensor(send, 1)
     (gram,) = call(
         gram_kernel,
         [(rank, 128)],
-        [VMEM_SPEC] * 5,
-        [pltpu.VMEM((rank, units), F32)],
-        flops=4 * rank * rank * units,
-        moved=8 * rank * units,
-    )(*p, b)
+        [VMEM_SPEC] * 6,
+        [pltpu.VMEM((rank, rest), F32)],
+        flops=4 * rank * rank * rest,
+        moved=8 * rank * rest,
+    )(*late_p, b, early_gram)
+    gram_came = swap_tensor(gram, 1)
+    plane = keep + other
+    plane_came = swap_tensor(plane, 2)
+    gram = gram + gram_came
     parts = call(
         push_kernel,
         [(2, half, owned)] * SQUARE,
         [VMEM_SPEC] * 4 + [ANY_SPEC],
         flops=8 * tokens * half * width,
         moved=4 * tokens * width + 4 * half * width,
-    )(keep, other, out_grad, prev_grad, gram)
-    came = [swap_dp(parts[m], m) for m in range(1, SQUARE)]
-
-    gram = gram + swap_tensor(gram, 1)
+    )(plane, plane_came, out_grad, prev_grad, gram)
+    came = swap_square(parts)
     gram = gram + swap_tensor(gram, 2)
     (solved,) = call(
         cholesky_kernel, [(rank, 128)], [VMEM_SPEC], flops=rank**3, moved=8 * rank * 128
@@ -341,23 +420,18 @@
     basis, fix = call(
         functools.partial(basis_kernel, norm_scale=norm_scale),
         [(rank, units), (rank, owned)],
-        [VMEM_SPEC] * 6,
-        [pltpu.VMEM((rank, units), F32)],
+        [VMEM_SPEC] * 10,
+        [pltpu.VMEM((rank, first), F32), pltpu.VMEM((rank, rest), F32)],
         flops=2 * rank * rank * units,
         moved=8 * rank * units,
-    )(*p, solved, w)
-    far_far, near_up, far_up = (
-        swap_both(far, SQUARE, 2),
-        swap_both(near, 0, 2),
-        swap_both(far, SQUARE, 0),
-    )
+    )(*early_p, *late_p, solved, w)
     (mine,) = call(
         total_kernel,
         [(half, owned)],
-        [VMEM_SPEC] * 4 + [ANY_SPEC],
-        flops=3 * half * owned,
-        moved=20 * half * owned,
-    )(near, far_far, near_up, far_up, fix)
+        [VMEM_SPEC] * 2 + [ANY_SPEC],
+        flops=half * owned,
+        moved=12 * half * owned,
+    )(near, swap_dp(far, SQUARE), fix)
     (factor,) = call(
         functools.partial(factor_kernel, replicas=replicas),
         [(rank, owned)],

time: 76.3 us -> 67.2 us (0.88)
  waiting for transfers between devices: 35.9 us -> 20.1 us
  starting transfers between devices: 20.6 us -> 27.8 us
  other arithmetic: 1.18 us -> 0.09 us
    ppermute x10 -> x18, waiting for transfers between devices: 26.8 us -> 14.4 us  [swap_dp(): return lax.ppermute(x, 'dp', [(i, i ^ m) for i in range(n)])]
    ppermute x10 -> x18, starting transfers between devices: 14.5 us -> 24 us  [swap_dp(): return lax.ppermute(x, 'dp', [(i, i ^ m) for i in range(n)])]
    ppermute x3 -> x0, starting transfers between devices: 4.71 us -> none  [swap_both(): return lax.ppermute(x, ('dp', 'tensor'), pairs)]
    ppermute x3 -> x0, waiting for transfers between devices: 4.2 us -> none  [swap_both(): return lax.ppermute(x, ('dp', 'tensor'), pairs)]
    ppermute x4 -> x5, starting transfers between devices: 1.43 us -> 3.78 us  [swap_tensor(): return lax.ppermute(x, 'tensor', [(i, i ^ m) for i in range(n)])]
    add x2 -> x4, other arithmetic: 1.14 us -> 0.06 us  [the longest x1 0.02 us: on_device(): early = terms[0] + sum(swap_square(terms))]
    ppermute x4 -> x5, waiting for transfers between devices: 4.86 us -> 5.67 us  [swap_tensor(): return lax.ppermute(x, 'tensor', [(i, i ^ m) for i in range(n)])]
    pallas_call x5 -> x7, Pallas kernels: 11.2 us -> 11.7 us  [the longest x1 4.86 us: on_device(): call(first_term_kernel, [(rows, first)] * SQUARE + [(rank, 2 * tokens)],...]
  transfers between devices with their start and end apart: 17 -> 23, of which waited for: 12 -> 12; matrix products, arithmetic and copies ran while one was open for 0% -> 0% of each run, Pallas kernels for 11% -> 16%
where the time goes in v3:
time: 67.2 us; the launch traced here: 67 us
  starting transfers between devices  27.8 us (41%)
  waiting for transfers between devices  20.1 us (30%)
  Pallas kernels  18.2 us (27%)
  between operations  0.76 us (1%)
    ppermute x18, starting transfers between devices, swap_dp(): return lax.ppermute(x, 'dp', [(i, i ^ m) for i in range(n)])  24 us
    ppermute x18, waiting for transfers between devices, swap_dp(): return lax.ppermute(x, 'dp', [(i, i ^ m) for i in range(n)])  14.4 us
    ppermute x5, waiting for transfers between devices, swap_tensor(): return lax.ppermute(x, 'tensor', [(i, i ^ m) for i in range(n)])  5.67 us
    pallas_call x1, Pallas kernels, on_device(): call(first_term_kernel, [(rows, first)] * SQUARE + [(rank, 2 * tokens)],...  4.86 us
    ppermute x5, starting transfers between devices, swap_tensor(): return lax.ppermute(x, 'tensor', [(i, i ^ m) for i in range(n)])  3.78 us
    pallas_call x1, Pallas kernels, on_device(): call(cholesky_kernel, [(rank, 128)], [VMEM_SPEC], flops=rank ** 3, moved=...  3.01 us
    pallas_call x1, Pallas kernels, on_device(): call(feedback_kernel, [(rows, units)], [VMEM_SPEC] * 2, [pltpu.VMEM((rank...  2.04 us
    pallas_call x1, Pallas kernels, on_device(): call(second_term_kernel, [(rows, rest)] * SQUARE, [VMEM_SPEC] + [HBM_SPEC...  1.91 us
  transfers between devices with their start and end apart: 23, of which 12 were waited for; matrix products, arithmetic and copies ran while one was open for 0% of the time, Pallas kernels for 16%

profile of v3, /device:TPU:0, one launch (start us, length us, event | category | flops | bytes accessed | tf_op | source)
XLA Modules:
  0.0 67.0 jit_solution(7400373031712259634)
XLA Ops:
  0.6 4.9 %shard_map.77 = (f32[8,3584]{1,0:T(8,128)S(1)}, f32[8,3584]{1,0:T(8,128)S(1)}, f32[8,3584]{1,0:T(8,128)S(1)}, f32[8,3584]{1,0:T(8,128)S(1)}, f32[32,256]{1,0:T(8,128)S(1)}) custom-call(f32[32,8192]{1,0:T(8,128)} %bitcast.4, bf16[128,8192]{1,0:T(8,128)(2,1)} %o_ref.3, bf16[128,8192]{1,0:T(8,128)(2,1)} %o2_ref.3, bf16[128,7168]{1,0:T(8,128)(2,1)} %h_ref.7, ...), custom_call_target="tpu_custom_call" | custom-call | flops 192937984 | bytes 7536640 | tf_op jit(solution)/shard_map/pallas_call | solution.py:327
  5.5 3.0 %collective-permute-start = (f32[8,3584]{1,0:T(8,128)S(1)}, f32[8,3584]{1,0:T(8,128)S(1)}, u32[]{:S(2)}, u32[]{:S(2)}) collective-permute-start(f32[8,3584]{1,0:T(8,128)S(1)} %get-tuple-element.24), channel_id=1, source_target_pairs={{0,4},{4,0},{8,12},{12,8},{16,20},{20,16},{24,28},{28,24},{1,5},{5... | collective-permute-start | bytes 344072 | tf_op jit(solution)/shard_map/ppermute | solution.py:309
  8.5 1.6 %collective-permute-start.1 = (f32[8,3584]{1,0:T(8,128)S(1)}, f32[8,3584]{1,0:T(8,128)S(1)}, u32[]{:S(2)}, u32[]{:S(2)}) collective-permute-start(f32[8,3584]{1,0:T(8,128)S(1)} %get-tuple-element.25), channel_id=1, source_target_pairs={{0,8},{4,12},{8,0},{12,4},{16,24},{20,28},{24,16},{28,20},{1,9},{5... | collective-permute-start | bytes 344072 | tf_op jit(solution)/shard_map/ppermute | solution.py:309
  10.1 1.9 %shard_map.79 = (f32[8,3584]{1,0:T(8,128)S(1)}, f32[8,3584]{1,0:T(8,128)S(1)}, f32[8,3584]{1,0:T(8,128)S(1)}, f32[8,3584]{1,0:T(8,128)S(1)}) custom-call(f32[32,256]{1,0:T(8,128)S(1)} %get-tuple-element.27.y_ref, bf16[128,7168]{1,0:T(8,128)(2,1)} %h_ref.7, bf16[128,7168]{1,0:T(8,128)(2,1)} %h2_ref.7), custom_call_target="tpu_custom_call" | custom-call | flops 58720256 | bytes 2293760 | tf_op jit(solution)/shard_map/pallas_call | solution.py:340
  12.0 2.0 %collective-permute-start.7 = (f32[8,3584]{1,0:T(8,128)S(1)}, f32[8,3584]{1,0:T(8,128)S(1)}, u32[]{:S(2)}, u32[]{:S(2)}) collective-permute-start(f32[8,3584]{1,0:T(8,128)S(1)} %get-tuple-element.29), channel_id=1, source_target_pairs={{0,4},{4,0},{8,12},{12,8},{16,20},{20,16},{24,28},{28,24},{1,5},{5... | collective-permute-start | bytes 344072 | tf_op jit(solution)/shard_map/ppermute | solution.py:309
  14.0 1.6 %collective-permute-start.8 = (f32[8,3584]{1,0:T(8,128)S(1)}, f32[8,3584]{1,0:T(8,128)S(1)}, u32[]{:S(2)}, u32[]{:S(2)}) collective-permute-start(f32[8,3584]{1,0:T(8,128)S(1)} %get-tuple-element.30), channel_id=1, source_target_pairs={{0,8},{4,12},{8,0},{12,4},{16,24},{20,28},{24,16},{28,20},{1,9},{5... | collective-permute-start | bytes 344072 | tf_op jit(solution)/shard_map/ppermute | solution.py:309
  16.5 2.5 %collective-permute-start.3 = (f32[8,3584]{1,0:T(8,128)S(1)}, f32[8,3584]{1,0:T(8,128)S(1)}, u32[]{:S(2)}, u32[]{:S(2)}) collective-permute-start(f32[8,3584]{1,0:T(8,128)S(1)} %add_add_fusion.1), channel_id=1, source_target_pairs={{0,16},{4,20},{8,24},{12,28},{16,0},{20,4},{24,8},{28,12},{1,17},{... | collective-permute-start | bytes 344072 | tf_op jit(solution)/shard_map/ppermute | solution.py:309
  19.0 1.5 %collective-permute-done.8 = f32[8,3584]{1,0:T(8,128)S(1)} collective-permute-done((f32[8,3584]{1,0:T(8,128)S(1)}, f32[8,3584]{1,0:T(8,128)S(1)}, u32[]{:S(2)}, u32[]{:S(2)}) %collective-permute-start.8) | collective-permute-done | bytes 114720 | tf_op jit(solution)/shard_map/ppermute | solution.py:309
  20.5 2.3 %collective-permute-done.9 = f32[8,3584]{1,0:T(8,128)S(1)} collective-permute-done((f32[8,3584]{1,0:T(8,128)S(1)}, f32[8,3584]{1,0:T(8,128)S(1)}, u32[]{:S(2)}, u32[]{:S(2)}) %collective-permute-start.9) | collective-permute-done | bytes 114720 | tf_op jit(solution)/shard_map/ppermute | solution.py:309
  22.9 2.2 %collective-permute-start.10 = (f32[8,3584]{1,0:T(8,128)S(1)}, f32[8,3584]{1,0:T(8,128)S(1)}, u32[]{:S(2)}, u32[]{:S(2)}) collective-permute-start(f32[8,3584]{1,0:T(8,128)S(1)} %add_add_fusion), channel_id=1, source_target_pairs={{0,16},{4,20},{8,24},{12,28},{16,0},{20,4},{24,8},{28,12},{1,17},{... | collective-permute-start | bytes 344072 | tf_op jit(solution)/shard_map/ppermute | solution.py:309
  25.1 2.0 %shard_map.78 = f32[8,7168]{1,0:T(8,128)S(1)} custom-call(f32[32,8192]{1,0:T(8,128)S(1)} %bitcast.5, f32[32,7168]{1,0:T(8,128)S(1)} %bitcast.7), custom_call_target="tpu_custom_call" | custom-call | flops 31457280 | bytes 1966080 | tf_op jit(solution)/shard_map/pallas_call | solution.py:348
  27.1 2.8 %collective-permute-done.10 = f32[8,3584]{1,0:T(8,128)S(1)} collective-permute-done((f32[8,3584]{1,0:T(8,128)S(1)}, f32[8,3584]{1,0:T(8,128)S(1)}, u32[]{:S(2)}, u32[]{:S(2)}) %collective-permute-start.10) | collective-permute-done | bytes 114720 | tf_op jit(solution)/shard_map/ppermute | solution.py:309
  31.2 1.3 %collective-permute-start.5 = (f32[8,3584]{1,0:T(8,128)S(1)}, f32[8,3584]{1,0:T(8,128)S(1)}, u32[]{:S(2)}, u32[]{:S(2)}) collective-permute-start(f32[8,3584]{1,0:T(8,128)S(1)} %get-tuple-element.45.s0.u0), channel_id=1, source_target_pairs={{0,8},{4,12},{8,0},{12,4},{16,24},{20,28},{24,16},{28,20},{1,9},{5... | collective-permute-start | bytes 344072 | tf_op jit(solution)/shard_map/ppermute | solution.py:309
  34.7 1.3 %collective-permute-start.12 = (f32[8,3584]{1,0:T(8,128)S(1)}, f32[8,3584]{1,0:T(8,128)S(1)}, u32[]{:S(2)}, u32[]{:S(2)}) collective-permute-start(f32[8,3584]{1,0:T(8,128)S(1)} %get-tuple-element.44.s0), channel_id=1, source_target_pairs={{0,8},{4,12},{8,0},{12,4},{16,24},{20,28},{24,16},{28,20},{1,9},{5... | collective-permute-start | bytes 344072 | tf_op jit(solution)/shard_map/ppermute | solution.py:309
  38.9 1.3 %collective-permute-done.4.s1.u1 = f32[8,3584]{1,0:T(8,128)S(1)} collective-permute-done((f32[8,3584]{1,0:T(8,128)S(1)}, f32[8,3584]{1,0:T(8,128)S(1)}, u32[]{:S(2)}, u32[]{:S(2)}) %collective-permute-start.4) | collective-permute-done | bytes 114720 | tf_op jit(solution)/shard_map/ppermute | solution.py:309
  40.2 1.4 %shard_map.80 = (f32[32,256]{1,0:T(8,128)S(1)}, f32[32,128]{1,0:T(8,128)S(1)}) custom-call(f32[8,3584]{1,0:T(8,128)S(1)} %get-tuple-element.45.s0.u0, f32[8,3584]{1,0:T(8,128)S(1)} %collective-permute-done.4.s1.u1, f32[8,3584]{1,0:T(8,128)S(1)} %collective-permute-done.5.s2.u2, f32[8,3584]{1,0:T(8,128)S(1)} %collective-permute-done.6.s3.u3, ...), custom_call_target="tpu_custom_call" | custom-call | flops 117440512 | bytes 2293760 | tf_op jit(solution)/shard_map/pallas_call | solution.py:372
  44.4 1.6 %collective-permute-start.17 = (f32[16,256]{1,0:T(8,128)S(1)}, f32[16,256]{1,0:T(8,128)S(1)}, u32[]{:S(2)}, u32[]{:S(2)}) collective-permute-start(f32[16,256]{1,0:T(8,128)S(1)} %add.43.mine_ref), channel_id=1, source_target_pairs={{0,2},{1,3},{2,0},{3,1},{4,6},{5,7},{6,4},{7,5},{8,10},{9,11},{10,... | collective-permute-start | bytes 49160 | tf_op jit(solution)/shard_map/ppermute | solution.py:314
  46.0 2.2 %collective-permute-done.17.got_ref = f32[16,256]{1,0:T(8,128)S(1)} collective-permute-done((f32[16,256]{1,0:T(8,128)S(1)}, f32[16,256]{1,0:T(8,128)S(1)}, u32[]{:S(2)}, u32[]{:S(2)}) %collective-permute-start.17) | collective-permute-done | bytes 16416 | tf_op jit(solution)/shard_map/ppermute | solution.py:314
  50.2 2.3 %collective-permute-start.20 = (f32[2,16,1024]{2,1,0:T(8,128)S(1)}, f32[2,16,1024]{2,1,0:T(8,128)S(1)}, u32[]{:S(2)}, u32[]{:S(2)}) collective-permute-start(f32[2,16,1024]{2,1,0:T(8,128)S(1)} %get-tuple-element.40), channel_id=1, source_target_pairs={{0,12},{4,8},{8,4},{12,0},{16,28},{20,24},{24,20},{28,16},{1,13},{... | collective-permute-start | bytes 393224 | tf_op jit(solution)/shard_map/ppermute | solution.py:309
  52.4 1.5 %collective-permute-start.15 = (f32[32,128]{1,0:T(8,128)S(1)}, f32[32,128]{1,0:T(8,128)S(1)}, u32[]{:S(2)}, u32[]{:S(2)}) collective-permute-start(f32[32,128]{1,0:T(8,128)S(1)} %add.41.after_ref), channel_id=1, source_target_pairs={{0,2},{1,3},{2,0},{3,1},{4,6},{5,7},{6,4},{7,5},{8,10},{9,11},{10,... | collective-permute-start | bytes 49160 | tf_op jit(solution)/shard_map/ppermute | solution.py:314
  54.0 2.2 %collective-permute-done.15 = f32[32,128]{1,0:T(8,128)S(1)} collective-permute-done((f32[32,128]{1,0:T(8,128)S(1)}, f32[32,128]{1,0:T(8,128)S(1)}, u32[]{:S(2)}, u32[]{:S(2)}) %collective-permute-start.15) | collective-permute-done | bytes 16416 | tf_op jit(solution)/shard_map/ppermute | solution.py:314
  56.2 3.0 %shard_map.82.l_ref.after_ref = f32[32,128]{1,0:T(8,128)S(1)} custom-call(f32[32,128]{1,0:T(8,128)S(1)} %add.42.in_ref), custom_call_target="tpu_custom_call" | custom-call | flops 32768 | bytes 32768 | tf_op jit(solution)/shard_map/pallas_call | solution.py:410
  60.0 1.8 %shard_map.83 = (f32[32,7168]{1,0:T(8,128)}, f32[32,1024]{1,0:T(8,128)S(1)}) custom-call(f32[8,3584]{1,0:T(8,128)S(1)} %get-tuple-element.45.s0.u0, f32[8,3584]{1,0:T(8,128)S(1)} %collective-permute-done.4.s1.u1, f32[8,3584]{1,0:T(8,128)S(1)} %collective-permute-done.5.s2.u2, f32[8,3584]{1,0:T(8,128)S(1)} %collective-permute-done.6.s3.u3, ...), custom_call_target="tpu_custom_call" | custom-call | flops 14680064 | bytes 1835008 | tf_op jit(solution)/shard_map/pallas_call | solution.py:420
  61.9 2.9 %collective-permute-done.21.b_ref = f32[16,1024]{1,0:T(8,128)S(1)} collective-permute-done((f32[16,1024]{1,0:T(8,128)S(1)}, f32[16,1024]{1,0:T(8,128)S(1)}, u32[]{:S(2)}, u32[]{:S(2)}) %collective-permute-start.21) | collective-permute-done | bytes 65568 | tf_op jit(solution)/shard_map/ppermute | solution.py:309
  (52 shorter events, 15.3 us)
Async XLA Ops:
  5.5 10.1 %collective-permute-start = (f32[8,3584]{1,0:T(8,128)S(1)}, f32[8,3584]{1,0:T(8,128)S(1)}, u32[]{:S(2)}, u32[]{:S(2)}) collective-permute-start(f32[8,3584]{1,0:T(8,128)S(1)} %get-tuple-element.24), channel_id=1, source_target_pairs={{0,4},{4,0},{8,12},{12,8},{16,20},{20,16},{24,28},{28,24},{1,5},{5... | collective-permute-start | bytes 344072 | tf_op jit(solution)/shard_map/ppermute | solution.py:309
  8.5 7.1 %collective-permute-start.1 = (f32[8,3584]{1,0:T(8,128)S(1)}, f32[8,3584]{1,0:T(8,128)S(1)}, u32[]{:S(2)}, u32[]{:S(2)}) collective-permute-start(f32[8,3584]{1,0:T(8,128)S(1)} %get-tuple-element.25), channel_id=1, source_target_pairs={{0,8},{4,12},{8,0},{12,4},{16,24},{20,28},{24,16},{28,20},{1,9},{5... | collective-permute-start | bytes 344072 | tf_op jit(solution)/shard_map/ppermute | solution.py:309
  10.1 6.4 %collective-permute-start.2 = (f32[8,3584]{1,0:T(8,128)S(1)}, f32[8,3584]{1,0:T(8,128)S(1)}, u32[]{:S(2)}, u32[]{:S(2)}) collective-permute-start(f32[8,3584]{1,0:T(8,128)S(1)} %get-tuple-element.26), channel_id=1, source_target_pairs={{0,12},{4,8},{8,4},{12,0},{16,28},{20,24},{24,20},{28,16},{1,13},{... | collective-permute-start | bytes 344072 | tf_op jit(solution)/shard_map/ppermute | solution.py:309
  12.0 7.0 %collective-permute-start.7 = (f32[8,3584]{1,0:T(8,128)S(1)}, f32[8,3584]{1,0:T(8,128)S(1)}, u32[]{:S(2)}, u32[]{:S(2)}) collective-permute-start(f32[8,3584]{1,0:T(8,128)S(1)} %get-tuple-element.29), channel_id=1, source_target_pairs={{0,4},{4,0},{8,12},{12,8},{16,20},{20,16},{24,28},{28,24},{1,5},{5... | collective-permute-start | bytes 344072 | tf_op jit(solution)/shard_map/ppermute | solution.py:309
  14.0 6.5 %collective-permute-start.8 = (f32[8,3584]{1,0:T(8,128)S(1)}, f32[8,3584]{1,0:T(8,128)S(1)}, u32[]{:S(2)}, u32[]{:S(2)}) collective-permute-start(f32[8,3584]{1,0:T(8,128)S(1)} %get-tuple-element.30), channel_id=1, source_target_pairs={{0,8},{4,12},{8,0},{12,4},{16,24},{20,28},{24,16},{28,20},{1,9},{5... | collective-permute-start | bytes 344072 | tf_op jit(solution)/shard_map/ppermute | solution.py:309
  15.6 7.3 %collective-permute-start.9 = (f32[8,3584]{1,0:T(8,128)S(1)}, f32[8,3584]{1,0:T(8,128)S(1)}, u32[]{:S(2)}, u32[]{:S(2)}) collective-permute-start(f32[8,3584]{1,0:T(8,128)S(1)} %get-tuple-element.31), channel_id=1, source_target_pairs={{0,12},{4,8},{8,4},{12,0},{16,28},{20,24},{24,20},{28,16},{1,13},{... | collective-permute-start | bytes 344072 | tf_op jit(solution)/shard_map/ppermute | solution.py:309
  16.5 23.7 %copy-start.1 = (bf16[128,7168]{1,0:T(8,128)(2,1)S(1)}, bf16[128,7168]{1,0:T(8,128)(2,1)}, u32[]{:S(2)}) copy-start(bf16[128,7168]{1,0:T(8,128)(2,1)} %h2_ref.7) | copy-start | bytes 5505028
  16.5 10.6 %collective-permute-start.3 = (f32[8,3584]{1,0:T(8,128)S(1)}, f32[8,3584]{1,0:T(8,128)S(1)}, u32[]{:S(2)}, u32[]{:S(2)}) collective-permute-start(f32[8,3584]{1,0:T(8,128)S(1)} %add_add_fusion.1), channel_id=1, source_target_pairs={{0,16},{4,20},{8,24},{12,28},{16,0},{20,4},{24,8},{28,12},{1,17},{... | collective-permute-start | bytes 344072 | tf_op jit(solution)/shard_map/ppermute | solution.py:309
  22.9 7.0 %collective-permute-start.10 = (f32[8,3584]{1,0:T(8,128)S(1)}, f32[8,3584]{1,0:T(8,128)S(1)}, u32[]{:S(2)}, u32[]{:S(2)}) collective-permute-start(f32[8,3584]{1,0:T(8,128)S(1)} %add_add_fusion), channel_id=1, source_target_pairs={{0,16},{4,20},{8,24},{12,28},{16,0},{20,4},{24,8},{28,12},{1,17},{... | collective-permute-start | bytes 344072 | tf_op jit(solution)/shard_map/ppermute | solution.py:309
  30.0 7.1 %collective-permute-start.6 = (f32[8,3584]{1,0:T(8,128)S(1)}, f32[8,3584]{1,0:T(8,128)S(1)}, u32[]{:S(2)}, u32[]{:S(2)}) collective-permute-start(f32[8,3584]{1,0:T(8,128)S(1)} %get-tuple-element.45.s0.u0), channel_id=1, source_target_pairs={{0,12},{4,8},{8,4},{12,0},{16,28},{20,24},{24,20},{28,16},{1,13},{... | collective-permute-start | bytes 344072 | tf_op jit(solution)/shard_map/ppermute | solution.py:309
  31.2 7.7 %collective-permute-start.5 = (f32[8,3584]{1,0:T(8,128)S(1)}, f32[8,3584]{1,0:T(8,128)S(1)}, u32[]{:S(2)}, u32[]{:S(2)}) collective-permute-start(f32[8,3584]{1,0:T(8,128)S(1)} %get-tuple-element.45.s0.u0), channel_id=1, source_target_pairs={{0,8},{4,12},{8,0},{12,4},{16,24},{20,28},{24,16},{28,20},{1,9},{5... | collective-permute-start | bytes 344072 | tf_op jit(solution)/shard_map/ppermute | solution.py:309
  32.5 7.6 %collective-permute-start.4 = (f32[8,3584]{1,0:T(8,128)S(1)}, f32[8,3584]{1,0:T(8,128)S(1)}, u32[]{:S(2)}, u32[]{:S(2)}) collective-permute-start(f32[8,3584]{1,0:T(8,128)S(1)} %get-tuple-element.45.s0.u0), channel_id=1, source_target_pairs={{0,4},{4,0},{8,12},{12,8},{16,20},{20,16},{24,28},{28,24},{1,5},{5... | collective-permute-start | bytes 344072 | tf_op jit(solution)/shard_map/ppermute | solution.py:309
  33.5 8.0 %collective-permute-start.13 = (f32[8,3584]{1,0:T(8,128)S(1)}, f32[8,3584]{1,0:T(8,128)S(1)}, u32[]{:S(2)}, u32[]{:S(2)}) collective-permute-start(f32[8,3584]{1,0:T(8,128)S(1)} %get-tuple-element.44.s0), channel_id=1, source_target_pairs={{0,12},{4,8},{8,4},{12,0},{16,28},{20,24},{24,20},{28,16},{1,13},{... | collective-permute-start | bytes 344072 | tf_op jit(solution)/shard_map/ppermute | solution.py:309
  34.7 6.8 %collective-permute-start.12 = (f32[8,3584]{1,0:T(8,128)S(1)}, f32[8,3584]{1,0:T(8,128)S(1)}, u32[]{:S(2)}, u32[]{:S(2)}) collective-permute-start(f32[8,3584]{1,0:T(8,128)S(1)} %get-tuple-element.44.s0), channel_id=1, source_target_pairs={{0,8},{4,12},{8,0},{12,4},{16,24},{20,28},{24,16},{28,20},{1,9},{5... | collective-permute-start | bytes 344072 | tf_op jit(solution)/shard_map/ppermute | solution.py:309
  37.1 5.2 %collective-permute-start.11 = (f32[8,3584]{1,0:T(8,128)S(1)}, f32[8,3584]{1,0:T(8,128)S(1)}, u32[]{:S(2)}, u32[]{:S(2)}) collective-permute-start(f32[8,3584]{1,0:T(8,128)S(1)} %get-tuple-element.44.s0), channel_id=1, source_target_pairs={{0,4},{4,0},{8,12},{12,8},{16,20},{20,16},{24,28},{28,24},{1,5},{5... | collective-permute-start | bytes 344072 | tf_op jit(solution)/shard_map/ppermute | solution.py:309
  43.0 1.4 %collective-permute-start.16 = (f32[16,256]{1,0:T(8,128)S(1)}, f32[16,256]{1,0:T(8,128)S(1)}, u32[]{:S(2)}, u32[]{:S(2)}) collective-permute-start(f32[16,256]{1,0:T(8,128)S(1)} %get-tuple-element.36), channel_id=1, source_target_pairs={{0,1},{1,0},{2,3},{3,2},{4,5},{5,4},{6,7},{7,6},{8,9},{9,8},{10,11... | collective-permute-start | bytes 49160 | tf_op jit(solution)/shard_map/ppermute | solution.py:314
  43.9 2.1 %collective-permute-start.14 = (f32[32,128]{1,0:T(8,128)S(1)}, f32[32,128]{1,0:T(8,128)S(1)}, u32[]{:S(2)}, u32[]{:S(2)}) collective-permute-start(f32[32,128]{1,0:T(8,128)S(1)} %shard_map.81), channel_id=1, source_target_pairs={{0,1},{1,0},{2,3},{3,2},{4,5},{5,4},{6,7},{7,6},{8,9},{9,8},{10,11... | collective-permute-start | bytes 49160 | tf_op jit(solution)/shard_map/ppermute | solution.py:314
  44.4 3.8 %collective-permute-start.17 = (f32[16,256]{1,0:T(8,128)S(1)}, f32[16,256]{1,0:T(8,128)S(1)}, u32[]{:S(2)}, u32[]{:S(2)}) collective-permute-start(f32[16,256]{1,0:T(8,128)S(1)} %add.43.mine_ref), channel_id=1, source_target_pairs={{0,2},{1,3},{2,0},{3,1},{4,6},{5,7},{6,4},{7,5},{8,10},{9,11},{10,... | collective-permute-start | bytes 49160 | tf_op jit(solution)/shard_map/ppermute | solution.py:314
  48.9 10.3 %collective-permute-start.18 = (f32[2,16,1024]{2,1,0:T(8,128)S(1)}, f32[2,16,1024]{2,1,0:T(8,128)S(1)}, u32[]{:S(2)}, u32[]{:S(2)}) collective-permute-start(f32[2,16,1024]{2,1,0:T(8,128)S(1)} %get-tuple-element.38), channel_id=1, source_target_pairs={{0,4},{4,0},{8,12},{12,8},{16,20},{20,16},{24,28},{28,24},{1,5},{5... | collective-permute-start | bytes 393224 | tf_op jit(solution)/shard_map/ppermute | solution.py:309
  49.8 9.4 %collective-permute-start.19 = (f32[2,16,1024]{2,1,0:T(8,128)S(1)}, f32[2,16,1024]{2,1,0:T(8,128)S(1)}, u32[]{:S(2)}, u32[]{:S(2)}) collective-permute-start(f32[2,16,1024]{2,1,0:T(8,128)S(1)} %get-tuple-element.39), channel_id=1, source_target_pairs={{0,8},{4,12},{8,0},{12,4},{16,24},{20,28},{24,16},{28,20},{1,9},{5... | collective-permute-start | bytes 393224 | tf_op jit(solution)/shard_map/ppermute | solution.py:309
  50.2 9.1 %collective-permute-start.20 = (f32[2,16,1024]{2,1,0:T(8,128)S(1)}, f32[2,16,1024]{2,1,0:T(8,128)S(1)}, u32[]{:S(2)}, u32[]{:S(2)}) collective-permute-start(f32[2,16,1024]{2,1,0:T(8,128)S(1)} %get-tuple-element.40), channel_id=1, source_target_pairs={{0,12},{4,8},{8,4},{12,0},{16,28},{20,24},{24,20},{28,16},{1,13},{... | collective-permute-start | bytes 393224 | tf_op jit(solution)/shard_map/ppermute | solution.py:309
  52.4 3.7 %collective-permute-start.15 = (f32[32,128]{1,0:T(8,128)S(1)}, f32[32,128]{1,0:T(8,128)S(1)}, u32[]{:S(2)}, u32[]{:S(2)}) collective-permute-start(f32[32,128]{1,0:T(8,128)S(1)} %add.41.after_ref), channel_id=1, source_target_pairs={{0,2},{1,3},{2,0},{3,1},{4,6},{5,7},{6,4},{7,5},{8,10},{9,11},{10,... | collective-permute-start | bytes 49160 | tf_op jit(solution)/shard_map/ppermute | solution.py:314
  59.3 5.5 %collective-permute-start.21 = (f32[16,1024]{1,0:T(8,128)S(1)}, f32[16,1024]{1,0:T(8,128)S(1)}, u32[]{:S(2)}, u32[]{:S(2)}) collective-permute-start(f32[16,1024]{1,0:T(8,128)S(1)} %get-tuple-element.42), channel_id=1, source_target_pairs={{0,16},{4,20},{8,24},{12,28},{16,0},{20,4},{24,8},{28,12},{1,17},{... | collective-permute-start | bytes 196616 | tf_op jit(solution)/shard_map/ppermute | solution.py:309
  64.7 1.3 %collective-permute-start.22 = (f32[16,1024]{1,0:T(8,128)S(1)}, f32[16,1024]{1,0:T(8,128)S(1)}, u32[]{:S(2)}, u32[]{:S(2)}) collective-permute-start(f32[16,1024]{1,0:T(8,128)S(1)} %shard_map.87.t_ref), channel_id=1, source_target_pairs={{0,1},{1,0},{2,3},{3,2},{4,5},{5,4},{6,7},{7,6},{8,9},{9,8},{10,11... | collective-permute-start | bytes 196616 | tf_op jit(solution)/shard_map/ppermute | solution.py:314
  (5 other events, 65.6 us)

commit v4 on v3

v4 whole, which is shorter than its diff:
```python
import functools

import jax
import jax.numpy as jnp
from jax import lax
from jax.experimental import pallas as pl
from jax.experimental.pallas import tpu as pltpu
from jax.sharding import PartitionSpec as P

F32 = jnp.float32
BF16 = jnp.bfloat16
SQUARE = 4
TERMS_AWAY = (0, 3, 2, 1)
SUMS_AWAY = (0, 3, 2, 1)
RIGHT_AWAY = (0, 3, 2, 1)
NT = (((1,), (1,)), ((), ()))
NN = (((1,), (0,)), ((), ()))
VMEM_SPEC = pl.BlockSpec(memory_space=pltpu.VMEM)
ANY_SPEC = pl.BlockSpec(memory_space=pl.ANY)
HBM_SPEC = pl.BlockSpec(memory_space=pltpu.HBM)


def orthonormal(rows_in, gram_matrix, norm_scale):
    lower = jnp.linalg.cholesky(gram_matrix)
    return norm_scale * jax.scipy.linalg.solve_triangular(lower, rows_in.T, lower=True).T


def plain_on_device(hidden, out_grad, prev_hidden, prev_grad, prev_basis, warm_start, *, norm_scale):
    highest = lax.Precision.HIGHEST
    replicas = lax.axis_size("dp")
    warm_low = warm_start.astype(BF16)
    projected = jnp.dot(out_grad, warm_low, preferred_element_type=F32).astype(BF16)
    projected_prev = jnp.dot(prev_grad, warm_low, preferred_element_type=F32).astype(BF16)
    coupling = jnp.dot(warm_start.T, warm_start, precision=highest)
    summed = jnp.einsum("tf,tr->fr", hidden, projected, preferred_element_type=F32)
    summed = summed + jnp.einsum(
        "tf,tr->fr", prev_hidden, projected_prev, preferred_element_type=F32
    )
    local_p = (summed - jnp.dot(prev_basis, coupling, precision=highest)) / replicas
    p_mean = lax.psum(local_p, "dp")
    gram_matrix = lax.psum(jnp.dot(p_mean.T, p_mean, precision=highest), "tensor")
    new_basis = orthonormal(p_mean, gram_matrix, norm_scale)
    basis_low = new_basis.astype(BF16)
    pulled = jnp.dot(hidden, basis_low, preferred_element_type=F32).astype(BF16)
    pulled_prev = jnp.dot(prev_hidden, basis_low, preferred_element_type=F32).astype(BF16)
    cross_basis = jnp.dot(prev_basis.T, new_basis, precision=highest)
    summed_q = jnp.einsum("td,tr->dr", out_grad, pulled, preferred_element_type=F32)
    summed_q = summed_q + jnp.einsum(
        "td,tr->dr", prev_grad, pulled_prev, preferred_element_type=F32
    )
    local_q = (summed_q - jnp.dot(warm_start, cross_basis, precision=highest)) / replicas
    row_count = warm_start.shape[0] // replicas
    summed_all = lax.psum(local_q, ("dp", "tensor"))
    owned_rows = lax.dynamic_slice_in_dim(
        summed_all, lax.axis_index("dp") * row_count, row_count, 0
    )
    return (new_basis, owned_rows / norm_scale)


def split(x, terms):
    parts = []
    for i in range(terms):
        part = x.astype(BF16)
        parts.append(part)
        if i + 1 < terms:
            x = x - part.astype(F32)
    return parts


def dot(a, b, dims, precision=None):
    return lax.dot_general(a, b, dims, preferred_element_type=F32, precision=precision)


def chunks(extent, count):
    step = extent // count
    return [pl.ds(i * step, step) for i in range(count)]


def store_pieces(pieces, cut, summed):
    rows = pieces[0].shape[0]
    for i, piece in enumerate(pieces):
        piece[:, cut] = summed[i * rows : (i + 1) * rows]


def first_term_kernel(w_ref, o_ref, o2_ref, h_ref, h2_ref, *refs):
    pieces, (y_ref, ov, hv, wv, sem) = refs[:SQUARE], refs[SQUARE:]
    q = lax.axis_index("dp") % SQUARE
    rows = wv.shape[0] // SQUARE
    tokens = o_ref.shape[0]
    first = pieces[0].shape[1]
    copies = []

    def copy(source, target):
        copies.append(pltpu.make_async_copy(source, target, sem.at[len(copies)]))
        copies[-1].start()
        return copies[-1]

    def stacked(cut, ref, ref2, target):
        return [
            copy(r.at[:, cut], target.at[pl.ds(j * tokens, tokens), cut]) for j, r in enumerate((ref, ref2))
        ]

    def wait(pending):
        for c in pending:
            c.wait()

    o_cuts, h_cuts = chunks(o_ref.shape[1], 4), chunks(first, 2)
    w_copies = [
        copy(w_ref.at[pl.ds((q ^ m) * rows, rows), :], wv.at[pl.ds(i * rows, rows), :])
        for i, m in enumerate(TERMS_AWAY)
    ]
    o_copies = [stacked(cut, o_ref, o2_ref, ov) for cut in o_cuts]
    h_copies = [stacked(cut, h_ref, h2_ref, hv) for cut in h_cuts]
    wait(w_copies)
    projected = jnp.zeros((wv.shape[0], 2 * tokens), F32)
    for i, cut in enumerate(o_cuts):
        wait(o_copies[i])
        projected += dot(wv[:, cut].astype(BF16), ov[:, cut], NT)
    rest = stacked(pl.ds(first, h_ref.shape[1] - first), h_ref, h2_ref, hv)
    y_ref[...] = projected
    projected = projected.astype(BF16)
    for i, cut in enumerate(h_cuts):
        wait(h_copies[i])
        store_pieces(pieces, cut, dot(projected, hv[:, cut], NN))
    wait(rest)


def second_term_kernel(y_ref, h_ref, *pieces):
    first = h_ref.shape[1] - pieces[0].shape[1]
    projected = y_ref[...].astype(BF16)
    for cut, units in cuts_of(pieces, first, 2):
        store_pieces(pieces, cut, dot(projected, h_ref[:, units], NN))


def feedback_kernel(w_ref, b_ref, after_ref, first_ref, rest_ref, c_ref):
    q = lax.axis_index("dp") % SQUARE
    rank = w_ref.shape[0]
    rows = rank // SQUARE
    total = jnp.zeros((3 * rank, 3 * rank), F32)
    for cut in chunks(w_ref.shape[1], 4):
        terms = jnp.concatenate(split(w_ref[:, cut], 3), axis=0)
        total += dot(terms, terms, NT)
    total = total[:rank] + total[rank : 2 * rank] + total[2 * rank :]
    c_ref[...] = total[:, :rank] + total[:, rank : 2 * rank] + total[:, 2 * rank :]
    coupling = jnp.concatenate(
        [c_ref[pl.ds((q ^ m) * rows, rows), :] for m in SUMS_AWAY], axis=0
    )
    first = 0
    for ref in (first_ref, rest_ref):
        for cut, units in cuts_of((ref,), first, 2):
            ref[:, cut] = dot(coupling, b_ref[:, units], NN, lax.Precision.HIGHEST)
        first += ref.shape[1]


def products(pieces, f_ref, h_ref, b_ref, p_ref, first):
    q = lax.axis_index("dp") % SQUARE
    rows = pieces[0].shape[0]
    rank = SQUARE * rows
    pulled = jnp.zeros((2 * rank, h_ref.shape[0]), F32)
    total = jnp.zeros((3 * rank, 6 * rank), F32)
    for cut, units in cuts_of(pieces, first, 2):
        p = jnp.concatenate([s[:, cut] for s in pieces], axis=0) - f_ref[:, cut]
        for i, m in enumerate(SUMS_AWAY):
            p_ref[pl.ds((q ^ m) * rows, rows), cut] = p[i * rows : (i + 1) * rows]
        pulled += dot(jnp.concatenate(split(p, 2), axis=0), h_ref[:, units], NT)
    for cut, units in cuts_of(pieces, first, 2):
        p = split(p_ref[:, cut], 3)
        b = split(b_ref[:, units], 3)
        total += dot(jnp.concatenate(p, axis=0), jnp.concatenate(p + b, axis=0), NT)
    pulled = pulled[:rank] + pulled[rank:]
    total = total[:rank] + total[rank : 2 * rank] + total[2 * rank :]
    gram = total[:, :rank] + total[:, rank : 2 * rank] + total[:, 2 * rank : 3 * rank]
    cross = total[:, 3 * rank : 4 * rank] + total[:, 4 * rank : 5 * rank] + total[:, 5 * rank :]
    grams = jnp.concatenate([gram, cross, jnp.zeros((rank, 128 - 2 * rank), F32)], axis=1)
    return pulled, grams


def cuts_of(pieces, first, count):
    cuts = chunks(pieces[0].shape[1], count)
    return [(cut, pl.ds(first + cut.start, cut.size)) for cut in cuts]


def first_pull_kernel(s0, s1, s2, s3, f_ref, h_ref, b_ref, p_ref, v_ref, g_ref):
    v_ref[...], g_ref[...] = products((s0, s1, s2, s3), f_ref, h_ref, b_ref, p_ref, 0)


def pull_kernel(s0, s1, s2, s3, f_ref, h_ref, b_ref, v_ref, g_ref, p_ref, keep_ref, send_ref, t_ref):
    q = lax.axis_index("dp") % SQUARE
    core = lax.axis_index("tensor") % 2
    rows, half, tokens = s0.shape[0], keep_ref.shape[0], h_ref.shape[0]
    first = h_ref.shape[1] - s0.shape[1]
    pulled, grams = products((s0, s1, s2, s3), f_ref, h_ref, b_ref, p_ref, first)
    pulled += v_ref[...]
    grams += g_ref[...]
    for i, m in enumerate(SUMS_AWAY):
        t_ref[pl.ds((q ^ m) * rows, rows), :] = pulled[i * rows : (i + 1) * rows]
    keep_ref[:, :tokens] = t_ref[pl.ds(core * half, half), :]
    send_ref[:, :tokens] = t_ref[pl.ds((1 - core) * half, half), :]
    for ref in (keep_ref, send_ref):
        ref[:, tokens : tokens + 128] = grams[:half]
        ref[:, tokens + 128 :] = grams[half:]


def push_kernel(mine_ref, got_ref, o_ref, *outs):
    me = lax.axis_index("dp")
    tokens = o_ref.shape[0]
    half, width = outs[0].shape[1:]
    v = jnp.concatenate(split(mine_ref[:, :tokens] + got_ref[:, :tokens], 2), axis=0)
    for i, m in enumerate(RIGHT_AWAY):
        for z in range(2):
            cut = pl.ds(pl.multiple_of((me ^ m ^ (SQUARE * z)) * width, width), width)
            both = dot(v, o_ref[:, cut], NN)
            outs[i][z] = both[:half] + both[half:]


def cholesky_kernel(mine_ref, got_ref, out_ref):
    rank, lanes = out_ref.shape
    shape = out_ref.shape
    tokens = mine_ref.shape[1] - 2 * lanes
    grams = mine_ref[:, tokens:] + got_ref[:, tokens:]
    grams = jnp.concatenate([grams[:, :lanes], grams[:, lanes:]], axis=0)
    row = lax.broadcasted_iota(jnp.int32, shape, 0)
    lane = lax.broadcasted_iota(jnp.int32, shape, 1)
    a = jnp.where(lane == row + 2 * rank, 1.0, grams)
    for k in range(rank):
        pivot = a[k : k + 1, k : k + 1]
        scale = 1.0 / jnp.sqrt(pivot)
        top = a[k : k + 1, :] * scale
        below = jnp.where(row[:, :1] > k, a[:, k : k + 1] * scale, 0.0)
        a = jnp.where(row == k, top, a - below * top)
    out_ref[...] = a


def near_far_kernel(a_ref, b_ref, c_ref, d_ref, after_ref, near_ref, far_ref):
    near_ref[...] = a_ref[0] + b_ref[0] + c_ref[0] + d_ref[0]
    far_ref[...] = a_ref[1] + b_ref[1] + c_ref[1] + d_ref[1]


def total_kernel(a_ref, b_ref, after_ref, out_ref):
    out_ref[...] = a_ref[...] + b_ref[...]


def basis_kernel(p_ref, r_ref, l_ref, w_ref, out_ref, fix_ref, *, norm_scale):
    rank = l_ref.shape[0]
    width = fix_ref.shape[1]
    highest = lax.Precision.HIGHEST
    inverse = l_ref[:, 2 * rank : 3 * rank] * norm_scale
    first = 0
    for ref in (p_ref, r_ref):
        for cut, units in cuts_of((ref,), first, 2):
            out_ref[:, units] = dot(inverse, ref[:, cut], NN, highest)
        first += ref.shape[1]
    own = pl.ds(pl.multiple_of(lax.axis_index("dp") * width, width), width)
    fix_ref[...] = dot(l_ref[:, rank : 2 * rank], w_ref[:, own], NN, highest)


def factor_kernel(t_ref, u_ref, l_ref, fix_ref, out_ref, z_ref, *, replicas):
    core = lax.axis_index("tensor") % 2
    half = t_ref.shape[0]
    rank = 2 * half
    z_ref[pl.ds(core * half, half), :] = t_ref[...]
    z_ref[pl.ds((1 - core) * half, half), :] = u_ref[...]
    inverse = l_ref[:, 2 * rank : 3 * rank] * (1.0 / replicas)
    out_ref[...] = dot(inverse, z_ref[...], NN, lax.Precision.HIGHEST) - fix_ref[...]


def call(kernel, outs, specs, scratch=(), flops=0, moved=0, vmem=32 << 20):
    return pl.pallas_call(
        kernel,
        out_shape=[jax.ShapeDtypeStruct(shape[:2] if BF16 in shape else shape, BF16 if BF16 in shape else F32) for shape in outs],
        in_specs=specs,
        out_specs=[VMEM_SPEC] * len(outs),
        scratch_shapes=scratch,
        compiler_params=pltpu.CompilerParams(vmem_limit_bytes=vmem),
        cost_estimate=pl.CostEstimate(flops=flops, bytes_accessed=moved, transcendentals=0),
    )


def in_hbm(x):
    return pltpu.with_memory_space_constraint(x, pltpu.HBM)


def swap_dp(x, m):
    n = lax.axis_size("dp")
    return lax.ppermute(x, "dp", [(i, i ^ m) for i in range(n)])


def swap_tensor(x, m):
    n = lax.axis_size("tensor")
    return lax.ppermute(x, "tensor", [(i, i ^ m) for i in range(n)])


def on_device(hidden, out_grad, prev_hidden, prev_grad, prev_basis, warm_start, *, norm_scale):
    replicas = lax.axis_size("dp")
    tokens, units = hidden.shape
    width = out_grad.shape[1]
    rank = warm_start.shape[1]
    rows, half, owned = rank // SQUARE, rank // 2, width // replicas
    w, b = warm_start.T, prev_basis.T
    first = units // 256 * 128
    rest = units - first

    *terms, projected, out_grads, hiddens = call(
        first_term_kernel,
        [(rows, first)] * SQUARE + [(rank, 2 * tokens), (2 * tokens, width, BF16), (2 * tokens, units, BF16)],
        [HBM_SPEC] * 5,
        [pltpu.VMEM((rank, width), F32), pltpu.SemaphoreType.DMA((18,))],
        flops=4 * tokens * rank * (first + width),
        moved=4 * tokens * (units + width) + 4 * rank * (first + width),
    )(*[in_hbm(x) for x in (w, out_grad, prev_grad, hidden, prev_hidden)])
    late_terms = call(
        second_term_kernel,
        [(rows, rest)] * SQUARE,
        [VMEM_SPEC] * 2,
        flops=4 * tokens * rank * rest,
        moved=4 * tokens * rest + 4 * rank * rest,
    )(projected, hiddens)

    def swap_square(x, away):
        return [swap_dp(x[i], m) for i, m in enumerate(away) if m]

    def mean(summed, came):
        own = (summed + came) * (1.0 / replicas)
        return [own] + swap_square([own] * SQUARE, SUMS_AWAY)

    early = terms[0] + sum(swap_square(terms, TERMS_AWAY))
    early_came = swap_dp(early, SQUARE)
    late = late_terms[0] + sum(swap_square(late_terms, TERMS_AWAY))
    late_came = swap_dp(late, SQUARE)
    early_feedback, late_feedback = call(
        feedback_kernel,
        [(rank, first), (rank, rest)],
        [VMEM_SPEC] * 2 + [ANY_SPEC],
        [pltpu.VMEM((rank, rank), F32)],
        flops=2 * rank * rank * (units + width),
        moved=4 * rank * (units + width),
    )(w, b, late)
    early_came, early_feedback = lax.optimization_barrier((early_came, early_feedback))
    early_p = mean(early, early_came)
    late_p = mean(late, late_came)

    p_first, early_v, early_gram = call(
        first_pull_kernel,
        [(rank, first), (rank, 2 * tokens), (rank, 128)],
        [VMEM_SPEC] * 7,
        flops=8 * tokens * rank * first,
        moved=4 * tokens * first + 4 * rank * first,
    )(*early_p, early_feedback, hiddens, b)
    p_rest, keep, send = call(
        pull_kernel,
        [(rank, rest)] + [(half, 2 * tokens + 256)] * 2,
        [VMEM_SPEC] * 9,
        [pltpu.VMEM((rank, 2 * tokens), F32)],
        flops=8 * tokens * rank * rest,
        moved=4 * tokens * rest + 4 * rank * rest,
    )(*late_p, late_feedback, hiddens, b, early_v, early_gram)
    plane = keep + swap_tensor(send, 1)
    plane_came = swap_tensor(plane, 2)
    parts = call(
        push_kernel,
        [(2, half, owned)] * SQUARE,
        [VMEM_SPEC] * 3,
        flops=8 * tokens * half * width,
        moved=4 * tokens * width + 4 * half * width,
    )(plane, plane_came, out_grads)
    came = swap_square(parts, RIGHT_AWAY)
    (solved,) = call(
        cholesky_kernel, [(rank, 128)], [VMEM_SPEC] * 2, flops=rank**3, moved=8 * rank * 128
    )(plane, plane_came)
    near, far = call(
        near_far_kernel,
        [(half, owned)] * 2,
        [VMEM_SPEC] * 4 + [ANY_SPEC],
        flops=6 * half * owned,
        moved=40 * half * owned,
    )(parts[0], *came, solved)
    basis, fix = call(
        functools.partial(basis_kernel, norm_scale=norm_scale),
        [(rank, units), (rank, owned)],
        [VMEM_SPEC] * 4,
        flops=2 * rank * rank * units,
        moved=8 * rank * units,
    )(p_first, p_rest, solved, w)
    (mine,) = call(
        total_kernel,
        [(half, owned)],
        [VMEM_SPEC] * 2 + [ANY_SPEC],
        flops=half * owned,
        moved=12 * half * owned,
    )(near, swap_dp(far, SQUARE), fix)
    (factor,) = call(
        functools.partial(factor_kernel, replicas=replicas),
        [(rank, owned)],
        [VMEM_SPEC] * 4,
        [pltpu.VMEM((rank, owned), F32)],
        flops=2 * rank * rank * owned,
        moved=12 * rank * owned,
    )(mine, swap_tensor(mine, 1), solved, fix)
    return (basis.T, factor.T)


def fits(mesh, dp=8, tensor=4):
    return mesh.shape["dp"] == dp and mesh.shape["tensor"] == tensor


def solution(mesh):
    def whole(hidden, out_grad, prev_hidden, prev_grad, prev_basis, warm_start):
        norm_scale = float(prev_basis.shape[0]) ** 0.5
        body = on_device if fits(mesh) else plain_on_device
        return jax.shard_map(
            functools.partial(body, norm_scale=norm_scale),
            mesh=mesh,
            in_specs=(
                P("dp", "tensor"),
                P("dp", None),
                P("dp", "tensor"),
                P("dp", None),
                P("tensor", None),
                P(),
            ),
            out_specs=(P("tensor", None), P("dp", None)),
            check_vma=False,
        )(hidden, out_grad, prev_hidden, prev_grad, prev_basis, warm_start)

    return whole
```

time: 67.2 us -> 62.9 us (0.936)
  waiting for transfers between devices: 20.1 us -> 17.5 us
  Pallas kernels: 18.2 us -> 16.9 us
    ppermute x5 -> x3, starting transfers between devices: 3.78 us -> 1.61 us  [swap_tensor(): return lax.ppermute(x, 'tensor', [(i, i ^ m) for i in range(n)])]
    ppermute x18, starting transfers between devices: 24 us -> 25.9 us  [swap_dp(): return lax.ppermute(x, 'dp', [(i, i ^ m) for i in range(n)])]
    ppermute x18, waiting for transfers between devices: 14.4 us -> 12.7 us  [swap_dp(): return lax.ppermute(x, 'dp', [(i, i ^ m) for i in range(n)])]
    pallas_call x8 -> x7, Pallas kernels: 15.4 us -> 14.1 us  [the longest x1 4.97 us: on_device(): call(first_term_kernel, [(rows, first)] * SQUARE + [(rank, 2 * tokens), (...]
    ppermute x5 -> x3, waiting for transfers between devices: 5.67 us -> 4.83 us  [swap_tensor(): return lax.ppermute(x, 'tensor', [(i, i ^ m) for i in range(n)])]
  transfers between devices with their start and end apart: 23 -> 21, of which waited for: 12 -> 16; matrix products, arithmetic and copies ran while one was open for 0% -> 0% of each run, Pallas kernels for 16% -> 14%
where the time goes in v4:
time: 62.9 us; the launch traced here: 62.8 us
  starting transfers between devices  27.5 us (44%)
  waiting for transfers between devices  17.5 us (28%)
  Pallas kernels  16.9 us (27%)
  between operations  0.72 us (1%)
    ppermute x18, starting transfers between devices, swap_dp(): return lax.ppermute(x, 'dp', [(i, i ^ m) for i in range(n)])  25.9 us
    ppermute x18, waiting for transfers between devices, swap_dp(): return lax.ppermute(x, 'dp', [(i, i ^ m) for i in range(n)])  12.7 us
    pallas_call x1, Pallas kernels, on_device(): call(first_term_kernel, [(rows, first)] * SQUARE + [(rank, 2 * tokens), (...  4.97 us
    ppermute x3, waiting for transfers between devices, swap_tensor(): return lax.ppermute(x, 'tensor', [(i, i ^ m) for i in range(n)])  4.83 us
    pallas_call x1, Pallas kernels, on_device(): call(cholesky_kernel, [(rank, 128)], [VMEM_SPEC] * 2, flops=rank ** 3, mo...  3.01 us
    pallas_call x1, Pallas kernels, on_device(): call(feedback_kernel, [(rank, first), (rank, rest)], [VMEM_SPEC] * 2 + [A...  2.36 us
    pallas_call x1, Pallas kernels, on_device(): call(functools.partial(basis_kernel, norm_scale=norm_scale), [(rank, unit...  1.84 us
    ppermute x3, starting transfers between devices, swap_tensor(): return lax.ppermute(x, 'tensor', [(i, i ^ m) for i in range(n)])  1.61 us
  transfers between devices with their start and end apart: 21, of which 16 were waited for; matrix products, arithmetic and copies ran while one was open for 0% of the time, Pallas kernels for 14%

profile of v4, /device:TPU:0, one launch (start us, length us, event | category | flops | bytes accessed | tf_op | source)
XLA Modules:
  0.0 62.8 jit_solution(2679147706241972554)
XLA Ops:
  0.6 5.0 %shard_map.77 = (f32[8,3584]{1,0:T(8,128)S(1)}, f32[8,3584]{1,0:T(8,128)S(1)}, f32[8,3584]{1,0:T(8,128)S(1)}, f32[8,3584]{1,0:T(8,128)S(1)}, f32[32,256]{1,0:T(8...) custom-call(f32[32,8192]{1,0:T(8,128)} %bitcast.4, bf16[128,8192]{1,0:T(8,128)(2,1)} %o_ref.1, ...), custom_call_target="tpu_custom_call" | custom-call | flops 192937984 | bytes 9371648 | tf_op jit(solution)/shard_map/pallas_call | solution.py:303
  5.6 3.0 %collective-permute-start.2 = (f32[8,3584]{1,0:T(8,128)S(1)}, f32[8,3584]{1,0:T(8,128)S(1)}, u32[]{:S(2)}, u32[]{:S(2)}) collective-permute-start(f32[8,3584]{1,0:T(8,128)S(1)} %get-tuple-element.34), channel_id=1, source_target_pairs={{0,4},{4,0},{8,12},{12,8},{16,20},{20,16},{24,28},{28,24},{1,5},{5... | collective-permute-start | bytes 344072 | tf_op jit(solution)/shard_map/ppermute | solution.py:285
  8.6 1.5 %collective-permute-start = (f32[8,3584]{1,0:T(8,128)S(1)}, f32[8,3584]{1,0:T(8,128)S(1)}, u32[]{:S(2)}, u32[]{:S(2)}) collective-permute-start(f32[8,3584]{1,0:T(8,128)S(1)} %get-tuple-element.32), channel_id=1, source_target_pairs={{0,12},{4,8},{8,4},{12,0},{16,28},{20,24},{24,20},{28,16},{1,13},{... | collective-permute-start | bytes 344072 | tf_op jit(solution)/shard_map/ppermute | solution.py:285
  10.6 1.9 %collective-permute-start.6 = (f32[8,3584]{1,0:T(8,128)S(1)}, f32[8,3584]{1,0:T(8,128)S(1)}, u32[]{:S(2)}, u32[]{:S(2)}) collective-permute-start(f32[8,3584]{1,0:T(8,128)S(1)} %get-tuple-element.40), channel_id=1, source_target_pairs={{0,4},{4,0},{8,12},{12,8},{16,20},{20,16},{24,28},{28,24},{1,5},{5... | collective-permute-start | bytes 344072 | tf_op jit(solution)/shard_map/ppermute | solution.py:285
  12.6 1.5 %collective-permute-start.4 = (f32[8,3584]{1,0:T(8,128)S(1)}, f32[8,3584]{1,0:T(8,128)S(1)}, u32[]{:S(2)}, u32[]{:S(2)}) collective-permute-start(f32[8,3584]{1,0:T(8,128)S(1)} %get-tuple-element.38), channel_id=1, source_target_pairs={{0,12},{4,8},{8,4},{12,0},{16,28},{20,24},{24,20},{28,16},{1,13},{... | collective-permute-start | bytes 344072 | tf_op jit(solution)/shard_map/ppermute | solution.py:285
  15.1 1.2 %collective-permute-start.5 = (f32[8,3584]{1,0:T(8,128)S(1)}, f32[8,3584]{1,0:T(8,128)S(1)}, u32[]{:S(2)}, u32[]{:S(2)}) collective-permute-start(f32[8,3584]{1,0:T(8,128)S(1)} %get-tuple-element.39), channel_id=1, source_target_pairs={{0,8},{4,12},{8,0},{12,4},{16,24},{20,28},{24,16},{28,20},{1,9},{5... | collective-permute-start | bytes 344072 | tf_op jit(solution)/shard_map/ppermute | solution.py:285
  16.7 3.1 %collective-permute-start.3 = (f32[8,3584]{1,0:T(8,128)S(1)}, f32[8,3584]{1,0:T(8,128)S(1)}, u32[]{:S(2)}, u32[]{:S(2)}) collective-permute-start(f32[8,3584]{1,0:T(8,128)S(1)} %add_add_fusion.1), channel_id=1, source_target_pairs={{0,16},{4,20},{8,24},{12,28},{16,0},{20,4},{24,8},{28,12},{1,17},{... | collective-permute-start | bytes 344072 | tf_op jit(solution)/shard_map/ppermute | solution.py:285
  19.7 1.8 %collective-permute-done.4 = f32[8,3584]{1,0:T(8,128)S(1)} collective-permute-done((f32[8,3584]{1,0:T(8,128)S(1)}, f32[8,3584]{1,0:T(8,128)S(1)}, u32[]{:S(2)}, u32[]{:S(2)}) %collective-permute-start.4) | collective-permute-done | bytes 114720 | tf_op jit(solution)/shard_map/ppermute | solution.py:285
  22.2 2.4 %collective-permute-start.10 = (f32[8,3584]{1,0:T(8,128)S(1)}, f32[8,3584]{1,0:T(8,128)S(1)}, u32[]{:S(2)}, u32[]{:S(2)}) collective-permute-start(f32[8,3584]{1,0:T(8,128)S(1)} %add_add_fusion.after_ref), channel_id=1, source_target_pairs={{0,16},{4,20},{8,24},{12,28},{16,0},{20,4},{24,8},{28,12},{1,17},{... | collective-permute-start | bytes 344072 | tf_op jit(solution)/shard_map/ppermute | solution.py:285
  24.5 2.4 %shard_map.79 = (f32[32,3584]{1,0:T(8,128)S(1)}, f32[32,3584]{1,0:T(8,128)S(1)}) custom-call(f32[32,8192]{1,0:T(8,128)S(1)} %bitcast.5, f32[32,7168]{1,0:T(8,128)S(1)} %bitcast.7, f32[8,3584]{1,0:T(8,128)S(1)} %add_add_fusion.after_ref), custom_call_target="tpu_custom_call" | custom-call | flops 31457280 | bytes 1966080 | tf_op jit(solution)/shard_map/pallas_call | solution.py:330
  26.9 3.2 %collective-permute-start.7 = (f32[8,3584]{1,0:T(8,128)S(1)}, f32[8,3584]{1,0:T(8,128)S(1)}, u32[]{:S(2)}, u32[]{:S(2)}) collective-permute-start(f32[8,3584]{1,0:T(8,128)S(1)} %add_multiply_fusion.1.s0), channel_id=1, source_target_pairs={{0,12},{4,8},{8,4},{12,0},{16,28},{20,24},{24,20},{28,16},{1,13},{... | collective-permute-start | bytes 344072 | tf_op jit(solution)/shard_map/ppermute | solution.py:285
  30.8 2.9 %collective-permute-start.11 = (f32[8,3584]{1,0:T(8,128)S(1)}, f32[8,3584]{1,0:T(8,128)S(1)}, u32[]{:S(2)}, u32[]{:S(2)}) collective-permute-start(f32[8,3584]{1,0:T(8,128)S(1)} %add_multiply_fusion.s0), channel_id=1, source_target_pairs={{0,12},{4,8},{8,4},{12,0},{16,28},{20,24},{24,20},{28,16},{1,13},{... | collective-permute-start | bytes 344072 | tf_op jit(solution)/shard_map/ppermute | solution.py:285
  34.4 1.6 %collective-permute-done.8.s2 = f32[8,3584]{1,0:T(8,128)S(1)} collective-permute-done((f32[8,3584]{1,0:T(8,128)S(1)}, f32[8,3584]{1,0:T(8,128)S(1)}, u32[]{:S(2)}, u32[]{:S(2)}) %collective-permute-start.8) | collective-permute-done | bytes 114720 | tf_op jit(solution)/shard_map/ppermute | solution.py:285
  36.8 1.2 %shard_map.80 = (f32[32,3584]{1,0:T(8,128)S(1)}, f32[32,256]{1,0:T(8,128)S(1)}, f32[32,128]{1,0:T(8,128)S(1)}) custom-call(f32[8,3584]{1,0:T(8,128)S(1)} %add_multiply_fusion.1.s0, f32[8,3584]{1,0:T(8,128)S(1)} %collective-permute-done.7.s1, f32[8,3584]{1,0:T(8,128)S(1)} %collective-permute-done.8.s2, f32[8,3584]{1,0:T(8,128)S(1)} %collective-permute-done.9.s3, ...), custom_call_target="tpu_custom_call" | custom-call | flops 117440512 | bytes 2293760 | tf_op jit(solution)/shard_map/pallas_call | solution.py:342
  39.9 1.3 %shard_map.81 = (f32[32,3584]{1,0:T(8,128)S(1)}, f32[16,512]{1,0:T(8,128)S(1)}, f32[16,512]{1,0:T(8,128)S(1)}) custom-call(f32[8,3584]{1,0:T(8,128)S(1)} %add_multiply_fusion.s0, f32[8,3584]{1,0:T(8,128)S(1)} %collective-permute-done.11.s1, f32[8,3584]{1,0:T(8,128)S(1)} %collective-permute-done.12.s2, f32[8,3584]{1,0:T(8,128)S(1)} %collective-permute-done.13.s3, ...), custom_call_target="tpu_custom_call" | custom-call | flops 117440512 | bytes 2293760 | tf_op jit(solution)/shard_map/pallas_call | solution.py:349
  41.1 1.2 %collective-permute-done.14 = f32[16,512]{1,0:T(8,128)S(1)} collective-permute-done((f32[16,512]{1,0:T(8,128)S(1)}, f32[16,512]{1,0:T(8,128)S(1)}, u32[]{:S(2)}, u32[]{:S(2)}) %collective-permute-start.14) | collective-permute-done | bytes 32800 | tf_op jit(solution)/shard_map/ppermute | solution.py:290
  42.3 1.5 %collective-permute-start.15 = (f32[16,512]{1,0:T(8,128)S(1)}, f32[16,512]{1,0:T(8,128)S(1)}, u32[]{:S(2)}, u32[]{:S(2)}) collective-permute-start(f32[16,512]{1,0:T(8,128)S(1)} %add.35.mine_ref), channel_id=1, source_target_pairs={{0,2},{1,3},{2,0},{3,1},{4,6},{5,7},{6,4},{7,5},{8,10},{9,11},{10,... | collective-permute-start | bytes 98312 | tf_op jit(solution)/shard_map/ppermute | solution.py:290
  43.9 2.4 %collective-permute-done.15.got_ref = f32[16,512]{1,0:T(8,128)S(1)} collective-permute-done((f32[16,512]{1,0:T(8,128)S(1)}, f32[16,512]{1,0:T(8,128)S(1)}, u32[]{:S(2)}, u32[]{:S(2)}) %collective-permute-start.15) | collective-permute-done | bytes 32800 | tf_op jit(solution)/shard_map/ppermute | solution.py:290
  47.1 1.7 %collective-permute-start.16 = (f32[2,16,1024]{2,1,0:T(8,128)S(1)}, f32[2,16,1024]{2,1,0:T(8,128)S(1)}, u32[]{:S(2)}, u32[]{:S(2)}) collective-permute-start(f32[2,16,1024]{2,1,0:T(8,128)S(1)} %get-tuple-element.54), channel_id=1, source_target_pairs={{0,12},{4,8},{8,4},{12,0},{16,28},{20,24},{24,20},{28,16},{1,13},{... | collective-permute-start | bytes 393224 | tf_op jit(solution)/shard_map/ppermute | solution.py:285
  49.2 1.4 %collective-permute-start.18 = (f32[2,16,1024]{2,1,0:T(8,128)S(1)}, f32[2,16,1024]{2,1,0:T(8,128)S(1)}, u32[]{:S(2)}, u32[]{:S(2)}) collective-permute-start(f32[2,16,1024]{2,1,0:T(8,128)S(1)} %get-tuple-element.56), channel_id=1, source_target_pairs={{0,4},{4,0},{8,12},{12,8},{16,20},{20,16},{24,28},{28,24},{1,5},{5... | collective-permute-start | bytes 393224 | tf_op jit(solution)/shard_map/ppermute | solution.py:285
  50.6 3.0 %shard_map.82.l_ref.after_ref = f32[32,128]{1,0:T(8,128)S(1)} custom-call(f32[16,512]{1,0:T(8,128)S(1)} %add.35.mine_ref, f32[16,512]{1,0:T(8,128)S(1)} %collective-permute-done.15.got_ref), custom_call_target="tpu_custom_call" | custom-call | flops 32768 | bytes 32768 | tf_op jit(solution)/shard_map/pallas_call | solution.py:367
  55.9 1.8 %shard_map.83 = (f32[32,7168]{1,0:T(8,128)}, f32[32,1024]{1,0:T(8,128)S(1)}) custom-call(f32[32,3584]{1,0:T(8,128)S(1)} %get-tuple-element.44.p_ref, f32[32,3584]{1,0:T(8,128)S(1)} %get-tuple-element.48.r_ref, f32[32,128]{1,0:T(8,128)S(1)} %shard_map.82.l_ref.after_ref, f32[32,8192]{1,0:T(8,128)S(1)} %bitcast.6), custom_call_target="tpu_custom_call" | custom-call | flops 14680064 | bytes 1835008 | tf_op jit(solution)/shard_map/pallas_call | solution.py:377
  57.7 2.7 %collective-permute-done.19.b_ref = f32[16,1024]{1,0:T(8,128)S(1)} collective-permute-done((f32[16,1024]{1,0:T(8,128)S(1)}, f32[16,1024]{1,0:T(8,128)S(1)}, u32[]{:S(2)}, u32[]{:S(2)}) %collective-permute-start.19) | collective-permute-done | bytes 65568 | tf_op jit(solution)/shard_map/ppermute | solution.py:285
  60.5 1.2 %collective-permute-done.20.u_ref = f32[16,1024]{1,0:T(8,128)S(1)} collective-permute-done((f32[16,1024]{1,0:T(8,128)S(1)}, f32[16,1024]{1,0:T(8,128)S(1)}, u32[]{:S(2)}, u32[]{:S(2)}) %collective-permute-start.20) | collective-permute-done | bytes 65568 | tf_op jit(solution)/shard_map/ppermute | solution.py:290
  (38 shorter events, 11.0 us)
Async XLA Ops:
  5.6 9.5 %collective-permute-start.2 = (f32[8,3584]{1,0:T(8,128)S(1)}, f32[8,3584]{1,0:T(8,128)S(1)}, u32[]{:S(2)}, u32[]{:S(2)}) collective-permute-start(f32[8,3584]{1,0:T(8,128)S(1)} %get-tuple-element.34), channel_id=1, source_target_pairs={{0,4},{4,0},{8,12},{12,8},{16,20},{20,16},{24,28},{28,24},{1,5},{5... | collective-permute-start | bytes 344072 | tf_op jit(solution)/shard_map/ppermute | solution.py:285
  8.6 7.7 %collective-permute-start = (f32[8,3584]{1,0:T(8,128)S(1)}, f32[8,3584]{1,0:T(8,128)S(1)}, u32[]{:S(2)}, u32[]{:S(2)}) collective-permute-start(f32[8,3584]{1,0:T(8,128)S(1)} %get-tuple-element.32), channel_id=1, source_target_pairs={{0,12},{4,8},{8,4},{12,0},{16,28},{20,24},{24,20},{28,16},{1,13},{... | collective-permute-start | bytes 344072 | tf_op jit(solution)/shard_map/ppermute | solution.py:285
  10.2 6.5 %collective-permute-start.1 = (f32[8,3584]{1,0:T(8,128)S(1)}, f32[8,3584]{1,0:T(8,128)S(1)}, u32[]{:S(2)}, u32[]{:S(2)}) collective-permute-start(f32[8,3584]{1,0:T(8,128)S(1)} %get-tuple-element.33), channel_id=1, source_target_pairs={{0,8},{4,12},{8,0},{12,4},{16,24},{20,28},{24,16},{28,20},{1,9},{5... | collective-permute-start | bytes 344072 | tf_op jit(solution)/shard_map/ppermute | solution.py:285
  10.2 14.4 %copy-start = (f32[8192,32]{0,1:T(8,128)S(1)}, f32[8192,32]{0,1:T(8,128)}, u32[]{:S(2)}) copy-start(f32[8192,32]{0,1:T(8,128)} %param.11) | copy-start | bytes 3145732
  10.2 14.4 %copy-start.1 = (f32[7168,32]{0,1:T(8,128)S(1)}, f32[7168,32]{0,1:T(8,128)}, u32[]{:S(2)}) copy-start(f32[7168,32]{0,1:T(8,128)} %param.10) | copy-start | bytes 2752516
  10.6 9.1 %collective-permute-start.6 = (f32[8,3584]{1,0:T(8,128)S(1)}, f32[8,3584]{1,0:T(8,128)S(1)}, u32[]{:S(2)}, u32[]{:S(2)}) collective-permute-start(f32[8,3584]{1,0:T(8,128)S(1)} %get-tuple-element.40), channel_id=1, source_target_pairs={{0,4},{4,0},{8,12},{12,8},{16,20},{20,16},{24,28},{28,24},{1,5},{5... | collective-permute-start | bytes 344072 | tf_op jit(solution)/shard_map/ppermute | solution.py:285
  12.6 9.0 %collective-permute-start.4 = (f32[8,3584]{1,0:T(8,128)S(1)}, f32[8,3584]{1,0:T(8,128)S(1)}, u32[]{:S(2)}, u32[]{:S(2)}) collective-permute-start(f32[8,3584]{1,0:T(8,128)S(1)} %get-tuple-element.38), channel_id=1, source_target_pairs={{0,12},{4,8},{8,4},{12,0},{16,28},{20,24},{24,20},{28,16},{1,13},{... | collective-permute-start | bytes 344072 | tf_op jit(solution)/shard_map/ppermute | solution.py:285
  15.1 7.0 %collective-permute-start.5 = (f32[8,3584]{1,0:T(8,128)S(1)}, f32[8,3584]{1,0:T(8,128)S(1)}, u32[]{:S(2)}, u32[]{:S(2)}) collective-permute-start(f32[8,3584]{1,0:T(8,128)S(1)} %get-tuple-element.39), channel_id=1, source_target_pairs={{0,8},{4,12},{8,0},{12,4},{16,24},{20,28},{24,16},{28,20},{1,9},{5... | collective-permute-start | bytes 344072 | tf_op jit(solution)/shard_map/ppermute | solution.py:285
  16.7 10.3 %collective-permute-start.3 = (f32[8,3584]{1,0:T(8,128)S(1)}, f32[8,3584]{1,0:T(8,128)S(1)}, u32[]{:S(2)}, u32[]{:S(2)}) collective-permute-start(f32[8,3584]{1,0:T(8,128)S(1)} %add_add_fusion.1), channel_id=1, source_target_pairs={{0,16},{4,20},{8,24},{12,28},{16,0},{20,4},{24,8},{28,12},{1,17},{... | collective-permute-start | bytes 344072 | tf_op jit(solution)/shard_map/ppermute | solution.py:285
  22.2 8.6 %collective-permute-start.10 = (f32[8,3584]{1,0:T(8,128)S(1)}, f32[8,3584]{1,0:T(8,128)S(1)}, u32[]{:S(2)}, u32[]{:S(2)}) collective-permute-start(f32[8,3584]{1,0:T(8,128)S(1)} %add_add_fusion.after_ref), channel_id=1, source_target_pairs={{0,16},{4,20},{8,24},{12,28},{16,0},{20,4},{24,8},{28,12},{1,17},{... | collective-permute-start | bytes 344072 | tf_op jit(solution)/shard_map/ppermute | solution.py:285
  26.9 7.1 %collective-permute-start.7 = (f32[8,3584]{1,0:T(8,128)S(1)}, f32[8,3584]{1,0:T(8,128)S(1)}, u32[]{:S(2)}, u32[]{:S(2)}) collective-permute-start(f32[8,3584]{1,0:T(8,128)S(1)} %add_multiply_fusion.1.s0), channel_id=1, source_target_pairs={{0,12},{4,8},{8,4},{12,0},{16,28},{20,24},{24,20},{28,16},{1,13},{... | collective-permute-start | bytes 344072 | tf_op jit(solution)/shard_map/ppermute | solution.py:285
  30.1 5.8 %collective-permute-start.8 = (f32[8,3584]{1,0:T(8,128)S(1)}, f32[8,3584]{1,0:T(8,128)S(1)}, u32[]{:S(2)}, u32[]{:S(2)}) collective-permute-start(f32[8,3584]{1,0:T(8,128)S(1)} %add_multiply_fusion.1.s0), channel_id=1, source_target_pairs={{0,8},{4,12},{8,0},{12,4},{16,24},{20,28},{24,16},{28,20},{1,9},{5... | collective-permute-start | bytes 344072 | tf_op jit(solution)/shard_map/ppermute | solution.py:285
  30.1 6.6 %collective-permute-start.9 = (f32[8,3584]{1,0:T(8,128)S(1)}, f32[8,3584]{1,0:T(8,128)S(1)}, u32[]{:S(2)}, u32[]{:S(2)}) collective-permute-start(f32[8,3584]{1,0:T(8,128)S(1)} %add_multiply_fusion.1.s0), channel_id=1, source_target_pairs={{0,4},{4,0},{8,12},{12,8},{16,20},{20,16},{24,28},{28,24},{1,5},{5... | collective-permute-start | bytes 344072 | tf_op jit(solution)/shard_map/ppermute | solution.py:285
  30.8 7.9 %collective-permute-start.11 = (f32[8,3584]{1,0:T(8,128)S(1)}, f32[8,3584]{1,0:T(8,128)S(1)}, u32[]{:S(2)}, u32[]{:S(2)}) collective-permute-start(f32[8,3584]{1,0:T(8,128)S(1)} %add_multiply_fusion.s0), channel_id=1, source_target_pairs={{0,12},{4,8},{8,4},{12,0},{16,28},{20,24},{24,20},{28,16},{1,13},{... | collective-permute-start | bytes 344072 | tf_op jit(solution)/shard_map/ppermute | solution.py:285
  33.7 6.1 %collective-permute-start.12 = (f32[8,3584]{1,0:T(8,128)S(1)}, f32[8,3584]{1,0:T(8,128)S(1)}, u32[]{:S(2)}, u32[]{:S(2)}) collective-permute-start(f32[8,3584]{1,0:T(8,128)S(1)} %add_multiply_fusion.s0), channel_id=1, source_target_pairs={{0,8},{4,12},{8,0},{12,4},{16,24},{20,28},{24,16},{28,20},{1,9},{5... | collective-permute-start | bytes 344072 | tf_op jit(solution)/shard_map/ppermute | solution.py:285
  34.0 5.8 %collective-permute-start.13 = (f32[8,3584]{1,0:T(8,128)S(1)}, f32[8,3584]{1,0:T(8,128)S(1)}, u32[]{:S(2)}, u32[]{:S(2)}) collective-permute-start(f32[8,3584]{1,0:T(8,128)S(1)} %add_multiply_fusion.s0), channel_id=1, source_target_pairs={{0,4},{4,0},{8,12},{12,8},{16,20},{20,16},{24,28},{28,24},{1,5},{5... | collective-permute-start | bytes 344072 | tf_op jit(solution)/shard_map/ppermute | solution.py:285
  41.1 1.2 %collective-permute-start.14 = (f32[16,512]{1,0:T(8,128)S(1)}, f32[16,512]{1,0:T(8,128)S(1)}, u32[]{:S(2)}, u32[]{:S(2)}) collective-permute-start(f32[16,512]{1,0:T(8,128)S(1)} %get-tuple-element.50), channel_id=1, source_target_pairs={{0,1},{1,0},{2,3},{3,2},{4,5},{5,4},{6,7},{7,6},{8,9},{9,8},{10,11... | collective-permute-start | bytes 98312 | tf_op jit(solution)/shard_map/ppermute | solution.py:290
  42.3 3.9 %collective-permute-start.15 = (f32[16,512]{1,0:T(8,128)S(1)}, f32[16,512]{1,0:T(8,128)S(1)}, u32[]{:S(2)}, u32[]{:S(2)}) collective-permute-start(f32[16,512]{1,0:T(8,128)S(1)} %add.35.mine_ref), channel_id=1, source_target_pairs={{0,2},{1,3},{2,0},{3,1},{4,6},{5,7},{6,4},{7,5},{8,10},{9,11},{10,... | collective-permute-start | bytes 98312 | tf_op jit(solution)/shard_map/ppermute | solution.py:290
  47.1 6.8 %collective-permute-start.16 = (f32[2,16,1024]{2,1,0:T(8,128)S(1)}, f32[2,16,1024]{2,1,0:T(8,128)S(1)}, u32[]{:S(2)}, u32[]{:S(2)}) collective-permute-start(f32[2,16,1024]{2,1,0:T(8,128)S(1)} %get-tuple-element.54), channel_id=1, source_target_pairs={{0,12},{4,8},{8,4},{12,0},{16,28},{20,24},{24,20},{28,16},{1,13},{... | collective-permute-start | bytes 393224 | tf_op jit(solution)/shard_map/ppermute | solution.py:285
  48.7 5.6 %collective-permute-start.17 = (f32[2,16,1024]{2,1,0:T(8,128)S(1)}, f32[2,16,1024]{2,1,0:T(8,128)S(1)}, u32[]{:S(2)}, u32[]{:S(2)}) collective-permute-start(f32[2,16,1024]{2,1,0:T(8,128)S(1)} %get-tuple-element.55), channel_id=1, source_target_pairs={{0,8},{4,12},{8,0},{12,4},{16,24},{20,28},{24,16},{28,20},{1,9},{5... | collective-permute-start | bytes 393224 | tf_op jit(solution)/shard_map/ppermute | solution.py:285
  49.2 6.0 %collective-permute-start.18 = (f32[2,16,1024]{2,1,0:T(8,128)S(1)}, f32[2,16,1024]{2,1,0:T(8,128)S(1)}, u32[]{:S(2)}, u32[]{:S(2)}) collective-permute-start(f32[2,16,1024]{2,1,0:T(8,128)S(1)} %get-tuple-element.56), channel_id=1, source_target_pairs={{0,4},{4,0},{8,12},{12,8},{16,20},{20,16},{24,28},{28,24},{1,5},{5... | collective-permute-start | bytes 393224 | tf_op jit(solution)/shard_map/ppermute | solution.py:285
  55.2 5.2 %collective-permute-start.19 = (f32[16,1024]{1,0:T(8,128)S(1)}, f32[16,1024]{1,0:T(8,128)S(1)}, u32[]{:S(2)}, u32[]{:S(2)}) collective-permute-start(f32[16,1024]{1,0:T(8,128)S(1)} %get-tuple-element.58), channel_id=1, source_target_pairs={{0,16},{4,20},{8,24},{12,28},{16,0},{20,4},{24,8},{28,12},{1,17},{... | collective-permute-start | bytes 196616 | tf_op jit(solution)/shard_map/ppermute | solution.py:285
  60.5 1.3 %collective-permute-start.20 = (f32[16,1024]{1,0:T(8,128)S(1)}, f32[16,1024]{1,0:T(8,128)S(1)}, u32[]{:S(2)}, u32[]{:S(2)}) collective-permute-start(f32[16,1024]{1,0:T(8,128)S(1)} %shard_map.86.t_ref), channel_id=1, source_target_pairs={{0,1},{1,0},{2,3},{3,2},{4,5},{5,4},{6,7},{7,6},{8,9},{9,8},{10,11... | collective-permute-start | bytes 196616 | tf_op jit(solution)/shard_map/ppermute | solution.py:290

commit v5 on v4

--- a/solution.py
+++ b/solution.py
@@ -71,6 +71,14 @@
     return lax.dot_general(a, b, dims, preferred_element_type=F32, precision=precision)
 
 
+def exact_dot(a, b):
+    a1, a2, a3 = split(a, 3)
+    b1, b2, b3 = split(b, 3)
+    left = jnp.concatenate([a1, a1, a1, a2, a2, a3], axis=1)
+    right = jnp.concatenate([b1, b2, b3, b1, b2, b1], axis=0)
+    return dot(left, right, NN)
+
+
 def chunks(extent, count):
     step = extent // count
     return [pl.ds(i * step, step) for i in range(count)]
@@ -148,31 +156,34 @@
     first = 0
     for ref in (first_ref, rest_ref):
         for cut, units in cuts_of((ref,), first, 2):
-            ref[:, cut] = dot(coupling, b_ref[:, units], NN, lax.Precision.HIGHEST)
+            ref[:, cut] = exact_dot(coupling, b_ref[:, units])
         first += ref.shape[1]
 
 
-def products(pieces, f_ref, h_ref, b_ref, p_ref, first):
+def pulled_rows(pieces, f_ref, h_ref, p_ref, first):
     q = lax.axis_index("dp") % SQUARE
     rows = pieces[0].shape[0]
     rank = SQUARE * rows
     pulled = jnp.zeros((2 * rank, h_ref.shape[0]), F32)
-    total = jnp.zeros((3 * rank, 6 * rank), F32)
     for cut, units in cuts_of(pieces, first, 2):
         p = jnp.concatenate([s[:, cut] for s in pieces], axis=0) - f_ref[:, cut]
         for i, m in enumerate(SUMS_AWAY):
             p_ref[pl.ds((q ^ m) * rows, rows), cut] = p[i * rows : (i + 1) * rows]
         pulled += dot(jnp.concatenate(split(p, 2), axis=0), h_ref[:, units], NT)
-    for cut, units in cuts_of(pieces, first, 2):
+    return pulled[:rank] + pulled[rank:]
+
+
+def gram_terms(p_ref, b_ref, first):
+    rank = p_ref.shape[0]
+    total = jnp.zeros((3 * rank, 6 * rank), F32)
+    for cut, units in cuts_of((p_ref,), first, 2):
         p = split(p_ref[:, cut], 3)
         b = split(b_ref[:, units], 3)
         total += dot(jnp.concatenate(p, axis=0), jnp.concatenate(p + b, axis=0), NT)
-    pulled = pulled[:rank] + pulled[rank:]
     total = total[:rank] + total[rank : 2 * rank] + total[2 * rank :]
     gram = total[:, :rank] + total[:, rank : 2 * rank] + total[:, 2 * rank : 3 * rank]
     cross = total[:, 3 * rank : 4 * rank] + total[:, 4 * rank : 5 * rank] + total[:, 5 * rank :]
-    grams = jnp.concatenate([gram, cross, jnp.zeros((rank, 128 - 2 * rank), F32)], axis=1)
-    return pulled, grams
+    return jnp.concatenate([gram, cross, jnp.zeros((rank, 128 - 2 * rank), F32)], axis=1)
 
 
 def cuts_of(pieces, first, count):
@@ -181,31 +192,31 @@
 
 
 def first_pull_kernel(s0, s1, s2, s3, f_ref, h_ref, b_ref, p_ref, v_ref, g_ref):
-    v_ref[...], g_ref[...] = products((s0, s1, s2, s3), f_ref, h_ref, b_ref, p_ref, 0)
-
-
-def pull_kernel(s0, s1, s2, s3, f_ref, h_ref, b_ref, v_ref, g_ref, p_ref, keep_ref, send_ref, t_ref):
+    v_ref[...] = pulled_rows((s0, s1, s2, s3), f_ref, h_ref, p_ref, 0)
+    g_ref[...] = gram_terms(p_ref, b_ref, 0)
+
+
+def pull_kernel(s0, s1, s2, s3, f_ref, h_ref, v_ref, p_ref, keep_ref, send_ref, t_ref):
     q = lax.axis_index("dp") % SQUARE
     core = lax.axis_index("tensor") % 2
-    rows, half, tokens = s0.shape[0], keep_ref.shape[0], h_ref.shape[0]
+    rows, half = s0.shape[0], keep_ref.shape[0]
     first = h_ref.shape[1] - s0.shape[1]
-    pulled, grams = products((s0, s1, s2, s3), f_ref, h_ref, b_ref, p_ref, first)
-    pulled += v_ref[...]
-    grams += g_ref[...]
+    pulled = v_ref[...] + pulled_rows((s0, s1, s2, s3), f_ref, h_ref, p_ref, first)
     for i, m in enumerate(SUMS_AWAY):
         t_ref[pl.ds((q ^ m) * rows, rows), :] = pulled[i * rows : (i + 1) * rows]
-    keep_ref[:, :tokens] = t_ref[pl.ds(core * half, half), :]
-    send_ref[:, :tokens] = t_ref[pl.ds((1 - core) * half, half), :]
-    for ref in (keep_ref, send_ref):
-        ref[:, tokens : tokens + 128] = grams[:half]
-        ref[:, tokens + 128 :] = grams[half:]
-
-
-def push_kernel(mine_ref, got_ref, o_ref, *outs):
+    keep_ref[...] = t_ref[pl.ds(core * half, half), :]
+    send_ref[...] = t_ref[pl.ds((1 - core) * half, half), :]
+
+
+def gram_kernel(p_ref, b_ref, g_ref, out_ref):
+    out_ref[...] = g_ref[...] + gram_terms(p_ref, b_ref, b_ref.shape[1] - p_ref.shape[1])
+
+
+def push_kernel(mine_ref, got_ref, o_ref, after_ref, *outs):
     me = lax.axis_index("dp")
     tokens = o_ref.shape[0]
     half, width = outs[0].shape[1:]
-    v = jnp.concatenate(split(mine_ref[:, :tokens] + got_ref[:, :tokens], 2), axis=0)
+    v = jnp.concatenate(split(mine_ref[...] + got_ref[...], 2), axis=0)
     for i, m in enumerate(RIGHT_AWAY):
         for z in range(2):
             cut = pl.ds(pl.multiple_of((me ^ m ^ (SQUARE * z)) * width, width), width)
@@ -214,21 +225,25 @@
 
 
 def cholesky_kernel(mine_ref, got_ref, out_ref):
-    rank, lanes = out_ref.shape
-    shape = out_ref.shape
-    tokens = mine_ref.shape[1] - 2 * lanes
-    grams = mine_ref[:, tokens:] + got_ref[:, tokens:]
-    grams = jnp.concatenate([grams[:, :lanes], grams[:, lanes:]], axis=0)
+    rank = out_ref.shape[0]
+    shape, block = out_ref.shape, 8
     row = lax.broadcasted_iota(jnp.int32, shape, 0)
     lane = lax.broadcasted_iota(jnp.int32, shape, 1)
-    a = jnp.where(lane == row + 2 * rank, 1.0, grams)
-    for k in range(rank):
-        pivot = a[k : k + 1, k : k + 1]
-        scale = 1.0 / jnp.sqrt(pivot)
-        top = a[k : k + 1, :] * scale
-        below = jnp.where(row[:, :1] > k, a[:, k : k + 1] * scale, 0.0)
-        a = jnp.where(row == k, top, a - below * top)
-    out_ref[...] = a
+    a = jnp.where(lane == row + 2 * rank, 1.0, mine_ref[...] + got_ref[...])
+    for k in range(0, rank, block):
+        rows = [jnp.broadcast_to(a[k + i : k + i + 1, :], shape) for i in range(block)]
+        columns = [jnp.broadcast_to(a[:, k + i : k + i + 1], shape) for i in range(block)]
+        change = jnp.zeros(shape, F32)
+        for i in range(block):
+            inverse = 1.0 / columns[i][k + i : k + i + 1, :]
+            change += jnp.where(row > k + i, columns[i], 0.0) * (rows[i] * inverse)
+            for j in range(i + 1, block):
+                factor = columns[i][k + j : k + j + 1, :] * inverse
+                rows[j] = rows[j] - factor * rows[i]
+                columns[j] = columns[j] - factor * columns[i]
+        a = a - change
+    pivots = jnp.sum(jnp.where(lane == row, a, 0.0), axis=1, keepdims=True)
+    out_ref[...] = a * (1.0 / jnp.sqrt(pivots))
 
 
 def near_far_kernel(a_ref, b_ref, c_ref, d_ref, after_ref, near_ref, far_ref):
@@ -243,15 +258,14 @@
 def basis_kernel(p_ref, r_ref, l_ref, w_ref, out_ref, fix_ref, *, norm_scale):
     rank = l_ref.shape[0]
     width = fix_ref.shape[1]
-    highest = lax.Precision.HIGHEST
     inverse = l_ref[:, 2 * rank : 3 * rank] * norm_scale
     first = 0
     for ref in (p_ref, r_ref):
         for cut, units in cuts_of((ref,), first, 2):
-            out_ref[:, units] = dot(inverse, ref[:, cut], NN, highest)
+            out_ref[:, units] = exact_dot(inverse, ref[:, cut])
         first += ref.shape[1]
     own = pl.ds(pl.multiple_of(lax.axis_index("dp") * width, width), width)
-    fix_ref[...] = dot(l_ref[:, rank : 2 * rank], w_ref[:, own], NN, highest)
+    fix_ref[...] = exact_dot(l_ref[:, rank : 2 * rank], w_ref[:, own])
 
 
 def factor_kernel(t_ref, u_ref, l_ref, fix_ref, out_ref, z_ref, *, replicas):
@@ -261,7 +275,7 @@
     z_ref[pl.ds(core * half, half), :] = t_ref[...]
     z_ref[pl.ds((1 - core) * half, half), :] = u_ref[...]
     inverse = l_ref[:, 2 * rank : 3 * rank] * (1.0 / replicas)
-    out_ref[...] = dot(inverse, z_ref[...], NN, lax.Precision.HIGHEST) - fix_ref[...]
+    out_ref[...] = exact_dot(inverse, z_ref[...]) - fix_ref[...]
 
 
 def call(kernel, outs, specs, scratch=(), flops=0, moved=0, vmem=32 << 20):
@@ -348,25 +362,36 @@
     )(*early_p, early_feedback, hiddens, b)
     p_rest, keep, send = call(
         pull_kernel,
-        [(rank, rest)] + [(half, 2 * tokens + 256)] * 2,
-        [VMEM_SPEC] * 9,
+        [(rank, rest)] + [(half, 2 * tokens)] * 2,
+        [VMEM_SPEC] * 7,
         [pltpu.VMEM((rank, 2 * tokens), F32)],
         flops=8 * tokens * rank * rest,
         moved=4 * tokens * rest + 4 * rank * rest,
-    )(*late_p, late_feedback, hiddens, b, early_v, early_gram)
-    plane = keep + swap_tensor(send, 1)
+    )(*late_p, late_feedback, hiddens, early_v)
+    other = swap_tensor(send, 1)
+    (gram,) = call(
+        gram_kernel,
+        [(rank, 128)],
+        [VMEM_SPEC] * 3,
+        flops=36 * rank * rank * rest,
+        moved=8 * rank * rest,
+    )(p_rest, b, early_gram)
+    other, gram = lax.optimization_barrier((other, gram))
+    plane = keep + other
     plane_came = swap_tensor(plane, 2)
+    gram = gram + swap_tensor(gram, 1)
+    gram_came = swap_tensor(gram, 2)
     parts = call(
         push_kernel,
         [(2, half, owned)] * SQUARE,
-        [VMEM_SPEC] * 3,
+        [VMEM_SPEC] * 3 + [ANY_SPEC],
         flops=8 * tokens * half * width,
         moved=4 * tokens * width + 4 * half * width,
-    )(plane, plane_came, out_grads)
+    )(plane, plane_came, out_grads, gram)
     came = swap_square(parts, RIGHT_AWAY)
     (solved,) = call(
         cholesky_kernel, [(rank, 128)], [VMEM_SPEC] * 2, flops=rank**3, moved=8 * rank * 128
-    )(plane, plane_came)
+    )(gram, gram_came)
     near, far = call(
         near_far_kernel,
         [(half, owned)] * 2,

time: 62.9 us -> 62.3 us (level)
  Pallas kernels: 16.9 us -> 14.1 us
  starting transfers between devices: 27.5 us -> 29.3 us
    pallas_call x1, Pallas kernels: 3.01 us -> 0.79 us  [on_device(): call(cholesky_kernel, [(rank, 128)], [VMEM_SPEC] * 2, flops=rank ** 3, mo...]
    ppermute x3 -> x5, starting transfers between devices: 1.61 us -> 3.33 us  [swap_tensor(): return lax.ppermute(x, 'tensor', [(i, i ^ m) for i in range(n)])]
    ppermute x3 -> x5, waiting for transfers between devices: 4.83 us -> 6.13 us  [swap_tensor(): return lax.ppermute(x, 'tensor', [(i, i ^ m) for i in range(n)])]
    ppermute x18, waiting for transfers between devices: 12.7 us -> 11.8 us  [swap_dp(): return lax.ppermute(x, 'dp', [(i, i ^ m) for i in range(n)])]
    pallas_call x2 -> x3, Pallas kernels: 2.05 us -> 2.22 us  [the longest x1 0.8 us: on_device(): call(push_kernel, [(2, half, owned)] * SQUARE, [VMEM_SPEC] * 3 + [ANY_SPE...]
  transfers between devices with their start and end apart: 21 -> 23, of which waited for: 16 -> 16; matrix products, arithmetic and copies ran while one was open for 0% -> 0% of each run, Pallas kernels for 14% -> 11%
where the time goes in v5:
time: 62.3 us; the launch traced here: 62.1 us
  starting transfers between devices  29.3 us (47%)
  waiting for transfers between devices  17.9 us (29%)
  Pallas kernels  14.1 us (23%)
  between operations  0.73 us (1%)
    ppermute x18, starting transfers between devices, swap_dp(): return lax.ppermute(x, 'dp', [(i, i ^ m) for i in range(n)])  26 us
    ppermute x18, waiting for transfers between devices, swap_dp(): return lax.ppermute(x, 'dp', [(i, i ^ m) for i in range(n)])  11.8 us
    ppermute x5, waiting for transfers between devices, swap_tensor(): return lax.ppermute(x, 'tensor', [(i, i ^ m) for i in range(n)])  6.13 us
    pallas_call x1, Pallas kernels, on_device(): call(first_term_kernel, [(rows, first)] * SQUARE + [(rank, 2 * tokens), (...  4.97 us
    ppermute x5, starting transfers between devices, swap_tensor(): return lax.ppermute(x, 'tensor', [(i, i ^ m) for i in range(n)])  3.33 us
    pallas_call x1, Pallas kernels, on_device(): call(feedback_kernel, [(rank, first), (rank, rest)], [VMEM_SPEC] * 2 + [A...  1.91 us
    pallas_call x1, Pallas kernels, on_device(): call(functools.partial(basis_kernel, norm_scale=norm_scale), [(rank, unit...  1.59 us
    pallas_call x1, Pallas kernels, on_device(): call(first_pull_kernel, [(rank, first), (rank, 2 * tokens), (rank, 128)],...  1.25 us
  transfers between devices with their start and end apart: 23, of which 16 were waited for; matrix products, arithmetic and copies ran while one was open for 0% of the time, Pallas kernels for 11%

profile of v5, /device:TPU:0, one launch (start us, length us, event | category | flops | bytes accessed | tf_op | source)
XLA Modules:
  0.0 62.1 jit_solution(8756220822396739127)
XLA Ops:
  0.6 5.0 %shard_map.77 = (f32[8,3584]{1,0:T(8,128)S(1)}, f32[8,3584]{1,0:T(8,128)S(1)}, f32[8,3584]{1,0:T(8,128)S(1)}, f32[8,3584]{1,0:T(8,128)S(1)}, f32[32,256]{1,0:T(8...) custom-call(f32[32,8192]{1,0:T(8,128)} %bitcast.4, bf16[128,8192]{1,0:T(8,128)(2,1)} %o_ref.1, ...), custom_call_target="tpu_custom_call" | custom-call | flops 192937984 | bytes 9371648 | tf_op jit(solution)/shard_map/pallas_call | solution.py:317
  5.6 3.0 %collective-permute-start.2 = (f32[8,3584]{1,0:T(8,128)S(1)}, f32[8,3584]{1,0:T(8,128)S(1)}, u32[]{:S(2)}, u32[]{:S(2)}) collective-permute-start(f32[8,3584]{1,0:T(8,128)S(1)} %get-tuple-element.36), channel_id=1, source_target_pairs={{0,4},{4,0},{8,12},{12,8},{16,20},{20,16},{24,28},{28,24},{1,5},{5... | collective-permute-start | bytes 344072 | tf_op jit(solution)/shard_map/ppermute | solution.py:299
  8.6 1.5 %collective-permute-start = (f32[8,3584]{1,0:T(8,128)S(1)}, f32[8,3584]{1,0:T(8,128)S(1)}, u32[]{:S(2)}, u32[]{:S(2)}) collective-permute-start(f32[8,3584]{1,0:T(8,128)S(1)} %get-tuple-element.34), channel_id=1, source_target_pairs={{0,12},{4,8},{8,4},{12,0},{16,28},{20,24},{24,20},{28,16},{1,13},{... | collective-permute-start | bytes 344072 | tf_op jit(solution)/shard_map/ppermute | solution.py:299
  10.6 1.9 %collective-permute-start.6 = (f32[8,3584]{1,0:T(8,128)S(1)}, f32[8,3584]{1,0:T(8,128)S(1)}, u32[]{:S(2)}, u32[]{:S(2)}) collective-permute-start(f32[8,3584]{1,0:T(8,128)S(1)} %get-tuple-element.42), channel_id=1, source_target_pairs={{0,4},{4,0},{8,12},{12,8},{16,20},{20,16},{24,28},{28,24},{1,5},{5... | collective-permute-start | bytes 344072 | tf_op jit(solution)/shard_map/ppermute | solution.py:299
  12.6 1.5 %collective-permute-start.4 = (f32[8,3584]{1,0:T(8,128)S(1)}, f32[8,3584]{1,0:T(8,128)S(1)}, u32[]{:S(2)}, u32[]{:S(2)}) collective-permute-start(f32[8,3584]{1,0:T(8,128)S(1)} %get-tuple-element.40), channel_id=1, source_target_pairs={{0,12},{4,8},{8,4},{12,0},{16,28},{20,24},{24,20},{28,16},{1,13},{... | collective-permute-start | bytes 344072 | tf_op jit(solution)/shard_map/ppermute | solution.py:299
  15.1 1.2 %collective-permute-start.5 = (f32[8,3584]{1,0:T(8,128)S(1)}, f32[8,3584]{1,0:T(8,128)S(1)}, u32[]{:S(2)}, u32[]{:S(2)}) collective-permute-start(f32[8,3584]{1,0:T(8,128)S(1)} %get-tuple-element.41), channel_id=1, source_target_pairs={{0,8},{4,12},{8,0},{12,4},{16,24},{20,28},{24,16},{28,20},{1,9},{5... | collective-permute-start | bytes 344072 | tf_op jit(solution)/shard_map/ppermute | solution.py:299
  16.7 3.1 %collective-permute-start.3 = (f32[8,3584]{1,0:T(8,128)S(1)}, f32[8,3584]{1,0:T(8,128)S(1)}, u32[]{:S(2)}, u32[]{:S(2)}) collective-permute-start(f32[8,3584]{1,0:T(8,128)S(1)} %add_add_fusion.1), channel_id=1, source_target_pairs={{0,16},{4,20},{8,24},{12,28},{16,0},{20,4},{24,8},{28,12},{1,17},{... | collective-permute-start | bytes 344072 | tf_op jit(solution)/shard_map/ppermute | solution.py:299
  19.7 1.8 %collective-permute-done.4 = f32[8,3584]{1,0:T(8,128)S(1)} collective-permute-done((f32[8,3584]{1,0:T(8,128)S(1)}, f32[8,3584]{1,0:T(8,128)S(1)}, u32[]{:S(2)}, u32[]{:S(2)}) %collective-permute-start.4) | collective-permute-done | bytes 114720 | tf_op jit(solution)/shard_map/ppermute | solution.py:299
  22.2 2.4 %collective-permute-start.10 = (f32[8,3584]{1,0:T(8,128)S(1)}, f32[8,3584]{1,0:T(8,128)S(1)}, u32[]{:S(2)}, u32[]{:S(2)}) collective-permute-start(f32[8,3584]{1,0:T(8,128)S(1)} %add_add_fusion.after_ref), channel_id=1, source_target_pairs={{0,16},{4,20},{8,24},{12,28},{16,0},{20,4},{24,8},{28,12},{1,17},{... | collective-permute-start | bytes 344072 | tf_op jit(solution)/shard_map/ppermute | solution.py:299
  24.5 1.9 %shard_map.79 = (f32[32,3584]{1,0:T(8,128)S(1)}, f32[32,3584]{1,0:T(8,128)S(1)}) custom-call(f32[32,8192]{1,0:T(8,128)S(1)} %bitcast.5, f32[32,7168]{1,0:T(8,128)S(1)} %bitcast.7, f32[8,3584]{1,0:T(8,128)S(1)} %add_add_fusion.after_ref), custom_call_target="tpu_custom_call" | custom-call | flops 31457280 | bytes 1966080 | tf_op jit(solution)/shard_map/pallas_call | solution.py:344
  26.5 3.2 %collective-permute-start.7 = (f32[8,3584]{1,0:T(8,128)S(1)}, f32[8,3584]{1,0:T(8,128)S(1)}, u32[]{:S(2)}, u32[]{:S(2)}) collective-permute-start(f32[8,3584]{1,0:T(8,128)S(1)} %add_multiply_fusion.1.s0), channel_id=1, source_target_pairs={{0,12},{4,8},{8,4},{12,0},{16,28},{20,24},{24,20},{28,16},{1,13},{... | collective-permute-start | bytes 344072 | tf_op jit(solution)/shard_map/ppermute | solution.py:299
  30.4 2.9 %collective-permute-start.11 = (f32[8,3584]{1,0:T(8,128)S(1)}, f32[8,3584]{1,0:T(8,128)S(1)}, u32[]{:S(2)}, u32[]{:S(2)}) collective-permute-start(f32[8,3584]{1,0:T(8,128)S(1)} %add_multiply_fusion.s0), channel_id=1, source_target_pairs={{0,12},{4,8},{8,4},{12,0},{16,28},{20,24},{24,20},{28,16},{1,13},{... | collective-permute-start | bytes 344072 | tf_op jit(solution)/shard_map/ppermute | solution.py:299
  34.0 1.1 %collective-permute-done.8.s2 = f32[8,3584]{1,0:T(8,128)S(1)} collective-permute-done((f32[8,3584]{1,0:T(8,128)S(1)}, f32[8,3584]{1,0:T(8,128)S(1)}, u32[]{:S(2)}, u32[]{:S(2)}) %collective-permute-start.8) | collective-permute-done | bytes 114720 | tf_op jit(solution)/shard_map/ppermute | solution.py:299
  36.2 1.2 %shard_map.80 = (f32[32,3584]{1,0:T(8,128)S(1)}, f32[32,256]{1,0:T(8,128)S(1)}, f32[32,128]{1,0:T(8,128)S(1)}) custom-call(f32[8,3584]{1,0:T(8,128)S(1)} %add_multiply_fusion.1.s0, f32[8,3584]{1,0:T(8,128)S(1)} %collective-permute-done.7.s1, f32[8,3584]{1,0:T(8,128)S(1)} %collective-permute-done.8.s2, f32[8,3584]{1,0:T(8,128)S(1)} %collective-permute-done.9.s3, ...), custom_call_target="tpu_custom_call" | custom-call | flops 117440512 | bytes 2293760 | tf_op jit(solution)/shard_map/pallas_call | solution.py:356
  37.5 1.1 %collective-permute-done.11.s1 = f32[8,3584]{1,0:T(8,128)S(1)} collective-permute-done((f32[8,3584]{1,0:T(8,128)S(1)}, f32[8,3584]{1,0:T(8,128)S(1)}, u32[]{:S(2)}, u32[]{:S(2)}) %collective-permute-start.11) | collective-permute-done | bytes 114720 | tf_op jit(solution)/shard_map/ppermute | solution.py:299
  41.8 1.5 %collective-permute-start.17 = (f32[16,256]{1,0:T(8,128)S(1)}, f32[16,256]{1,0:T(8,128)S(1)}, u32[]{:S(2)}, u32[]{:S(2)}) collective-permute-start(f32[16,256]{1,0:T(8,128)S(1)} %add.39.mine_ref), channel_id=1, source_target_pairs={{0,2},{1,3},{2,0},{3,1},{4,6},{5,7},{6,4},{7,5},{8,10},{9,11},{10,... | collective-permute-start | bytes 49160 | tf_op jit(solution)/shard_map/ppermute | solution.py:304
  43.3 2.2 %collective-permute-done.17.got_ref = f32[16,256]{1,0:T(8,128)S(1)} collective-permute-done((f32[16,256]{1,0:T(8,128)S(1)}, f32[16,256]{1,0:T(8,128)S(1)}, u32[]{:S(2)}, u32[]{:S(2)}) %collective-permute-start.17) | collective-permute-done | bytes 16416 | tf_op jit(solution)/shard_map/ppermute | solution.py:304
  46.3 1.4 %collective-permute-start.18 = (f32[2,16,1024]{2,1,0:T(8,128)S(1)}, f32[2,16,1024]{2,1,0:T(8,128)S(1)}, u32[]{:S(2)}, u32[]{:S(2)}) collective-permute-start(f32[2,16,1024]{2,1,0:T(8,128)S(1)} %get-tuple-element.58), channel_id=1, source_target_pairs={{0,12},{4,8},{8,4},{12,0},{16,28},{20,24},{24,20},{28,16},{1,13},{... | collective-permute-start | bytes 393224 | tf_op jit(solution)/shard_map/ppermute | solution.py:299
  48.5 1.3 %collective-permute-start.20 = (f32[2,16,1024]{2,1,0:T(8,128)S(1)}, f32[2,16,1024]{2,1,0:T(8,128)S(1)}, u32[]{:S(2)}, u32[]{:S(2)}) collective-permute-start(f32[2,16,1024]{2,1,0:T(8,128)S(1)} %get-tuple-element.60), channel_id=1, source_target_pairs={{0,4},{4,0},{8,12},{12,8},{16,20},{20,16},{24,28},{28,24},{1,5},{5... | collective-permute-start | bytes 393224 | tf_op jit(solution)/shard_map/ppermute | solution.py:299
  49.8 1.5 %collective-permute-start.16 = (f32[32,128]{1,0:T(8,128)S(1)}, f32[32,128]{1,0:T(8,128)S(1)}, u32[]{:S(2)}, u32[]{:S(2)}) collective-permute-start(f32[32,128]{1,0:T(8,128)S(1)} %add.38.mine_ref.after_ref), channel_id=1, source_target_pairs={{0,2},{1,3},{2,0},{3,1},{4,6},{5,7},{6,4},{7,5},{8,10},{9,11},{10,... | collective-permute-start | bytes 49160 | tf_op jit(solution)/shard_map/ppermute | solution.py:304
  51.3 2.2 %collective-permute-done.16.got_ref = f32[32,128]{1,0:T(8,128)S(1)} collective-permute-done((f32[32,128]{1,0:T(8,128)S(1)}, f32[32,128]{1,0:T(8,128)S(1)}, u32[]{:S(2)}, u32[]{:S(2)}) %collective-permute-start.16) | collective-permute-done | bytes 16416 | tf_op jit(solution)/shard_map/ppermute | solution.py:304
  55.5 1.6 %shard_map.84 = (f32[32,7168]{1,0:T(8,128)}, f32[32,1024]{1,0:T(8,128)S(1)}) custom-call(f32[32,3584]{1,0:T(8,128)S(1)} %get-tuple-element.46.p_ref, f32[32,3584]{1,0:T(8,128)S(1)} %get-tuple-element.49.p_ref.r_ref, f32[32,128]{1,0:T(8,128)S(1)} %shard_map.83.l_ref.after_ref, f32[32,8192]{1,0:T(8,128)S(1)} %bitcast.6), custom_call_target="tpu_custom_call" | custom-call | flops 14680064 | bytes 1835008 | tf_op jit(solution)/shard_map/pallas_call | solution.py:402
  57.1 2.8 %collective-permute-done.21.b_ref = f32[16,1024]{1,0:T(8,128)S(1)} collective-permute-done((f32[16,1024]{1,0:T(8,128)S(1)}, f32[16,1024]{1,0:T(8,128)S(1)}, u32[]{:S(2)}, u32[]{:S(2)}) %collective-permute-start.21) | collective-permute-done | bytes 65568 | tf_op jit(solution)/shard_map/ppermute | solution.py:299
  60.0 1.2 %collective-permute-done.22.u_ref = f32[16,1024]{1,0:T(8,128)S(1)} collective-permute-done((f32[16,1024]{1,0:T(8,128)S(1)}, f32[16,1024]{1,0:T(8,128)S(1)}, u32[]{:S(2)}, u32[]{:S(2)}) %collective-permute-start.22) | collective-permute-done | bytes 65568 | tf_op jit(solution)/shard_map/ppermute | solution.py:304
  (44 shorter events, 12.6 us)
Async XLA Ops:
  5.6 9.5 %collective-permute-start.2 = (f32[8,3584]{1,0:T(8,128)S(1)}, f32[8,3584]{1,0:T(8,128)S(1)}, u32[]{:S(2)}, u32[]{:S(2)}) collective-permute-start(f32[8,3584]{1,0:T(8,128)S(1)} %get-tuple-element.36), channel_id=1, source_target_pairs={{0,4},{4,0},{8,12},{12,8},{16,20},{20,16},{24,28},{28,24},{1,5},{5... | collective-permute-start | bytes 344072 | tf_op jit(solution)/shard_map/ppermute | solution.py:299
  8.6 7.7 %collective-permute-start = (f32[8,3584]{1,0:T(8,128)S(1)}, f32[8,3584]{1,0:T(8,128)S(1)}, u32[]{:S(2)}, u32[]{:S(2)}) collective-permute-start(f32[8,3584]{1,0:T(8,128)S(1)} %get-tuple-element.34), channel_id=1, source_target_pairs={{0,12},{4,8},{8,4},{12,0},{16,28},{20,24},{24,20},{28,16},{1,13},{... | collective-permute-start | bytes 344072 | tf_op jit(solution)/shard_map/ppermute | solution.py:299
  10.2 6.5 %collective-permute-start.1 = (f32[8,3584]{1,0:T(8,128)S(1)}, f32[8,3584]{1,0:T(8,128)S(1)}, u32[]{:S(2)}, u32[]{:S(2)}) collective-permute-start(f32[8,3584]{1,0:T(8,128)S(1)} %get-tuple-element.35), channel_id=1, source_target_pairs={{0,8},{4,12},{8,0},{12,4},{16,24},{20,28},{24,16},{28,20},{1,9},{5... | collective-permute-start | bytes 344072 | tf_op jit(solution)/shard_map/ppermute | solution.py:299
  10.2 14.4 %copy-start.1 = (f32[7168,32]{0,1:T(8,128)S(1)}, f32[7168,32]{0,1:T(8,128)}, u32[]{:S(2)}) copy-start(f32[7168,32]{0,1:T(8,128)} %param.10) | copy-start | bytes 2752516
  10.6 9.1 %collective-permute-start.6 = (f32[8,3584]{1,0:T(8,128)S(1)}, f32[8,3584]{1,0:T(8,128)S(1)}, u32[]{:S(2)}, u32[]{:S(2)}) collective-permute-start(f32[8,3584]{1,0:T(8,128)S(1)} %get-tuple-element.42), channel_id=1, source_target_pairs={{0,4},{4,0},{8,12},{12,8},{16,20},{20,16},{24,28},{28,24},{1,5},{5... | collective-permute-start | bytes 344072 | tf_op jit(solution)/shard_map/ppermute | solution.py:299
  12.6 9.0 %collective-permute-start.4 = (f32[8,3584]{1,0:T(8,128)S(1)}, f32[8,3584]{1,0:T(8,128)S(1)}, u32[]{:S(2)}, u32[]{:S(2)}) collective-permute-start(f32[8,3584]{1,0:T(8,128)S(1)} %get-tuple-element.40), channel_id=1, source_target_pairs={{0,12},{4,8},{8,4},{12,0},{16,28},{20,24},{24,20},{28,16},{1,13},{... | collective-permute-start | bytes 344072 | tf_op jit(solution)/shard_map/ppermute | solution.py:299
  15.1 7.0 %collective-permute-start.5 = (f32[8,3584]{1,0:T(8,128)S(1)}, f32[8,3584]{1,0:T(8,128)S(1)}, u32[]{:S(2)}, u32[]{:S(2)}) collective-permute-start(f32[8,3584]{1,0:T(8,128)S(1)} %get-tuple-element.41), channel_id=1, source_target_pairs={{0,8},{4,12},{8,0},{12,4},{16,24},{20,28},{24,16},{28,20},{1,9},{5... | collective-permute-start | bytes 344072 | tf_op jit(solution)/shard_map/ppermute | solution.py:299
  16.7 9.8 %collective-permute-start.3 = (f32[8,3584]{1,0:T(8,128)S(1)}, f32[8,3584]{1,0:T(8,128)S(1)}, u32[]{:S(2)}, u32[]{:S(2)}) collective-permute-start(f32[8,3584]{1,0:T(8,128)S(1)} %add_add_fusion.1), channel_id=1, source_target_pairs={{0,16},{4,20},{8,24},{12,28},{16,0},{20,4},{24,8},{28,12},{1,17},{... | collective-permute-start | bytes 344072 | tf_op jit(solution)/shard_map/ppermute | solution.py:299
  22.2 8.2 %collective-permute-start.10 = (f32[8,3584]{1,0:T(8,128)S(1)}, f32[8,3584]{1,0:T(8,128)S(1)}, u32[]{:S(2)}, u32[]{:S(2)}) collective-permute-start(f32[8,3584]{1,0:T(8,128)S(1)} %add_add_fusion.after_ref), channel_id=1, source_target_pairs={{0,16},{4,20},{8,24},{12,28},{16,0},{20,4},{24,8},{28,12},{1,17},{... | collective-permute-start | bytes 344072 | tf_op jit(solution)/shard_map/ppermute | solution.py:299
  26.5 7.4 %collective-permute-start.7 = (f32[8,3584]{1,0:T(8,128)S(1)}, f32[8,3584]{1,0:T(8,128)S(1)}, u32[]{:S(2)}, u32[]{:S(2)}) collective-permute-start(f32[8,3584]{1,0:T(8,128)S(1)} %add_multiply_fusion.1.s0), channel_id=1, source_target_pairs={{0,12},{4,8},{8,4},{12,0},{16,28},{20,24},{24,20},{28,16},{1,13},{... | collective-permute-start | bytes 344072 | tf_op jit(solution)/shard_map/ppermute | solution.py:299
  29.7 5.4 %collective-permute-start.8 = (f32[8,3584]{1,0:T(8,128)S(1)}, f32[8,3584]{1,0:T(8,128)S(1)}, u32[]{:S(2)}, u32[]{:S(2)}) collective-permute-start(f32[8,3584]{1,0:T(8,128)S(1)} %add_multiply_fusion.1.s0), channel_id=1, source_target_pairs={{0,8},{4,12},{8,0},{12,4},{16,24},{20,28},{24,16},{28,20},{1,9},{5... | collective-permute-start | bytes 344072 | tf_op jit(solution)/shard_map/ppermute | solution.py:299
  29.7 6.5 %collective-permute-start.9 = (f32[8,3584]{1,0:T(8,128)S(1)}, f32[8,3584]{1,0:T(8,128)S(1)}, u32[]{:S(2)}, u32[]{:S(2)}) collective-permute-start(f32[8,3584]{1,0:T(8,128)S(1)} %add_multiply_fusion.1.s0), channel_id=1, source_target_pairs={{0,4},{4,0},{8,12},{12,8},{16,20},{20,16},{24,28},{28,24},{1,5},{5... | collective-permute-start | bytes 344072 | tf_op jit(solution)/shard_map/ppermute | solution.py:299
  30.4 8.2 %collective-permute-start.11 = (f32[8,3584]{1,0:T(8,128)S(1)}, f32[8,3584]{1,0:T(8,128)S(1)}, u32[]{:S(2)}, u32[]{:S(2)}) collective-permute-start(f32[8,3584]{1,0:T(8,128)S(1)} %add_multiply_fusion.s0), channel_id=1, source_target_pairs={{0,12},{4,8},{8,4},{12,0},{16,28},{20,24},{24,20},{28,16},{1,13},{... | collective-permute-start | bytes 344072 | tf_op jit(solution)/shard_map/ppermute | solution.py:299
  33.3 6.2 %collective-permute-start.12 = (f32[8,3584]{1,0:T(8,128)S(1)}, f32[8,3584]{1,0:T(8,128)S(1)}, u32[]{:S(2)}, u32[]{:S(2)}) collective-permute-start(f32[8,3584]{1,0:T(8,128)S(1)} %add_multiply_fusion.s0), channel_id=1, source_target_pairs={{0,8},{4,12},{8,0},{12,4},{16,24},{20,28},{24,16},{28,20},{1,9},{5... | collective-permute-start | bytes 344072 | tf_op jit(solution)/shard_map/ppermute | solution.py:299
  33.9 5.8 %collective-permute-start.13 = (f32[8,3584]{1,0:T(8,128)S(1)}, f32[8,3584]{1,0:T(8,128)S(1)}, u32[]{:S(2)}, u32[]{:S(2)}) collective-permute-start(f32[8,3584]{1,0:T(8,128)S(1)} %add_multiply_fusion.s0), channel_id=1, source_target_pairs={{0,4},{4,0},{8,12},{12,8},{16,20},{20,16},{24,28},{28,24},{1,5},{5... | collective-permute-start | bytes 344072 | tf_op jit(solution)/shard_map/ppermute | solution.py:299
  40.4 1.2 %collective-permute-start.14 = (f32[16,256]{1,0:T(8,128)S(1)}, f32[16,256]{1,0:T(8,128)S(1)}, u32[]{:S(2)}, u32[]{:S(2)}) collective-permute-start(f32[16,256]{1,0:T(8,128)S(1)} %get-tuple-element.50), channel_id=1, source_target_pairs={{0,1},{1,0},{2,3},{3,2},{4,5},{5,4},{6,7},{7,6},{8,9},{9,8},{10,11... | collective-permute-start | bytes 49160 | tf_op jit(solution)/shard_map/ppermute | solution.py:304
  41.6 1.7 %collective-permute-start.15 = (f32[32,128]{1,0:T(8,128)S(1)}, f32[32,128]{1,0:T(8,128)S(1)}, u32[]{:S(2)}, u32[]{:S(2)}) collective-permute-start(f32[32,128]{1,0:T(8,128)S(1)} %shard_map.82), channel_id=1, source_target_pairs={{0,1},{1,0},{2,3},{3,2},{4,5},{5,4},{6,7},{7,6},{8,9},{9,8},{10,11... | collective-permute-start | bytes 49160 | tf_op jit(solution)/shard_map/ppermute | solution.py:304
  41.8 3.7 %collective-permute-start.17 = (f32[16,256]{1,0:T(8,128)S(1)}, f32[16,256]{1,0:T(8,128)S(1)}, u32[]{:S(2)}, u32[]{:S(2)}) collective-permute-start(f32[16,256]{1,0:T(8,128)S(1)} %add.39.mine_ref), channel_id=1, source_target_pairs={{0,2},{1,3},{2,0},{3,1},{4,6},{5,7},{6,4},{7,5},{8,10},{9,11},{10,... | collective-permute-start | bytes 49160 | tf_op jit(solution)/shard_map/ppermute | solution.py:304
  46.3 8.0 %collective-permute-start.18 = (f32[2,16,1024]{2,1,0:T(8,128)S(1)}, f32[2,16,1024]{2,1,0:T(8,128)S(1)}, u32[]{:S(2)}, u32[]{:S(2)}) collective-permute-start(f32[2,16,1024]{2,1,0:T(8,128)S(1)} %get-tuple-element.58), channel_id=1, source_target_pairs={{0,12},{4,8},{8,4},{12,0},{16,28},{20,24},{24,20},{28,16},{1,13},{... | collective-permute-start | bytes 393224 | tf_op jit(solution)/shard_map/ppermute | solution.py:299
  47.7 6.7 %collective-permute-start.19 = (f32[2,16,1024]{2,1,0:T(8,128)S(1)}, f32[2,16,1024]{2,1,0:T(8,128)S(1)}, u32[]{:S(2)}, u32[]{:S(2)}) collective-permute-start(f32[2,16,1024]{2,1,0:T(8,128)S(1)} %get-tuple-element.59), channel_id=1, source_target_pairs={{0,8},{4,12},{8,0},{12,4},{16,24},{20,28},{24,16},{28,20},{1,9},{5... | collective-permute-start | bytes 393224 | tf_op jit(solution)/shard_map/ppermute | solution.py:299
  48.5 6.1 %collective-permute-start.20 = (f32[2,16,1024]{2,1,0:T(8,128)S(1)}, f32[2,16,1024]{2,1,0:T(8,128)S(1)}, u32[]{:S(2)}, u32[]{:S(2)}) collective-permute-start(f32[2,16,1024]{2,1,0:T(8,128)S(1)} %get-tuple-element.60), channel_id=1, source_target_pairs={{0,4},{4,0},{8,12},{12,8},{16,20},{20,16},{24,28},{28,24},{1,5},{5... | collective-permute-start | bytes 393224 | tf_op jit(solution)/shard_map/ppermute | solution.py:299
  49.8 3.7 %collective-permute-start.16 = (f32[32,128]{1,0:T(8,128)S(1)}, f32[32,128]{1,0:T(8,128)S(1)}, u32[]{:S(2)}, u32[]{:S(2)}) collective-permute-start(f32[32,128]{1,0:T(8,128)S(1)} %add.38.mine_ref.after_ref), channel_id=1, source_target_pairs={{0,2},{1,3},{2,0},{3,1},{4,6},{5,7},{6,4},{7,5},{8,10},{9,11},{10,... | collective-permute-start | bytes 49160 | tf_op jit(solution)/shard_map/ppermute | solution.py:304
  54.7 5.2 %collective-permute-start.21 = (f32[16,1024]{1,0:T(8,128)S(1)}, f32[16,1024]{1,0:T(8,128)S(1)}, u32[]{:S(2)}, u32[]{:S(2)}) collective-permute-start(f32[16,1024]{1,0:T(8,128)S(1)} %get-tuple-element.62), channel_id=1, source_target_pairs={{0,16},{4,20},{8,24},{12,28},{16,0},{20,4},{24,8},{28,12},{1,17},{... | collective-permute-start | bytes 196616 | tf_op jit(solution)/shard_map/ppermute | solution.py:299
  59.9 1.3 %collective-permute-start.22 = (f32[16,1024]{1,0:T(8,128)S(1)}, f32[16,1024]{1,0:T(8,128)S(1)}, u32[]{:S(2)}, u32[]{:S(2)}) collective-permute-start(f32[16,1024]{1,0:T(8,128)S(1)} %shard_map.87.t_ref), channel_id=1, source_target_pairs={{0,1},{1,0},{2,3},{3,2},{4,5},{5,4},{6,7},{7,6},{8,9},{9,8},{10,11... | collective-permute-start | bytes 196616 | tf_op jit(solution)/shard_map/ppermute | solution.py:304
  (1 other events, 14.4 us)

commit v6 on v5

--- a/solution.py
+++ b/solution.py
@@ -196,31 +196,41 @@
     g_ref[...] = gram_terms(p_ref, b_ref, 0)
 
 
+def side():
+    tensor = lax.axis_index("tensor")
+    return (tensor ^ (tensor // 2)) % 2
+
+
 def pull_kernel(s0, s1, s2, s3, f_ref, h_ref, v_ref, p_ref, keep_ref, send_ref, t_ref):
     q = lax.axis_index("dp") % SQUARE
-    core = lax.axis_index("tensor") % 2
+    mine = side()
     rows, half = s0.shape[0], keep_ref.shape[0]
     first = h_ref.shape[1] - s0.shape[1]
     pulled = v_ref[...] + pulled_rows((s0, s1, s2, s3), f_ref, h_ref, p_ref, first)
     for i, m in enumerate(SUMS_AWAY):
         t_ref[pl.ds((q ^ m) * rows, rows), :] = pulled[i * rows : (i + 1) * rows]
-    keep_ref[...] = t_ref[pl.ds(core * half, half), :]
-    send_ref[...] = t_ref[pl.ds((1 - core) * half, half), :]
-
-
-def gram_kernel(p_ref, b_ref, g_ref, out_ref):
-    out_ref[...] = g_ref[...] + gram_terms(p_ref, b_ref, b_ref.shape[1] - p_ref.shape[1])
-
-
-def push_kernel(mine_ref, got_ref, o_ref, after_ref, *outs):
+    keep_ref[...] = t_ref[pl.ds(mine * half, half), :]
+    send_ref[...] = t_ref[pl.ds((1 - mine) * half, half), :]
+
+
+def gram_kernel(p_ref, b_ref, g_ref, keep_ref, out_ref):
+    grams = g_ref[...] + gram_terms(p_ref, b_ref, b_ref.shape[1] - p_ref.shape[1])
+    half, tokens = keep_ref.shape
+    out_ref[:, :tokens] = keep_ref[...]
+    out_ref[:, tokens : tokens + 128] = grams[:half]
+    out_ref[:, tokens + 128 :] = grams[half:]
+
+
+def push_kernel(mine_ref, got_ref, o_ref, *outs):
     me = lax.axis_index("dp")
+    up = lax.axis_index("tensor") // 2
     tokens = o_ref.shape[0]
     half, width = outs[0].shape[1:]
-    v = jnp.concatenate(split(mine_ref[...] + got_ref[...], 2), axis=0)
+    v = jnp.concatenate(split(mine_ref[:, :tokens] + got_ref[:, :tokens], 2), axis=0)
     for i, m in enumerate(RIGHT_AWAY):
         for z in range(2):
-            cut = pl.ds(pl.multiple_of((me ^ m ^ (SQUARE * z)) * width, width), width)
-            both = dot(v, o_ref[:, cut], NN)
+            start = pl.multiple_of((me ^ m ^ (SQUARE * z)) * (2 * width) + up * width, width)
+            both = dot(v, o_ref[:, pl.ds(start, width)], NN)
             outs[i][z] = both[:half] + both[half:]
 
 
@@ -229,7 +239,9 @@
     shape, block = out_ref.shape, 8
     row = lax.broadcasted_iota(jnp.int32, shape, 0)
     lane = lax.broadcasted_iota(jnp.int32, shape, 1)
-    a = jnp.where(lane == row + 2 * rank, 1.0, mine_ref[...] + got_ref[...])
+    grams = mine_ref[...] + got_ref[...]
+    grams = jnp.concatenate([grams[:, : shape[1]], grams[:, shape[1] :]], axis=0)
+    a = jnp.where(lane == row + 2 * rank, 1.0, grams)
     for k in range(0, rank, block):
         rows = [jnp.broadcast_to(a[k + i : k + i + 1, :], shape) for i in range(block)]
         columns = [jnp.broadcast_to(a[:, k + i : k + i + 1], shape) for i in range(block)]
@@ -251,8 +263,13 @@
     far_ref[...] = a_ref[1] + b_ref[1] + c_ref[1] + d_ref[1]
 
 
-def total_kernel(a_ref, b_ref, after_ref, out_ref):
-    out_ref[...] = a_ref[...] + b_ref[...]
+def total_kernel(up_far_ref, far_ref, up_near_ref, near_ref, after_ref, out_ref):
+    up = lax.axis_index("tensor") // 2
+    width = near_ref.shape[1]
+    mine = pl.ds(pl.multiple_of(up * width, width), width)
+    other = pl.ds(pl.multiple_of((1 - up) * width, width), width)
+    out_ref[:, mine] = near_ref[...] + far_ref[...]
+    out_ref[:, other] = up_near_ref[...] + up_far_ref[...]
 
 
 def basis_kernel(p_ref, r_ref, l_ref, w_ref, out_ref, fix_ref, *, norm_scale):
@@ -269,11 +286,11 @@
 
 
 def factor_kernel(t_ref, u_ref, l_ref, fix_ref, out_ref, z_ref, *, replicas):
-    core = lax.axis_index("tensor") % 2
+    mine = side()
     half = t_ref.shape[0]
     rank = 2 * half
-    z_ref[pl.ds(core * half, half), :] = t_ref[...]
-    z_ref[pl.ds((1 - core) * half, half), :] = u_ref[...]
+    z_ref[pl.ds(mine * half, half), :] = t_ref[...]
+    z_ref[pl.ds((1 - mine) * half, half), :] = u_ref[...]
     inverse = l_ref[:, 2 * rank : 3 * rank] * (1.0 / replicas)
     out_ref[...] = exact_dot(inverse, z_ref[...]) - fix_ref[...]
 
@@ -302,6 +319,12 @@
 def swap_tensor(x, m):
     n = lax.axis_size("tensor")
     return lax.ppermute(x, "tensor", [(i, i ^ m) for i in range(n)])
+
+
+def swap_both(x, md, mt):
+    n, k = lax.axis_size("dp"), lax.axis_size("tensor")
+    pairs = [(i * k + t, (i ^ md) * k + (t ^ mt)) for i in range(n) for t in range(k)]
+    return lax.ppermute(x, ("dp", "tensor"), pairs)
 
 
 def on_device(hidden, out_grad, prev_hidden, prev_grad, prev_basis, warm_start, *, norm_scale):
@@ -369,32 +392,31 @@
         moved=4 * tokens * rest + 4 * rank * rest,
     )(*late_p, late_feedback, hiddens, early_v)
     other = swap_tensor(send, 1)
-    (gram,) = call(
+    (kept,) = call(
         gram_kernel,
-        [(rank, 128)],
-        [VMEM_SPEC] * 3,
+        [(half, 2 * tokens + 256)],
+        [VMEM_SPEC] * 4,
         flops=36 * rank * rank * rest,
         moved=8 * rank * rest,
-    )(p_rest, b, early_gram)
-    other, gram = lax.optimization_barrier((other, gram))
-    plane = keep + other
-    plane_came = swap_tensor(plane, 2)
-    gram = gram + swap_tensor(gram, 1)
-    gram_came = swap_tensor(gram, 2)
+    )(p_rest, b, early_gram, keep)
+    plane = kept + jnp.pad(other, ((0, 0), (0, 256)))
+    plane_came = swap_both(plane, 0, 3)
+    grams = (plane + plane_came)[:, 2 * tokens :]
+    grams_came = swap_tensor(grams, 1)
     parts = call(
         push_kernel,
-        [(2, half, owned)] * SQUARE,
-        [VMEM_SPEC] * 3 + [ANY_SPEC],
+        [(2, half, owned // 2)] * SQUARE,
+        [VMEM_SPEC] * 3,
         flops=8 * tokens * half * width,
         moved=4 * tokens * width + 4 * half * width,
-    )(plane, plane_came, out_grads, gram)
+    )(plane, plane_came, out_grads)
     came = swap_square(parts, RIGHT_AWAY)
     (solved,) = call(
         cholesky_kernel, [(rank, 128)], [VMEM_SPEC] * 2, flops=rank**3, moved=8 * rank * 128
-    )(gram, gram_came)
+    )(grams, grams_came)
     near, far = call(
         near_far_kernel,
-        [(half, owned)] * 2,
+        [(half, owned // 2)] * 2,
         [VMEM_SPEC] * 4 + [ANY_SPEC],
         flops=6 * half * owned,
         moved=40 * half * owned,
@@ -406,13 +428,16 @@
         flops=2 * rank * rank * units,
         moved=8 * rank * units,
     )(p_first, p_rest, solved, w)
+    up_far = swap_both(far, SQUARE, 3)
+    far_came = swap_both(far, SQUARE, 0)
+    up_near = swap_both(near, 0, 3)
     (mine,) = call(
         total_kernel,
         [(half, owned)],
-        [VMEM_SPEC] * 2 + [ANY_SPEC],
+        [VMEM_SPEC] * 4 + [ANY_SPEC],
         flops=half * owned,
         moved=12 * half * owned,
-    )(near, swap_dp(far, SQUARE), fix)
+    )(up_far, far_came, up_near, near, fix)
     (factor,) = call(
         functools.partial(factor_kernel, replicas=replicas),
         [(rank, owned)],

time: 62.3 us -> 61.1 us (0.981)
  waiting for transfers between devices: 17.9 us -> 15.5 us
  starting transfers between devices: 29.3 us -> 30.9 us
    ppermute x0 -> x4, starting transfers between devices: none -> 5.18 us  [swap_both(): return lax.ppermute(x, ('dp', 'tensor'), pairs)]
    ppermute x5 -> x3, waiting for transfers between devices: 6.13 us -> 2.53 us  [swap_tensor(): return lax.ppermute(x, 'tensor', [(i, i ^ m) for i in range(n)])]
    ppermute x0 -> x4, waiting for transfers between devices: none -> 3.2 us  [swap_both(): return lax.ppermute(x, ('dp', 'tensor'), pairs)]
    ppermute x5 -> x3, starting transfers between devices: 3.33 us -> 0.61 us  [swap_tensor(): return lax.ppermute(x, 'tensor', [(i, i ^ m) for i in range(n)])]
    ppermute x18 -> x17, waiting for transfers between devices: 11.8 us -> 9.72 us  [swap_dp(): return lax.ppermute(x, 'dp', [(i, i ^ m) for i in range(n)])]
    ppermute x18 -> x17, starting transfers between devices: 26 us -> 25.2 us  [swap_dp(): return lax.ppermute(x, 'dp', [(i, i ^ m) for i in range(n)])]
  transfers between devices with their start and end apart: 23 -> 24, of which waited for: 16 -> 18; matrix products, arithmetic and copies ran while one was open for 0% -> 0% of each run, Pallas kernels for 11% -> 11%
where the time goes in v6:
time: 61.1 us; the launch traced here: 60.9 us
  starting transfers between devices  30.9 us (51%)
  waiting for transfers between devices  15.5 us (25%)
  Pallas kernels  13.7 us (22%)
  between operations  0.72 us (1%)
    ppermute x17, starting transfers between devices, swap_dp(): return lax.ppermute(x, 'dp', [(i, i ^ m) for i in range(n)])  25.2 us
    ppermute x17, waiting for transfers between devices, swap_dp(): return lax.ppermute(x, 'dp', [(i, i ^ m) for i in range(n)])  9.72 us
    ppermute x4, starting transfers between devices, swap_both(): return lax.ppermute(x, ('dp', 'tensor'), pairs)  5.18 us
    pallas_call x1, Pallas kernels, on_device(): call(first_term_kernel, [(rows, first)] * SQUARE + [(rank, 2 * tokens), (...  4.97 us
    ppermute x4, waiting for transfers between devices, swap_both(): return lax.ppermute(x, ('dp', 'tensor'), pairs)  3.2 us
    ppermute x3, waiting for transfers between devices, swap_tensor(): return lax.ppermute(x, 'tensor', [(i, i ^ m) for i in range(n)])  2.53 us
    pallas_call x1, Pallas kernels, on_device(): call(feedback_kernel, [(rank, first), (rank, rest)], [VMEM_SPEC] * 2 + [A...  1.91 us
    pallas_call x1, Pallas kernels, on_device(): call(functools.partial(basis_kernel, norm_scale=norm_scale), [(rank, unit...  1.59 us
  transfers between devices with their start and end apart: 24, of which 18 were waited for; matrix products, arithmetic and copies ran while one was open for 0% of the time, Pallas kernels for 11%

profile of v6, /device:TPU:0, one launch (start us, length us, event | category | flops | bytes accessed | tf_op | source)
XLA Modules:
  0.0 60.9 jit_solution(12164090749199710572)
XLA Ops:
  0.6 5.0 %shard_map.77 = (f32[8,3584]{1,0:T(8,128)S(1)}, f32[8,3584]{1,0:T(8,128)S(1)}, f32[8,3584]{1,0:T(8,128)S(1)}, f32[8,3584]{1,0:T(8,128)S(1)}, f32[32,256]{1,0:T(8...) custom-call(f32[32,8192]{1,0:T(8,128)} %bitcast.4, bf16[128,8192]{1,0:T(8,128)(2,1)} %o_ref.1, ...), custom_call_target="tpu_custom_call" | custom-call | flops 192937984 | bytes 9371648 | tf_op jit(solution)/shard_map/pallas_call | solution.py:340
  5.6 3.0 %collective-permute-start.2 = (f32[8,3584]{1,0:T(8,128)S(1)}, f32[8,3584]{1,0:T(8,128)S(1)}, u32[]{:S(2)}, u32[]{:S(2)}) collective-permute-start(f32[8,3584]{1,0:T(8,128)S(1)} %get-tuple-element.34), channel_id=1, source_target_pairs={{0,4},{4,0},{8,12},{12,8},{16,20},{20,16},{24,28},{28,24},{1,5},{5... | collective-permute-start | bytes 344072 | tf_op jit(solution)/shard_map/ppermute | solution.py:316
  8.6 1.5 %collective-permute-start = (f32[8,3584]{1,0:T(8,128)S(1)}, f32[8,3584]{1,0:T(8,128)S(1)}, u32[]{:S(2)}, u32[]{:S(2)}) collective-permute-start(f32[8,3584]{1,0:T(8,128)S(1)} %get-tuple-element.32), channel_id=1, source_target_pairs={{0,12},{4,8},{8,4},{12,0},{16,28},{20,24},{24,20},{28,16},{1,13},{... | collective-permute-start | bytes 344072 | tf_op jit(solution)/shard_map/ppermute | solution.py:316
  10.6 1.9 %collective-permute-start.6 = (f32[8,3584]{1,0:T(8,128)S(1)}, f32[8,3584]{1,0:T(8,128)S(1)}, u32[]{:S(2)}, u32[]{:S(2)}) collective-permute-start(f32[8,3584]{1,0:T(8,128)S(1)} %get-tuple-element.40), channel_id=1, source_target_pairs={{0,4},{4,0},{8,12},{12,8},{16,20},{20,16},{24,28},{28,24},{1,5},{5... | collective-permute-start | bytes 344072 | tf_op jit(solution)/shard_map/ppermute | solution.py:316
  12.6 1.5 %collective-permute-start.4 = (f32[8,3584]{1,0:T(8,128)S(1)}, f32[8,3584]{1,0:T(8,128)S(1)}, u32[]{:S(2)}, u32[]{:S(2)}) collective-permute-start(f32[8,3584]{1,0:T(8,128)S(1)} %get-tuple-element.38), channel_id=1, source_target_pairs={{0,12},{4,8},{8,4},{12,0},{16,28},{20,24},{24,20},{28,16},{1,13},{... | collective-permute-start | bytes 344072 | tf_op jit(solution)/shard_map/ppermute | solution.py:316
  15.1 1.2 %collective-permute-start.5 = (f32[8,3584]{1,0:T(8,128)S(1)}, f32[8,3584]{1,0:T(8,128)S(1)}, u32[]{:S(2)}, u32[]{:S(2)}) collective-permute-start(f32[8,3584]{1,0:T(8,128)S(1)} %get-tuple-element.39), channel_id=1, source_target_pairs={{0,8},{4,12},{8,0},{12,4},{16,24},{20,28},{24,16},{28,20},{1,9},{5... | collective-permute-start | bytes 344072 | tf_op jit(solution)/shard_map/ppermute | solution.py:316
  16.7 3.1 %collective-permute-start.3 = (f32[8,3584]{1,0:T(8,128)S(1)}, f32[8,3584]{1,0:T(8,128)S(1)}, u32[]{:S(2)}, u32[]{:S(2)}) collective-permute-start(f32[8,3584]{1,0:T(8,128)S(1)} %add_add_fusion.1), channel_id=1, source_target_pairs={{0,16},{4,20},{8,24},{12,28},{16,0},{20,4},{24,8},{28,12},{1,17},{... | collective-permute-start | bytes 344072 | tf_op jit(solution)/shard_map/ppermute | solution.py:316
  19.7 1.8 %collective-permute-done.4 = f32[8,3584]{1,0:T(8,128)S(1)} collective-permute-done((f32[8,3584]{1,0:T(8,128)S(1)}, f32[8,3584]{1,0:T(8,128)S(1)}, u32[]{:S(2)}, u32[]{:S(2)}) %collective-permute-start.4) | collective-permute-done | bytes 114720 | tf_op jit(solution)/shard_map/ppermute | solution.py:316
  22.2 2.4 %collective-permute-start.10 = (f32[8,3584]{1,0:T(8,128)S(1)}, f32[8,3584]{1,0:T(8,128)S(1)}, u32[]{:S(2)}, u32[]{:S(2)}) collective-permute-start(f32[8,3584]{1,0:T(8,128)S(1)} %add_add_fusion.after_ref), channel_id=1, source_target_pairs={{0,16},{4,20},{8,24},{12,28},{16,0},{20,4},{24,8},{28,12},{1,17},{... | collective-permute-start | bytes 344072 | tf_op jit(solution)/shard_map/ppermute | solution.py:316
  24.5 1.9 %shard_map.79 = (f32[32,3584]{1,0:T(8,128)S(1)}, f32[32,3584]{1,0:T(8,128)S(1)}) custom-call(f32[32,8192]{1,0:T(8,128)S(1)} %bitcast.5, f32[32,7168]{1,0:T(8,128)S(1)} %bitcast.7, f32[8,3584]{1,0:T(8,128)S(1)} %add_add_fusion.after_ref), custom_call_target="tpu_custom_call" | custom-call | flops 31457280 | bytes 1966080 | tf_op jit(solution)/shard_map/pallas_call | solution.py:367
  26.5 3.2 %collective-permute-start.7 = (f32[8,3584]{1,0:T(8,128)S(1)}, f32[8,3584]{1,0:T(8,128)S(1)}, u32[]{:S(2)}, u32[]{:S(2)}) collective-permute-start(f32[8,3584]{1,0:T(8,128)S(1)} %add_multiply_fusion.1.s0), channel_id=1, source_target_pairs={{0,12},{4,8},{8,4},{12,0},{16,28},{20,24},{24,20},{28,16},{1,13},{... | collective-permute-start | bytes 344072 | tf_op jit(solution)/shard_map/ppermute | solution.py:316
  30.4 2.9 %collective-permute-start.11 = (f32[8,3584]{1,0:T(8,128)S(1)}, f32[8,3584]{1,0:T(8,128)S(1)}, u32[]{:S(2)}, u32[]{:S(2)}) collective-permute-start(f32[8,3584]{1,0:T(8,128)S(1)} %add_multiply_fusion.s0), channel_id=1, source_target_pairs={{0,12},{4,8},{8,4},{12,0},{16,28},{20,24},{24,20},{28,16},{1,13},{... | collective-permute-start | bytes 344072 | tf_op jit(solution)/shard_map/ppermute | solution.py:316
  34.0 1.1 %collective-permute-done.8.s2 = f32[8,3584]{1,0:T(8,128)S(1)} collective-permute-done((f32[8,3584]{1,0:T(8,128)S(1)}, f32[8,3584]{1,0:T(8,128)S(1)}, u32[]{:S(2)}, u32[]{:S(2)}) %collective-permute-start.8) | collective-permute-done | bytes 114720 | tf_op jit(solution)/shard_map/ppermute | solution.py:316
  35.1 1.1 %collective-permute-done.9.s3 = f32[8,3584]{1,0:T(8,128)S(1)} collective-permute-done((f32[8,3584]{1,0:T(8,128)S(1)}, f32[8,3584]{1,0:T(8,128)S(1)}, u32[]{:S(2)}, u32[]{:S(2)}) %collective-permute-start.9) | collective-permute-done | bytes 114720 | tf_op jit(solution)/shard_map/ppermute | solution.py:316
  36.2 1.2 %shard_map.80 = (f32[32,3584]{1,0:T(8,128)S(1)}, f32[32,256]{1,0:T(8,128)S(1)}, f32[32,128]{1,0:T(8,128)S(1)}) custom-call(f32[8,3584]{1,0:T(8,128)S(1)} %add_multiply_fusion.1.s0, f32[8,3584]{1,0:T(8,128)S(1)} %collective-permute-done.7.s1, f32[8,3584]{1,0:T(8,128)S(1)} %collective-permute-done.8.s2, f32[8,3584]{1,0:T(8,128)S(1)} %collective-permute-done.9.s3, ...), custom_call_target="tpu_custom_call" | custom-call | flops 117440512 | bytes 2293760 | tf_op jit(solution)/shard_map/pallas_call | solution.py:379
  37.5 1.1 %collective-permute-done.11.s1 = f32[8,3584]{1,0:T(8,128)S(1)} collective-permute-done((f32[8,3584]{1,0:T(8,128)S(1)}, f32[8,3584]{1,0:T(8,128)S(1)}, u32[]{:S(2)}, u32[]{:S(2)}) %collective-permute-start.11) | collective-permute-done | bytes 114720 | tf_op jit(solution)/shard_map/ppermute | solution.py:316
  41.6 1.3 %collective-permute-start.15 = (f32[16,512]{1,0:T(8,128)S(1)}, f32[16,512]{1,0:T(8,128)S(1)}, u32[]{:S(2)}, u32[]{:S(2)}) collective-permute-start(f32[16,512]{1,0:T(8,128)S(1)} %pad_add_fusion.mine_ref), channel_id=1, source_target_pairs={{0,3},{1,2},{2,1},{3,0},{4,7},{5,6},{6,5},{7,4},{8,11},{9,10},{10,... | collective-permute-start | bytes 98312 | tf_op jit(solution)/shard_map/ppermute | solution.py:327
  42.9 2.1 %collective-permute-done.15.got_ref = f32[16,512]{1,0:T(8,128)S(1)} collective-permute-done((f32[16,512]{1,0:T(8,128)S(1)}, f32[16,512]{1,0:T(8,128)S(1)}, u32[]{:S(2)}, u32[]{:S(2)}) %collective-permute-start.15) | collective-permute-done | bytes 32800 | tf_op jit(solution)/shard_map/ppermute | solution.py:327
  45.4 1.4 %collective-permute-start.17 = (f32[2,16,512]{2,1,0:T(8,128)S(1)}, f32[2,16,512]{2,1,0:T(8,128)S(1)}, u32[]{:S(2)}, u32[]{:S(2)}) collective-permute-start(f32[2,16,512]{2,1,0:T(8,128)S(1)} %get-tuple-element.54), channel_id=1, source_target_pairs={{0,12},{4,8},{8,4},{12,0},{16,28},{20,24},{24,20},{28,16},{1,13},{... | collective-permute-start | bytes 196616 | tf_op jit(solution)/shard_map/ppermute | solution.py:316
  47.6 1.3 %collective-permute-start.19 = (f32[2,16,512]{2,1,0:T(8,128)S(1)}, f32[2,16,512]{2,1,0:T(8,128)S(1)}, u32[]{:S(2)}, u32[]{:S(2)}) collective-permute-start(f32[2,16,512]{2,1,0:T(8,128)S(1)} %get-tuple-element.56), channel_id=1, source_target_pairs={{0,4},{4,0},{8,12},{12,8},{16,20},{20,16},{24,28},{28,24},{1,5},{5... | collective-permute-start | bytes 196616 | tf_op jit(solution)/shard_map/ppermute | solution.py:316
  48.9 1.2 %collective-permute-done.16.got_ref = f32[16,256]{1,0:T(8,128)S(1)} collective-permute-done((f32[16,256]{1,0:T(8,128)S(1)}, f32[16,256]{1,0:T(8,128)S(1)}, u32[]{:S(2)}, u32[]{:S(2)}) %collective-permute-start.16) | collective-permute-done | bytes 16416 | tf_op jit(solution)/shard_map/ppermute | solution.py:321
  52.8 2.1 %collective-permute-start.21 = (f32[16,512]{1,0:T(8,128)S(1)}, f32[16,512]{1,0:T(8,128)S(1)}, u32[]{:S(2)}, u32[]{:S(2)}) collective-permute-start(f32[16,512]{1,0:T(8,128)S(1)} %get-tuple-element.57), channel_id=1, source_target_pairs={{0,16},{1,17},{2,18},{3,19},{4,20},{5,21},{6,22},{7,23},{8,24},{9,... | collective-permute-start | bytes 98312 | tf_op jit(solution)/shard_map/ppermute | solution.py:327
  55.8 1.6 %shard_map.84 = (f32[32,7168]{1,0:T(8,128)}, f32[32,1024]{1,0:T(8,128)S(1)}) custom-call(f32[32,3584]{1,0:T(8,128)S(1)} %get-tuple-element.44.p_ref, f32[32,3584]{1,0:T(8,128)S(1)} %get-tuple-element.47.p_ref.r_ref, f32[32,128]{1,0:T(8,128)S(1)} %shard_map.83.l_ref.after_ref, f32[32,8192]{1,0:T(8,128)S(1)} %bitcast.6), custom_call_target="tpu_custom_call" | custom-call | flops 14680064 | bytes 1835008 | tf_op jit(solution)/shard_map/pallas_call | solution.py:424
  57.4 1.1 %collective-permute-done.21.far_ref = f32[16,512]{1,0:T(8,128)S(1)} collective-permute-done((f32[16,512]{1,0:T(8,128)S(1)}, f32[16,512]{1,0:T(8,128)S(1)}, u32[]{:S(2)}, u32[]{:S(2)}) %collective-permute-start.21) | collective-permute-done | bytes 32800 | tf_op jit(solution)/shard_map/ppermute | solution.py:327
  (46 shorter events, 14.1 us)
Async XLA Ops:
  5.6 9.5 %collective-permute-start.2 = (f32[8,3584]{1,0:T(8,128)S(1)}, f32[8,3584]{1,0:T(8,128)S(1)}, u32[]{:S(2)}, u32[]{:S(2)}) collective-permute-start(f32[8,3584]{1,0:T(8,128)S(1)} %get-tuple-element.34), channel_id=1, source_target_pairs={{0,4},{4,0},{8,12},{12,8},{16,20},{20,16},{24,28},{28,24},{1,5},{5... | collective-permute-start | bytes 344072 | tf_op jit(solution)/shard_map/ppermute | solution.py:316
  8.6 7.7 %collective-permute-start = (f32[8,3584]{1,0:T(8,128)S(1)}, f32[8,3584]{1,0:T(8,128)S(1)}, u32[]{:S(2)}, u32[]{:S(2)}) collective-permute-start(f32[8,3584]{1,0:T(8,128)S(1)} %get-tuple-element.32), channel_id=1, source_target_pairs={{0,12},{4,8},{8,4},{12,0},{16,28},{20,24},{24,20},{28,16},{1,13},{... | collective-permute-start | bytes 344072 | tf_op jit(solution)/shard_map/ppermute | solution.py:316
  10.2 6.5 %collective-permute-start.1 = (f32[8,3584]{1,0:T(8,128)S(1)}, f32[8,3584]{1,0:T(8,128)S(1)}, u32[]{:S(2)}, u32[]{:S(2)}) collective-permute-start(f32[8,3584]{1,0:T(8,128)S(1)} %get-tuple-element.33), channel_id=1, source_target_pairs={{0,8},{4,12},{8,0},{12,4},{16,24},{20,28},{24,16},{28,20},{1,9},{5... | collective-permute-start | bytes 344072 | tf_op jit(solution)/shard_map/ppermute | solution.py:316
  10.6 9.1 %collective-permute-start.6 = (f32[8,3584]{1,0:T(8,128)S(1)}, f32[8,3584]{1,0:T(8,128)S(1)}, u32[]{:S(2)}, u32[]{:S(2)}) collective-permute-start(f32[8,3584]{1,0:T(8,128)S(1)} %get-tuple-element.40), channel_id=1, source_target_pairs={{0,4},{4,0},{8,12},{12,8},{16,20},{20,16},{24,28},{28,24},{1,5},{5... | collective-permute-start | bytes 344072 | tf_op jit(solution)/shard_map/ppermute | solution.py:316
  12.6 9.0 %collective-permute-start.4 = (f32[8,3584]{1,0:T(8,128)S(1)}, f32[8,3584]{1,0:T(8,128)S(1)}, u32[]{:S(2)}, u32[]{:S(2)}) collective-permute-start(f32[8,3584]{1,0:T(8,128)S(1)} %get-tuple-element.38), channel_id=1, source_target_pairs={{0,12},{4,8},{8,4},{12,0},{16,28},{20,24},{24,20},{28,16},{1,13},{... | collective-permute-start | bytes 344072 | tf_op jit(solution)/shard_map/ppermute | solution.py:316
  15.1 7.0 %collective-permute-start.5 = (f32[8,3584]{1,0:T(8,128)S(1)}, f32[8,3584]{1,0:T(8,128)S(1)}, u32[]{:S(2)}, u32[]{:S(2)}) collective-permute-start(f32[8,3584]{1,0:T(8,128)S(1)} %get-tuple-element.39), channel_id=1, source_target_pairs={{0,8},{4,12},{8,0},{12,4},{16,24},{20,28},{24,16},{28,20},{1,9},{5... | collective-permute-start | bytes 344072 | tf_op jit(solution)/shard_map/ppermute | solution.py:316
  16.7 9.8 %collective-permute-start.3 = (f32[8,3584]{1,0:T(8,128)S(1)}, f32[8,3584]{1,0:T(8,128)S(1)}, u32[]{:S(2)}, u32[]{:S(2)}) collective-permute-start(f32[8,3584]{1,0:T(8,128)S(1)} %add_add_fusion.1), channel_id=1, source_target_pairs={{0,16},{4,20},{8,24},{12,28},{16,0},{20,4},{24,8},{28,12},{1,17},{... | collective-permute-start | bytes 344072 | tf_op jit(solution)/shard_map/ppermute | solution.py:316
  22.2 8.2 %collective-permute-start.10 = (f32[8,3584]{1,0:T(8,128)S(1)}, f32[8,3584]{1,0:T(8,128)S(1)}, u32[]{:S(2)}, u32[]{:S(2)}) collective-permute-start(f32[8,3584]{1,0:T(8,128)S(1)} %add_add_fusion.after_ref), channel_id=1, source_target_pairs={{0,16},{4,20},{8,24},{12,28},{16,0},{20,4},{24,8},{28,12},{1,17},{... | collective-permute-start | bytes 344072 | tf_op jit(solution)/shard_map/ppermute | solution.py:316
  26.5 7.4 %collective-permute-start.7 = (f32[8,3584]{1,0:T(8,128)S(1)}, f32[8,3584]{1,0:T(8,128)S(1)}, u32[]{:S(2)}, u32[]{:S(2)}) collective-permute-start(f32[8,3584]{1,0:T(8,128)S(1)} %add_multiply_fusion.1.s0), channel_id=1, source_target_pairs={{0,12},{4,8},{8,4},{12,0},{16,28},{20,24},{24,20},{28,16},{1,13},{... | collective-permute-start | bytes 344072 | tf_op jit(solution)/shard_map/ppermute | solution.py:316
  29.7 5.4 %collective-permute-start.8 = (f32[8,3584]{1,0:T(8,128)S(1)}, f32[8,3584]{1,0:T(8,128)S(1)}, u32[]{:S(2)}, u32[]{:S(2)}) collective-permute-start(f32[8,3584]{1,0:T(8,128)S(1)} %add_multiply_fusion.1.s0), channel_id=1, source_target_pairs={{0,8},{4,12},{8,0},{12,4},{16,24},{20,28},{24,16},{28,20},{1,9},{5... | collective-permute-start | bytes 344072 | tf_op jit(solution)/shard_map/ppermute | solution.py:316
  29.7 6.5 %collective-permute-start.9 = (f32[8,3584]{1,0:T(8,128)S(1)}, f32[8,3584]{1,0:T(8,128)S(1)}, u32[]{:S(2)}, u32[]{:S(2)}) collective-permute-start(f32[8,3584]{1,0:T(8,128)S(1)} %add_multiply_fusion.1.s0), channel_id=1, source_target_pairs={{0,4},{4,0},{8,12},{12,8},{16,20},{20,16},{24,28},{28,24},{1,5},{5... | collective-permute-start | bytes 344072 | tf_op jit(solution)/shard_map/ppermute | solution.py:316
  30.4 8.2 %collective-permute-start.11 = (f32[8,3584]{1,0:T(8,128)S(1)}, f32[8,3584]{1,0:T(8,128)S(1)}, u32[]{:S(2)}, u32[]{:S(2)}) collective-permute-start(f32[8,3584]{1,0:T(8,128)S(1)} %add_multiply_fusion.s0), channel_id=1, source_target_pairs={{0,12},{4,8},{8,4},{12,0},{16,28},{20,24},{24,20},{28,16},{1,13},{... | collective-permute-start | bytes 344072 | tf_op jit(solution)/shard_map/ppermute | solution.py:316
  33.3 6.2 %collective-permute-start.12 = (f32[8,3584]{1,0:T(8,128)S(1)}, f32[8,3584]{1,0:T(8,128)S(1)}, u32[]{:S(2)}, u32[]{:S(2)}) collective-permute-start(f32[8,3584]{1,0:T(8,128)S(1)} %add_multiply_fusion.s0), channel_id=1, source_target_pairs={{0,8},{4,12},{8,0},{12,4},{16,24},{20,28},{24,16},{28,20},{1,9},{5... | collective-permute-start | bytes 344072 | tf_op jit(solution)/shard_map/ppermute | solution.py:316
  33.9 5.8 %collective-permute-start.13 = (f32[8,3584]{1,0:T(8,128)S(1)}, f32[8,3584]{1,0:T(8,128)S(1)}, u32[]{:S(2)}, u32[]{:S(2)}) collective-permute-start(f32[8,3584]{1,0:T(8,128)S(1)} %add_multiply_fusion.s0), channel_id=1, source_target_pairs={{0,4},{4,0},{8,12},{12,8},{16,20},{20,16},{24,28},{28,24},{1,5},{5... | collective-permute-start | bytes 344072 | tf_op jit(solution)/shard_map/ppermute | solution.py:316
  40.4 1.2 %collective-permute-start.14 = (f32[16,256]{1,0:T(8,128)S(1)}, f32[16,256]{1,0:T(8,128)S(1)}, u32[]{:S(2)}, u32[]{:S(2)}) collective-permute-start(f32[16,256]{1,0:T(8,128)S(1)} %get-tuple-element.50), channel_id=1, source_target_pairs={{0,1},{1,0},{2,3},{3,2},{4,5},{5,4},{6,7},{7,6},{8,9},{9,8},{10,11... | collective-permute-start | bytes 49160 | tf_op jit(solution)/shard_map/ppermute | solution.py:321
  41.6 3.3 %collective-permute-start.15 = (f32[16,512]{1,0:T(8,128)S(1)}, f32[16,512]{1,0:T(8,128)S(1)}, u32[]{:S(2)}, u32[]{:S(2)}) collective-permute-start(f32[16,512]{1,0:T(8,128)S(1)} %pad_add_fusion.mine_ref), channel_id=1, source_target_pairs={{0,3},{1,2},{2,1},{3,0},{4,7},{5,6},{6,5},{7,4},{8,11},{9,10},{10,... | collective-permute-start | bytes 98312 | tf_op jit(solution)/shard_map/ppermute | solution.py:327
  45.4 5.7 %collective-permute-start.17 = (f32[2,16,512]{2,1,0:T(8,128)S(1)}, f32[2,16,512]{2,1,0:T(8,128)S(1)}, u32[]{:S(2)}, u32[]{:S(2)}) collective-permute-start(f32[2,16,512]{2,1,0:T(8,128)S(1)} %get-tuple-element.54), channel_id=1, source_target_pairs={{0,12},{4,8},{8,4},{12,0},{16,28},{20,24},{24,20},{28,16},{1,13},{... | collective-permute-start | bytes 196616 | tf_op jit(solution)/shard_map/ppermute | solution.py:316
  46.8 4.5 %collective-permute-start.18 = (f32[2,16,512]{2,1,0:T(8,128)S(1)}, f32[2,16,512]{2,1,0:T(8,128)S(1)}, u32[]{:S(2)}, u32[]{:S(2)}) collective-permute-start(f32[2,16,512]{2,1,0:T(8,128)S(1)} %get-tuple-element.55), channel_id=1, source_target_pairs={{0,8},{4,12},{8,0},{12,4},{16,24},{20,28},{24,16},{28,20},{1,9},{5... | collective-permute-start | bytes 196616 | tf_op jit(solution)/shard_map/ppermute | solution.py:316
  47.6 4.3 %collective-permute-start.19 = (f32[2,16,512]{2,1,0:T(8,128)S(1)}, f32[2,16,512]{2,1,0:T(8,128)S(1)}, u32[]{:S(2)}, u32[]{:S(2)}) collective-permute-start(f32[2,16,512]{2,1,0:T(8,128)S(1)} %get-tuple-element.56), channel_id=1, source_target_pairs={{0,4},{4,0},{8,12},{12,8},{16,20},{20,16},{24,28},{28,24},{1,5},{5... | collective-permute-start | bytes 196616 | tf_op jit(solution)/shard_map/ppermute | solution.py:316
  48.9 1.2 %collective-permute-start.16 = (f32[16,256]{1,0:T(8,128)S(1)}, f32[16,256]{1,0:T(8,128)S(1)}, u32[]{:S(2)}, u32[]{:S(2)}) collective-permute-start(f32[16,256]{1,0:T(8,128)S(1)} %slice_add_fusion.mine_ref), channel_id=1, source_target_pairs={{0,1},{1,0},{2,3},{3,2},{4,5},{5,4},{6,7},{7,6},{8,9},{9,8},{10,11... | collective-permute-start | bytes 49160 | tf_op jit(solution)/shard_map/ppermute | solution.py:321
  51.9 5.5 %collective-permute-start.20 = (f32[16,512]{1,0:T(8,128)S(1)}, f32[16,512]{1,0:T(8,128)S(1)}, u32[]{:S(2)}, u32[]{:S(2)}) collective-permute-start(f32[16,512]{1,0:T(8,128)S(1)} %get-tuple-element.57), channel_id=1, source_target_pairs={{0,19},{1,18},{2,17},{3,16},{4,23},{5,22},{6,21},{7,20},{8,27},{9,... | collective-permute-start | bytes 98312 | tf_op jit(solution)/shard_map/ppermute | solution.py:327
  52.8 5.8 %collective-permute-start.21 = (f32[16,512]{1,0:T(8,128)S(1)}, f32[16,512]{1,0:T(8,128)S(1)}, u32[]{:S(2)}, u32[]{:S(2)}) collective-permute-start(f32[16,512]{1,0:T(8,128)S(1)} %get-tuple-element.57), channel_id=1, source_target_pairs={{0,16},{1,17},{2,18},{3,19},{4,20},{5,21},{6,22},{7,23},{8,24},{9,... | collective-permute-start | bytes 98312 | tf_op jit(solution)/shard_map/ppermute | solution.py:327
  54.9 3.7 %collective-permute-start.22 = (f32[16,512]{1,0:T(8,128)S(1)}, f32[16,512]{1,0:T(8,128)S(1)}, u32[]{:S(2)}, u32[]{:S(2)}) collective-permute-start(f32[16,512]{1,0:T(8,128)S(1)} %get-tuple-element.58.near_ref), channel_id=1, source_target_pairs={{0,3},{1,2},{2,1},{3,0},{4,7},{5,6},{6,5},{7,4},{8,11},{9,10},{10,... | collective-permute-start | bytes 98312 | tf_op jit(solution)/shard_map/ppermute | solution.py:327
  58.6 1.4 %collective-permute-start.23 = (f32[16,1024]{1,0:T(8,128)S(1)}, f32[16,1024]{1,0:T(8,128)S(1)}, u32[]{:S(2)}, u32[]{:S(2)}) collective-permute-start(f32[16,1024]{1,0:T(8,128)S(1)} %shard_map.87.t_ref), channel_id=1, source_target_pairs={{0,1},{1,0},{2,3},{3,2},{4,5},{5,4},{6,7},{7,6},{8,9},{9,8},{10,11... | collective-permute-start | bytes 196616 | tf_op jit(solution)/shard_map/ppermute | solution.py:321
  (2 other events, 28.7 us)

commit v7 on v6

--- a/solution.py
+++ b/solution.py
@@ -263,13 +263,16 @@
     far_ref[...] = a_ref[1] + b_ref[1] + c_ref[1] + d_ref[1]
 
 
-def total_kernel(up_far_ref, far_ref, up_near_ref, near_ref, after_ref, out_ref):
+def total_kernel(up_far_ref, far_ref, up_near_ref, near_ref, l_ref, after_ref, out_ref, *, replicas):
     up = lax.axis_index("tensor") // 2
-    width = near_ref.shape[1]
+    half, width = near_ref.shape
+    rank = 2 * half
+    inverse = l_ref[:, 2 * rank : 3 * rank] * (1.0 / replicas)
+    inverse = jnp.where(side() == 0, inverse[:, :half], inverse[:, half:])
     mine = pl.ds(pl.multiple_of(up * width, width), width)
     other = pl.ds(pl.multiple_of((1 - up) * width, width), width)
-    out_ref[:, mine] = near_ref[...] + far_ref[...]
-    out_ref[:, other] = up_near_ref[...] + up_far_ref[...]
+    out_ref[:, mine] = exact_dot(inverse, near_ref[...] + far_ref[...])
+    out_ref[:, other] = exact_dot(inverse, up_near_ref[...] + up_far_ref[...])
 
 
 def basis_kernel(p_ref, r_ref, l_ref, w_ref, out_ref, fix_ref, *, norm_scale):
@@ -283,16 +286,6 @@
         first += ref.shape[1]
     own = pl.ds(pl.multiple_of(lax.axis_index("dp") * width, width), width)
     fix_ref[...] = exact_dot(l_ref[:, rank : 2 * rank], w_ref[:, own])
-
-
-def factor_kernel(t_ref, u_ref, l_ref, fix_ref, out_ref, z_ref, *, replicas):
-    mine = side()
-    half = t_ref.shape[0]
-    rank = 2 * half
-    z_ref[pl.ds(mine * half, half), :] = t_ref[...]
-    z_ref[pl.ds((1 - mine) * half, half), :] = u_ref[...]
-    inverse = l_ref[:, 2 * rank : 3 * rank] * (1.0 / replicas)
-    out_ref[...] = exact_dot(inverse, z_ref[...]) - fix_ref[...]
 
 
 def call(kernel, outs, specs, scratch=(), flops=0, moved=0, vmem=32 << 20):
@@ -432,20 +425,13 @@
     far_came = swap_both(far, SQUARE, 0)
     up_near = swap_both(near, 0, 3)
     (mine,) = call(
-        total_kernel,
-        [(half, owned)],
-        [VMEM_SPEC] * 4 + [ANY_SPEC],
-        flops=half * owned,
+        functools.partial(total_kernel, replicas=replicas),
+        [(rank, owned)],
+        [VMEM_SPEC] * 5 + [ANY_SPEC],
+        flops=rank * rank * owned,
         moved=12 * half * owned,
-    )(up_far, far_came, up_near, near, fix)
-    (factor,) = call(
-        functools.partial(factor_kernel, replicas=replicas),
-        [(rank, owned)],
-        [VMEM_SPEC] * 4,
-        [pltpu.VMEM((rank, owned), F32)],
-        flops=2 * rank * rank * owned,
-        moved=12 * rank * owned,
-    )(mine, swap_tensor(mine, 1), solved, fix)
+    )(up_far, far_came, up_near, near, solved, fix)
+    factor = mine + swap_tensor(mine, 1) - fix
     return (basis.T, factor.T)
 
 

time: 61.1 us -> 61.2 us (level)
  other arithmetic: 0.09 us -> 0.77 us
    transpose x0 -> x1, other arithmetic: none -> 0.68 us  [on_device(): return (basis.T, factor.T)]
    pallas_call x2 -> x1, Pallas kernels: 0.9 us -> 0.27 us  [on_device(): call(functools.partial(total_kernel, replicas=replicas), [(rank, owned)],...]
where the time goes in v7:
time: 61.2 us; the launch traced here: 61.1 us
  starting transfers between devices  31 us (51%)
  waiting for transfers between devices  15.5 us (25%)
  Pallas kernels  13.1 us (21%)
  other arithmetic  0.77 us (1%)
  between operations  0.71 us (1%)
    ppermute x17, starting transfers between devices, swap_dp(): return lax.ppermute(x, 'dp', [(i, i ^ m) for i in range(n)])  25.2 us
    ppermute x17, waiting for transfers between devices, swap_dp(): return lax.ppermute(x, 'dp', [(i, i ^ m) for i in range(n)])  9.72 us
    ppermute x4, starting transfers between devices, swap_both(): return lax.ppermute(x, ('dp', 'tensor'), pairs)  5.18 us
    pallas_call x1, Pallas kernels, on_device(): call(first_term_kernel, [(rows, first)] * SQUARE + [(rank, 2 * tokens), (...  4.97 us
    ppermute x4, waiting for transfers between devices, swap_both(): return lax.ppermute(x, ('dp', 'tensor'), pairs)  3.2 us
    ppermute x3, waiting for transfers between devices, swap_tensor(): return lax.ppermute(x, 'tensor', [(i, i ^ m) for i in range(n)])  2.61 us
    pallas_call x1, Pallas kernels, on_device(): call(feedback_kernel, [(rank, first), (rank, rest)], [VMEM_SPEC] * 2 + [A...  1.91 us
    pallas_call x1, Pallas kernels, on_device(): call(functools.partial(basis_kernel, norm_scale=norm_scale), [(rank, unit...  1.6 us
  transfers between devices with their start and end apart: 24, of which 18 were waited for; matrix products, arithmetic and copies ran while one was open for 0% of the time, Pallas kernels for 11%

profile of v7, /device:TPU:0, one launch (start us, length us, event | category | flops | bytes accessed | tf_op | source)
XLA Modules:
  0.0 61.1 jit_solution(1785371768494469025)
XLA Ops:
  0.6 5.0 %shard_map.77 = (f32[8,3584]{1,0:T(8,128)S(1)}, f32[8,3584]{1,0:T(8,128)S(1)}, f32[8,3584]{1,0:T(8,128)S(1)}, f32[8,3584]{1,0:T(8,128)S(1)}, f32[32,256]{1,0:T(8...) custom-call(f32[32,8192]{1,0:T(8,128)} %bitcast.5, bf16[128,8192]{1,0:T(8,128)(2,1)} %o_ref.1, ...), custom_call_target="tpu_custom_call" | custom-call | flops 192937984 | bytes 9371648 | tf_op jit(solution)/shard_map/pallas_call | solution.py:333
  5.6 3.0 %collective-permute-start.2 = (f32[8,3584]{1,0:T(8,128)S(1)}, f32[8,3584]{1,0:T(8,128)S(1)}, u32[]{:S(2)}, u32[]{:S(2)}) collective-permute-start(f32[8,3584]{1,0:T(8,128)S(1)} %get-tuple-element.34), channel_id=1, source_target_pairs={{0,4},{4,0},{8,12},{12,8},{16,20},{20,16},{24,28},{28,24},{1,5},{5... | collective-permute-start | bytes 344072 | tf_op jit(solution)/shard_map/ppermute | solution.py:309
  8.6 1.5 %collective-permute-start = (f32[8,3584]{1,0:T(8,128)S(1)}, f32[8,3584]{1,0:T(8,128)S(1)}, u32[]{:S(2)}, u32[]{:S(2)}) collective-permute-start(f32[8,3584]{1,0:T(8,128)S(1)} %get-tuple-element.32), channel_id=1, source_target_pairs={{0,12},{4,8},{8,4},{12,0},{16,28},{20,24},{24,20},{28,16},{1,13},{... | collective-permute-start | bytes 344072 | tf_op jit(solution)/shard_map/ppermute | solution.py:309
  10.6 1.9 %collective-permute-start.6 = (f32[8,3584]{1,0:T(8,128)S(1)}, f32[8,3584]{1,0:T(8,128)S(1)}, u32[]{:S(2)}, u32[]{:S(2)}) collective-permute-start(f32[8,3584]{1,0:T(8,128)S(1)} %get-tuple-element.40), channel_id=1, source_target_pairs={{0,4},{4,0},{8,12},{12,8},{16,20},{20,16},{24,28},{28,24},{1,5},{5... | collective-permute-start | bytes 344072 | tf_op jit(solution)/shard_map/ppermute | solution.py:309
  12.6 1.5 %collective-permute-start.4 = (f32[8,3584]{1,0:T(8,128)S(1)}, f32[8,3584]{1,0:T(8,128)S(1)}, u32[]{:S(2)}, u32[]{:S(2)}) collective-permute-start(f32[8,3584]{1,0:T(8,128)S(1)} %get-tuple-element.38), channel_id=1, source_target_pairs={{0,12},{4,8},{8,4},{12,0},{16,28},{20,24},{24,20},{28,16},{1,13},{... | collective-permute-start | bytes 344072 | tf_op jit(solution)/shard_map/ppermute | solution.py:309
  15.1 1.2 %collective-permute-start.5 = (f32[8,3584]{1,0:T(8,128)S(1)}, f32[8,3584]{1,0:T(8,128)S(1)}, u32[]{:S(2)}, u32[]{:S(2)}) collective-permute-start(f32[8,3584]{1,0:T(8,128)S(1)} %get-tuple-element.39), channel_id=1, source_target_pairs={{0,8},{4,12},{8,0},{12,4},{16,24},{20,28},{24,16},{28,20},{1,9},{5... | collective-permute-start | bytes 344072 | tf_op jit(solution)/shard_map/ppermute | solution.py:309
  16.7 3.1 %collective-permute-start.3 = (f32[8,3584]{1,0:T(8,128)S(1)}, f32[8,3584]{1,0:T(8,128)S(1)}, u32[]{:S(2)}, u32[]{:S(2)}) collective-permute-start(f32[8,3584]{1,0:T(8,128)S(1)} %add_add_fusion.1), channel_id=1, source_target_pairs={{0,16},{4,20},{8,24},{12,28},{16,0},{20,4},{24,8},{28,12},{1,17},{... | collective-permute-start | bytes 344072 | tf_op jit(solution)/shard_map/ppermute | solution.py:309
  19.7 1.8 %collective-permute-done.4 = f32[8,3584]{1,0:T(8,128)S(1)} collective-permute-done((f32[8,3584]{1,0:T(8,128)S(1)}, f32[8,3584]{1,0:T(8,128)S(1)}, u32[]{:S(2)}, u32[]{:S(2)}) %collective-permute-start.4) | collective-permute-done | bytes 114720 | tf_op jit(solution)/shard_map/ppermute | solution.py:309
  22.2 2.4 %collective-permute-start.10 = (f32[8,3584]{1,0:T(8,128)S(1)}, f32[8,3584]{1,0:T(8,128)S(1)}, u32[]{:S(2)}, u32[]{:S(2)}) collective-permute-start(f32[8,3584]{1,0:T(8,128)S(1)} %add_add_fusion.after_ref), channel_id=1, source_target_pairs={{0,16},{4,20},{8,24},{12,28},{16,0},{20,4},{24,8},{28,12},{1,17},{... | collective-permute-start | bytes 344072 | tf_op jit(solution)/shard_map/ppermute | solution.py:309
  24.5 1.9 %shard_map.79 = (f32[32,3584]{1,0:T(8,128)S(1)}, f32[32,3584]{1,0:T(8,128)S(1)}) custom-call(f32[32,8192]{1,0:T(8,128)S(1)} %bitcast.6, f32[32,7168]{1,0:T(8,128)S(1)} %bitcast.8, f32[8,3584]{1,0:T(8,128)S(1)} %add_add_fusion.after_ref), custom_call_target="tpu_custom_call" | custom-call | flops 31457280 | bytes 1966080 | tf_op jit(solution)/shard_map/pallas_call | solution.py:360
  26.5 3.2 %collective-permute-start.7 = (f32[8,3584]{1,0:T(8,128)S(1)}, f32[8,3584]{1,0:T(8,128)S(1)}, u32[]{:S(2)}, u32[]{:S(2)}) collective-permute-start(f32[8,3584]{1,0:T(8,128)S(1)} %add_multiply_fusion.1.s0), channel_id=1, source_target_pairs={{0,12},{4,8},{8,4},{12,0},{16,28},{20,24},{24,20},{28,16},{1,13},{... | collective-permute-start | bytes 344072 | tf_op jit(solution)/shard_map/ppermute | solution.py:309
  30.4 2.9 %collective-permute-start.11 = (f32[8,3584]{1,0:T(8,128)S(1)}, f32[8,3584]{1,0:T(8,128)S(1)}, u32[]{:S(2)}, u32[]{:S(2)}) collective-permute-start(f32[8,3584]{1,0:T(8,128)S(1)} %add_multiply_fusion.s0), channel_id=1, source_target_pairs={{0,12},{4,8},{8,4},{12,0},{16,28},{20,24},{24,20},{28,16},{1,13},{... | collective-permute-start | bytes 344072 | tf_op jit(solution)/shard_map/ppermute | solution.py:309
  34.0 1.1 %collective-permute-done.8.s2 = f32[8,3584]{1,0:T(8,128)S(1)} collective-permute-done((f32[8,3584]{1,0:T(8,128)S(1)}, f32[8,3584]{1,0:T(8,128)S(1)}, u32[]{:S(2)}, u32[]{:S(2)}) %collective-permute-start.8) | collective-permute-done | bytes 114720 | tf_op jit(solution)/shard_map/ppermute | solution.py:309
  35.1 1.1 %collective-permute-done.9.s3 = f32[8,3584]{1,0:T(8,128)S(1)} collective-permute-done((f32[8,3584]{1,0:T(8,128)S(1)}, f32[8,3584]{1,0:T(8,128)S(1)}, u32[]{:S(2)}, u32[]{:S(2)}) %collective-permute-start.9) | collective-permute-done | bytes 114720 | tf_op jit(solution)/shard_map/ppermute | solution.py:309
  36.2 1.3 %shard_map.80 = (f32[32,3584]{1,0:T(8,128)S(1)}, f32[32,256]{1,0:T(8,128)S(1)}, f32[32,128]{1,0:T(8,128)S(1)}) custom-call(f32[8,3584]{1,0:T(8,128)S(1)} %add_multiply_fusion.1.s0, f32[8,3584]{1,0:T(8,128)S(1)} %collective-permute-done.7.s1, f32[8,3584]{1,0:T(8,128)S(1)} %collective-permute-done.8.s2, f32[8,3584]{1,0:T(8,128)S(1)} %collective-permute-done.9.s3, ...), custom_call_target="tpu_custom_call" | custom-call | flops 117440512 | bytes 2293760 | tf_op jit(solution)/shard_map/pallas_call | solution.py:372
  37.5 1.1 %collective-permute-done.11.s1 = f32[8,3584]{1,0:T(8,128)S(1)} collective-permute-done((f32[8,3584]{1,0:T(8,128)S(1)}, f32[8,3584]{1,0:T(8,128)S(1)}, u32[]{:S(2)}, u32[]{:S(2)}) %collective-permute-start.11) | collective-permute-done | bytes 114720 | tf_op jit(solution)/shard_map/ppermute | solution.py:309
  41.6 1.3 %collective-permute-start.15 = (f32[16,512]{1,0:T(8,128)S(1)}, f32[16,512]{1,0:T(8,128)S(1)}, u32[]{:S(2)}, u32[]{:S(2)}) collective-permute-start(f32[16,512]{1,0:T(8,128)S(1)} %pad_add_fusion.mine_ref), channel_id=1, source_target_pairs={{0,3},{1,2},{2,1},{3,0},{4,7},{5,6},{6,5},{7,4},{8,11},{9,10},{10,... | collective-permute-start | bytes 98312 | tf_op jit(solution)/shard_map/ppermute | solution.py:320
  42.9 2.1 %collective-permute-done.15.got_ref = f32[16,512]{1,0:T(8,128)S(1)} collective-permute-done((f32[16,512]{1,0:T(8,128)S(1)}, f32[16,512]{1,0:T(8,128)S(1)}, u32[]{:S(2)}, u32[]{:S(2)}) %collective-permute-start.15) | collective-permute-done | bytes 32800 | tf_op jit(solution)/shard_map/ppermute | solution.py:320
  45.4 1.4 %collective-permute-start.17 = (f32[2,16,512]{2,1,0:T(8,128)S(1)}, f32[2,16,512]{2,1,0:T(8,128)S(1)}, u32[]{:S(2)}, u32[]{:S(2)}) collective-permute-start(f32[2,16,512]{2,1,0:T(8,128)S(1)} %get-tuple-element.54), channel_id=1, source_target_pairs={{0,12},{4,8},{8,4},{12,0},{16,28},{20,24},{24,20},{28,16},{1,13},{... | collective-permute-start | bytes 196616 | tf_op jit(solution)/shard_map/ppermute | solution.py:309
  47.6 1.3 %collective-permute-start.19 = (f32[2,16,512]{2,1,0:T(8,128)S(1)}, f32[2,16,512]{2,1,0:T(8,128)S(1)}, u32[]{:S(2)}, u32[]{:S(2)}) collective-permute-start(f32[2,16,512]{2,1,0:T(8,128)S(1)} %get-tuple-element.56), channel_id=1, source_target_pairs={{0,4},{4,0},{8,12},{12,8},{16,20},{20,16},{24,28},{28,24},{1,5},{5... | collective-permute-start | bytes 196616 | tf_op jit(solution)/shard_map/ppermute | solution.py:309
  48.9 1.2 %collective-permute-done.16.got_ref = f32[16,256]{1,0:T(8,128)S(1)} collective-permute-done((f32[16,256]{1,0:T(8,128)S(1)}, f32[16,256]{1,0:T(8,128)S(1)}, u32[]{:S(2)}, u32[]{:S(2)}) %collective-permute-start.16) | collective-permute-done | bytes 16416 | tf_op jit(solution)/shard_map/ppermute | solution.py:314
  52.8 2.1 %collective-permute-start.21 = (f32[16,512]{1,0:T(8,128)S(1)}, f32[16,512]{1,0:T(8,128)S(1)}, u32[]{:S(2)}, u32[]{:S(2)}) collective-permute-start(f32[16,512]{1,0:T(8,128)S(1)} %get-tuple-element.57), channel_id=1, source_target_pairs={{0,16},{1,17},{2,18},{3,19},{4,20},{5,21},{6,22},{7,23},{8,24},{9,... | collective-permute-start | bytes 98312 | tf_op jit(solution)/shard_map/ppermute | solution.py:320
  55.8 1.6 %shard_map.84 = (f32[32,7168]{1,0:T(8,128)}, f32[32,1024]{1,0:T(8,128)S(1)}) custom-call(f32[32,3584]{1,0:T(8,128)S(1)} %get-tuple-element.44.p_ref, f32[32,3584]{1,0:T(8,128)S(1)} %get-tuple-element.47.p_ref.r_ref, f32[32,128]{1,0:T(8,128)S(1)} %shard_map.83.l_ref.after_ref, f32[32,8192]{1,0:T(8,128)S(1)} %bitcast.7), custom_call_target="tpu_custom_call" | custom-call | flops 14680064 | bytes 1835008 | tf_op jit(solution)/shard_map/pallas_call | solution.py:417
  57.4 1.1 %collective-permute-done.21.far_ref = f32[16,512]{1,0:T(8,128)S(1)} collective-permute-done((f32[16,512]{1,0:T(8,128)S(1)}, f32[16,512]{1,0:T(8,128)S(1)}, u32[]{:S(2)}, u32[]{:S(2)}) %collective-permute-start.21) | collective-permute-done | bytes 32800 | tf_op jit(solution)/shard_map/ppermute | solution.py:320
  (46 shorter events, 14.2 us)
Async XLA Ops:
  5.6 9.5 %collective-permute-start.2 = (f32[8,3584]{1,0:T(8,128)S(1)}, f32[8,3584]{1,0:T(8,128)S(1)}, u32[]{:S(2)}, u32[]{:S(2)}) collective-permute-start(f32[8,3584]{1,0:T(8,128)S(1)} %get-tuple-element.34), channel_id=1, source_target_pairs={{0,4},{4,0},{8,12},{12,8},{16,20},{20,16},{24,28},{28,24},{1,5},{5... | collective-permute-start | bytes 344072 | tf_op jit(solution)/shard_map/ppermute | solution.py:309
  8.6 7.7 %collective-permute-start = (f32[8,3584]{1,0:T(8,128)S(1)}, f32[8,3584]{1,0:T(8,128)S(1)}, u32[]{:S(2)}, u32[]{:S(2)}) collective-permute-start(f32[8,3584]{1,0:T(8,128)S(1)} %get-tuple-element.32), channel_id=1, source_target_pairs={{0,12},{4,8},{8,4},{12,0},{16,28},{20,24},{24,20},{28,16},{1,13},{... | collective-permute-start | bytes 344072 | tf_op jit(solution)/shard_map/ppermute | solution.py:309
  10.2 6.5 %collective-permute-start.1 = (f32[8,3584]{1,0:T(8,128)S(1)}, f32[8,3584]{1,0:T(8,128)S(1)}, u32[]{:S(2)}, u32[]{:S(2)}) collective-permute-start(f32[8,3584]{1,0:T(8,128)S(1)} %get-tuple-element.33), channel_id=1, source_target_pairs={{0,8},{4,12},{8,0},{12,4},{16,24},{20,28},{24,16},{28,20},{1,9},{5... | collective-permute-start | bytes 344072 | tf_op jit(solution)/shard_map/ppermute | solution.py:309
  10.6 9.1 %collective-permute-start.6 = (f32[8,3584]{1,0:T(8,128)S(1)}, f32[8,3584]{1,0:T(8,128)S(1)}, u32[]{:S(2)}, u32[]{:S(2)}) collective-permute-start(f32[8,3584]{1,0:T(8,128)S(1)} %get-tuple-element.40), channel_id=1, source_target_pairs={{0,4},{4,0},{8,12},{12,8},{16,20},{20,16},{24,28},{28,24},{1,5},{5... | collective-permute-start | bytes 344072 | tf_op jit(solution)/shard_map/ppermute | solution.py:309
  12.6 9.0 %collective-permute-start.4 = (f32[8,3584]{1,0:T(8,128)S(1)}, f32[8,3584]{1,0:T(8,128)S(1)}, u32[]{:S(2)}, u32[]{:S(2)}) collective-permute-start(f32[8,3584]{1,0:T(8,128)S(1)} %get-tuple-element.38), channel_id=1, source_target_pairs={{0,12},{4,8},{8,4},{12,0},{16,28},{20,24},{24,20},{28,16},{1,13},{... | collective-permute-start | bytes 344072 | tf_op jit(solution)/shard_map/ppermute | solution.py:309
  15.1 7.0 %collective-permute-start.5 = (f32[8,3584]{1,0:T(8,128)S(1)}, f32[8,3584]{1,0:T(8,128)S(1)}, u32[]{:S(2)}, u32[]{:S(2)}) collective-permute-start(f32[8,3584]{1,0:T(8,128)S(1)} %get-tuple-element.39), channel_id=1, source_target_pairs={{0,8},{4,12},{8,0},{12,4},{16,24},{20,28},{24,16},{28,20},{1,9},{5... | collective-permute-start | bytes 344072 | tf_op jit(solution)/shard_map/ppermute | solution.py:309
  16.7 9.8 %collective-permute-start.3 = (f32[8,3584]{1,0:T(8,128)S(1)}, f32[8,3584]{1,0:T(8,128)S(1)}, u32[]{:S(2)}, u32[]{:S(2)}) collective-permute-start(f32[8,3584]{1,0:T(8,128)S(1)} %add_add_fusion.1), channel_id=1, source_target_pairs={{0,16},{4,20},{8,24},{12,28},{16,0},{20,4},{24,8},{28,12},{1,17},{... | collective-permute-start | bytes 344072 | tf_op jit(solution)/shard_map/ppermute | solution.py:309
  22.2 8.2 %collective-permute-start.10 = (f32[8,3584]{1,0:T(8,128)S(1)}, f32[8,3584]{1,0:T(8,128)S(1)}, u32[]{:S(2)}, u32[]{:S(2)}) collective-permute-start(f32[8,3584]{1,0:T(8,128)S(1)} %add_add_fusion.after_ref), channel_id=1, source_target_pairs={{0,16},{4,20},{8,24},{12,28},{16,0},{20,4},{24,8},{28,12},{1,17},{... | collective-permute-start | bytes 344072 | tf_op jit(solution)/shard_map/ppermute | solution.py:309
  26.5 7.4 %collective-permute-start.7 = (f32[8,3584]{1,0:T(8,128)S(1)}, f32[8,3584]{1,0:T(8,128)S(1)}, u32[]{:S(2)}, u32[]{:S(2)}) collective-permute-start(f32[8,3584]{1,0:T(8,128)S(1)} %add_multiply_fusion.1.s0), channel_id=1, source_target_pairs={{0,12},{4,8},{8,4},{12,0},{16,28},{20,24},{24,20},{28,16},{1,13},{... | collective-permute-start | bytes 344072 | tf_op jit(solution)/shard_map/ppermute | solution.py:309
  29.7 5.4 %collective-permute-start.8 = (f32[8,3584]{1,0:T(8,128)S(1)}, f32[8,3584]{1,0:T(8,128)S(1)}, u32[]{:S(2)}, u32[]{:S(2)}) collective-permute-start(f32[8,3584]{1,0:T(8,128)S(1)} %add_multiply_fusion.1.s0), channel_id=1, source_target_pairs={{0,8},{4,12},{8,0},{12,4},{16,24},{20,28},{24,16},{28,20},{1,9},{5... | collective-permute-start | bytes 344072 | tf_op jit(solution)/shard_map/ppermute | solution.py:309
  29.7 6.5 %collective-permute-start.9 = (f32[8,3584]{1,0:T(8,128)S(1)}, f32[8,3584]{1,0:T(8,128)S(1)}, u32[]{:S(2)}, u32[]{:S(2)}) collective-permute-start(f32[8,3584]{1,0:T(8,128)S(1)} %add_multiply_fusion.1.s0), channel_id=1, source_target_pairs={{0,4},{4,0},{8,12},{12,8},{16,20},{20,16},{24,28},{28,24},{1,5},{5... | collective-permute-start | bytes 344072 | tf_op jit(solution)/shard_map/ppermute | solution.py:309
  30.4 8.2 %collective-permute-start.11 = (f32[8,3584]{1,0:T(8,128)S(1)}, f32[8,3584]{1,0:T(8,128)S(1)}, u32[]{:S(2)}, u32[]{:S(2)}) collective-permute-start(f32[8,3584]{1,0:T(8,128)S(1)} %add_multiply_fusion.s0), channel_id=1, source_target_pairs={{0,12},{4,8},{8,4},{12,0},{16,28},{20,24},{24,20},{28,16},{1,13},{... | collective-permute-start | bytes 344072 | tf_op jit(solution)/shard_map/ppermute | solution.py:309
  33.3 6.2 %collective-permute-start.12 = (f32[8,3584]{1,0:T(8,128)S(1)}, f32[8,3584]{1,0:T(8,128)S(1)}, u32[]{:S(2)}, u32[]{:S(2)}) collective-permute-start(f32[8,3584]{1,0:T(8,128)S(1)} %add_multiply_fusion.s0), channel_id=1, source_target_pairs={{0,8},{4,12},{8,0},{12,4},{16,24},{20,28},{24,16},{28,20},{1,9},{5... | collective-permute-start | bytes 344072 | tf_op jit(solution)/shard_map/ppermute | solution.py:309
  33.9 5.8 %collective-permute-start.13 = (f32[8,3584]{1,0:T(8,128)S(1)}, f32[8,3584]{1,0:T(8,128)S(1)}, u32[]{:S(2)}, u32[]{:S(2)}) collective-permute-start(f32[8,3584]{1,0:T(8,128)S(1)} %add_multiply_fusion.s0), channel_id=1, source_target_pairs={{0,4},{4,0},{8,12},{12,8},{16,20},{20,16},{24,28},{28,24},{1,5},{5... | collective-permute-start | bytes 344072 | tf_op jit(solution)/shard_map/ppermute | solution.py:309
  40.4 1.2 %collective-permute-start.14 = (f32[16,256]{1,0:T(8,128)S(1)}, f32[16,256]{1,0:T(8,128)S(1)}, u32[]{:S(2)}, u32[]{:S(2)}) collective-permute-start(f32[16,256]{1,0:T(8,128)S(1)} %get-tuple-element.50), channel_id=1, source_target_pairs={{0,1},{1,0},{2,3},{3,2},{4,5},{5,4},{6,7},{7,6},{8,9},{9,8},{10,11... | collective-permute-start | bytes 49160 | tf_op jit(solution)/shard_map/ppermute | solution.py:314
  41.6 3.3 %collective-permute-start.15 = (f32[16,512]{1,0:T(8,128)S(1)}, f32[16,512]{1,0:T(8,128)S(1)}, u32[]{:S(2)}, u32[]{:S(2)}) collective-permute-start(f32[16,512]{1,0:T(8,128)S(1)} %pad_add_fusion.mine_ref), channel_id=1, source_target_pairs={{0,3},{1,2},{2,1},{3,0},{4,7},{5,6},{6,5},{7,4},{8,11},{9,10},{10,... | collective-permute-start | bytes 98312 | tf_op jit(solution)/shard_map/ppermute | solution.py:320
  45.4 5.7 %collective-permute-start.17 = (f32[2,16,512]{2,1,0:T(8,128)S(1)}, f32[2,16,512]{2,1,0:T(8,128)S(1)}, u32[]{:S(2)}, u32[]{:S(2)}) collective-permute-start(f32[2,16,512]{2,1,0:T(8,128)S(1)} %get-tuple-element.54), channel_id=1, source_target_pairs={{0,12},{4,8},{8,4},{12,0},{16,28},{20,24},{24,20},{28,16},{1,13},{... | collective-permute-start | bytes 196616 | tf_op jit(solution)/shard_map/ppermute | solution.py:309
  46.8 4.5 %collective-permute-start.18 = (f32[2,16,512]{2,1,0:T(8,128)S(1)}, f32[2,16,512]{2,1,0:T(8,128)S(1)}, u32[]{:S(2)}, u32[]{:S(2)}) collective-permute-start(f32[2,16,512]{2,1,0:T(8,128)S(1)} %get-tuple-element.55), channel_id=1, source_target_pairs={{0,8},{4,12},{8,0},{12,4},{16,24},{20,28},{24,16},{28,20},{1,9},{5... | collective-permute-start | bytes 196616 | tf_op jit(solution)/shard_map/ppermute | solution.py:309
  47.6 4.3 %collective-permute-start.19 = (f32[2,16,512]{2,1,0:T(8,128)S(1)}, f32[2,16,512]{2,1,0:T(8,128)S(1)}, u32[]{:S(2)}, u32[]{:S(2)}) collective-permute-start(f32[2,16,512]{2,1,0:T(8,128)S(1)} %get-tuple-element.56), channel_id=1, source_target_pairs={{0,4},{4,0},{8,12},{12,8},{16,20},{20,16},{24,28},{28,24},{1,5},{5... | collective-permute-start | bytes 196616 | tf_op jit(solution)/shard_map/ppermute | solution.py:309
  48.9 1.2 %collective-permute-start.16 = (f32[16,256]{1,0:T(8,128)S(1)}, f32[16,256]{1,0:T(8,128)S(1)}, u32[]{:S(2)}, u32[]{:S(2)}) collective-permute-start(f32[16,256]{1,0:T(8,128)S(1)} %slice_add_fusion.mine_ref), channel_id=1, source_target_pairs={{0,1},{1,0},{2,3},{3,2},{4,5},{5,4},{6,7},{7,6},{8,9},{9,8},{10,11... | collective-permute-start | bytes 49160 | tf_op jit(solution)/shard_map/ppermute | solution.py:314
  51.9 5.5 %collective-permute-start.20 = (f32[16,512]{1,0:T(8,128)S(1)}, f32[16,512]{1,0:T(8,128)S(1)}, u32[]{:S(2)}, u32[]{:S(2)}) collective-permute-start(f32[16,512]{1,0:T(8,128)S(1)} %get-tuple-element.57), channel_id=1, source_target_pairs={{0,19},{1,18},{2,17},{3,16},{4,23},{5,22},{6,21},{7,20},{8,27},{9,... | collective-permute-start | bytes 98312 | tf_op jit(solution)/shard_map/ppermute | solution.py:320
  52.8 5.8 %collective-permute-start.21 = (f32[16,512]{1,0:T(8,128)S(1)}, f32[16,512]{1,0:T(8,128)S(1)}, u32[]{:S(2)}, u32[]{:S(2)}) collective-permute-start(f32[16,512]{1,0:T(8,128)S(1)} %get-tuple-element.57), channel_id=1, source_target_pairs={{0,16},{1,17},{2,18},{3,19},{4,20},{5,21},{6,22},{7,23},{8,24},{9,... | collective-permute-start | bytes 98312 | tf_op jit(solution)/shard_map/ppermute | solution.py:320
  54.9 3.7 %collective-permute-start.22 = (f32[16,512]{1,0:T(8,128)S(1)}, f32[16,512]{1,0:T(8,128)S(1)}, u32[]{:S(2)}, u32[]{:S(2)}) collective-permute-start(f32[16,512]{1,0:T(8,128)S(1)} %get-tuple-element.58.near_ref), channel_id=1, source_target_pairs={{0,3},{1,2},{2,1},{3,0},{4,7},{5,6},{6,5},{7,4},{8,11},{9,10},{10,... | collective-permute-start | bytes 98312 | tf_op jit(solution)/shard_map/ppermute | solution.py:320
  58.9 1.5 %collective-permute-start.23 = (f32[32,1024]{1,0:T(8,128)S(1)}, f32[32,1024]{1,0:T(8,128)S(1)}, u32[]{:S(2)}, u32[]{:S(2)}) collective-permute-start(f32[32,1024]{1,0:T(8,128)S(1)} %shard_map.87), channel_id=1, source_target_pairs={{0,1},{1,0},{2,3},{3,2},{4,5},{5,4},{6,7},{7,6},{8,9},{9,8},{10,11... | collective-permute-start | bytes 393224 | tf_op jit(solution)/shard_map/ppermute | solution.py:314
  (2 other events, 28.7 us)

commit v8 on v6

--- a/solution.py
+++ b/solution.py
@@ -360,7 +360,9 @@
         own = (summed + came) * (1.0 / replicas)
         return [own] + swap_square([own] * SQUARE, SUMS_AWAY)
 
-    early = terms[0] + sum(swap_square(terms, TERMS_AWAY))
+    got = swap_square(terms, TERMS_AWAY)
+    got[1], late_terms = lax.optimization_barrier((got[1], late_terms))
+    early = terms[0] + sum(got)
     early_came = swap_dp(early, SQUARE)
     late = late_terms[0] + sum(swap_square(late_terms, TERMS_AWAY))
     late_came = swap_dp(late, SQUARE)

time: 61.1 us -> 61.1 us (level)
  starting transfers between devices: 30.9 us -> 32.5 us
  waiting for transfers between devices: 15.5 us -> 13.9 us
    ppermute x17, waiting for transfers between devices: 9.72 us -> 8.45 us  [swap_dp(): return lax.ppermute(x, 'dp', [(i, i ^ m) for i in range(n)])]
    ppermute x17, starting transfers between devices: 25.2 us -> 26.4 us  [swap_dp(): return lax.ppermute(x, 'dp', [(i, i ^ m) for i in range(n)])]
  transfers between devices with their start and end apart: 24 -> 24, of which waited for: 18 -> 17; matrix products, arithmetic and copies ran while one was open for 0% -> 0% of each run, Pallas kernels for 11% -> 11%
where the time goes in v8:
time: 61.1 us; the launch traced here: 60.9 us
  starting transfers between devices  32.5 us (53%)
  waiting for transfers between devices  13.9 us (23%)
  Pallas kernels  13.7 us (22%)
  between operations  0.72 us (1%)
    ppermute x17, starting transfers between devices, swap_dp(): return lax.ppermute(x, 'dp', [(i, i ^ m) for i in range(n)])  26.4 us
    ppermute x17, waiting for transfers between devices, swap_dp(): return lax.ppermute(x, 'dp', [(i, i ^ m) for i in range(n)])  8.45 us
    ppermute x4, starting transfers between devices, swap_both(): return lax.ppermute(x, ('dp', 'tensor'), pairs)  5.2 us
    pallas_call x1, Pallas kernels, on_device(): call(first_term_kernel, [(rows, first)] * SQUARE + [(rank, 2 * tokens), (...  4.97 us
    ppermute x4, waiting for transfers between devices, swap_both(): return lax.ppermute(x, ('dp', 'tensor'), pairs)  2.91 us
    ppermute x3, waiting for transfers between devices, swap_tensor(): return lax.ppermute(x, 'tensor', [(i, i ^ m) for i in range(n)])  2.53 us
    pallas_call x1, Pallas kernels, on_device(): call(feedback_kernel, [(rank, first), (rank, rest)], [VMEM_SPEC] * 2 + [A...  1.91 us
    pallas_call x1, Pallas kernels, on_device(): call(functools.partial(basis_kernel, norm_scale=norm_scale), [(rank, unit...  1.59 us
  transfers between devices with their start and end apart: 24, of which 17 were waited for; matrix products, arithmetic and copies ran while one was open for 0% of the time, Pallas kernels for 11%

profile of v8, /device:TPU:0, one launch (start us, length us, event | category | flops | bytes accessed | tf_op | source)
XLA Modules:
  0.0 60.9 jit_solution(5075500738272630367)
XLA Ops:
  0.6 5.0 %shard_map.77 = (f32[8,3584]{1,0:T(8,128)S(1)}, f32[8,3584]{1,0:T(8,128)S(1)}, f32[8,3584]{1,0:T(8,128)S(1)}, f32[8,3584]{1,0:T(8,128)S(1)}, f32[32,256]{1,0:T(8...) custom-call(f32[32,8192]{1,0:T(8,128)} %bitcast.4, bf16[128,8192]{1,0:T(8,128)(2,1)} %o_ref.1, ...), custom_call_target="tpu_custom_call" | custom-call | flops 192937984 | bytes 9371648 | tf_op jit(solution)/shard_map/pallas_call | solution.py:340
  5.6 3.1 %collective-permute-start.1 = (f32[8,3584]{1,0:T(8,128)S(1)}, f32[8,3584]{1,0:T(8,128)S(1)}, u32[]{:S(2)}, u32[]{:S(2)}) collective-permute-start(f32[8,3584]{1,0:T(8,128)S(1)} %get-tuple-element.38), channel_id=1, source_target_pairs={{0,8},{4,12},{8,0},{12,4},{16,24},{20,28},{24,16},{28,20},{1,9},{5... | collective-permute-start | bytes 344072 | tf_op jit(solution)/shard_map/ppermute | solution.py:316
  8.7 1.5 %collective-permute-start.2 = (f32[8,3584]{1,0:T(8,128)S(1)}, f32[8,3584]{1,0:T(8,128)S(1)}, u32[]{:S(2)}, u32[]{:S(2)}) collective-permute-start(f32[8,3584]{1,0:T(8,128)S(1)} %get-tuple-element.46), channel_id=1, source_target_pairs={{0,4},{4,0},{8,12},{12,8},{16,20},{20,16},{24,28},{28,24},{1,5},{5... | collective-permute-start | bytes 344072 | tf_op jit(solution)/shard_map/ppermute | solution.py:316
  10.7 1.6 %collective-permute-done.1 = f32[8,3584]{1,0:T(8,128)S(1)} collective-permute-done((f32[8,3584]{1,0:T(8,128)S(1)}, f32[8,3584]{1,0:T(8,128)S(1)}, u32[]{:S(2)}, u32[]{:S(2)}) %collective-permute-start.1) | collective-permute-done | bytes 114720 | tf_op jit(solution)/shard_map/ppermute | solution.py:316
  12.2 1.4 %collective-permute-start.6 = (f32[8,3584]{1,0:T(8,128)S(1)}, f32[8,3584]{1,0:T(8,128)S(1)}, u32[]{:S(2)}, u32[]{:S(2)}) collective-permute-start(f32[8,3584]{1,0:T(8,128)S(1)} %get-tuple-element.50), channel_id=1, source_target_pairs={{0,4},{4,0},{8,12},{12,8},{16,20},{20,16},{24,28},{28,24},{1,5},{5... | collective-permute-start | bytes 344072 | tf_op jit(solution)/shard_map/ppermute | solution.py:316
  13.7 2.5 %collective-permute-start.4 = (f32[8,3584]{1,0:T(8,128)S(1)}, f32[8,3584]{1,0:T(8,128)S(1)}, u32[]{:S(2)}, u32[]{:S(2)}) collective-permute-start(f32[8,3584]{1,0:T(8,128)S(1)} %get-tuple-element.48), channel_id=1, source_target_pairs={{0,12},{4,8},{8,4},{12,0},{16,28},{20,24},{24,20},{28,16},{1,13},{... | collective-permute-start | bytes 344072 | tf_op jit(solution)/shard_map/ppermute | solution.py:316
  16.2 1.4 %collective-permute-done.2 = f32[8,3584]{1,0:T(8,128)S(1)} collective-permute-done((f32[8,3584]{1,0:T(8,128)S(1)}, f32[8,3584]{1,0:T(8,128)S(1)}, u32[]{:S(2)}, u32[]{:S(2)}) %collective-permute-start.2) | collective-permute-done | bytes 114720 | tf_op jit(solution)/shard_map/ppermute | solution.py:316
  17.6 2.7 %collective-permute-start.3 = (f32[8,3584]{1,0:T(8,128)S(1)}, f32[8,3584]{1,0:T(8,128)S(1)}, u32[]{:S(2)}, u32[]{:S(2)}) collective-permute-start(f32[8,3584]{1,0:T(8,128)S(1)} %add_add_fusion.1), channel_id=1, source_target_pairs={{0,16},{4,20},{8,24},{12,28},{16,0},{20,4},{24,8},{28,12},{1,17},{... | collective-permute-start | bytes 344072 | tf_op jit(solution)/shard_map/ppermute | solution.py:316
  21.5 3.0 %collective-permute-start.10 = (f32[8,3584]{1,0:T(8,128)S(1)}, f32[8,3584]{1,0:T(8,128)S(1)}, u32[]{:S(2)}, u32[]{:S(2)}) collective-permute-start(f32[8,3584]{1,0:T(8,128)S(1)} %add_add_fusion.after_ref), channel_id=1, source_target_pairs={{0,16},{4,20},{8,24},{12,28},{16,0},{20,4},{24,8},{28,12},{1,17},{... | collective-permute-start | bytes 344072 | tf_op jit(solution)/shard_map/ppermute | solution.py:316
  24.5 1.9 %shard_map.79 = (f32[32,3584]{1,0:T(8,128)S(1)}, f32[32,3584]{1,0:T(8,128)S(1)}) custom-call(f32[32,8192]{1,0:T(8,128)S(1)} %bitcast.5, f32[32,7168]{1,0:T(8,128)S(1)} %bitcast.7, f32[8,3584]{1,0:T(8,128)S(1)} %add_add_fusion.after_ref), custom_call_target="tpu_custom_call" | custom-call | flops 31457280 | bytes 1966080 | tf_op jit(solution)/shard_map/pallas_call | solution.py:369
  26.4 4.0 %collective-permute-start.7 = (f32[8,3584]{1,0:T(8,128)S(1)}, f32[8,3584]{1,0:T(8,128)S(1)}, u32[]{:S(2)}, u32[]{:S(2)}) collective-permute-start(f32[8,3584]{1,0:T(8,128)S(1)} %add_multiply_fusion.1.s0), channel_id=1, source_target_pairs={{0,12},{4,8},{8,4},{12,0},{16,28},{20,24},{24,20},{28,16},{1,13},{... | collective-permute-start | bytes 344072 | tf_op jit(solution)/shard_map/ppermute | solution.py:316
  31.1 2.9 %collective-permute-start.11 = (f32[8,3584]{1,0:T(8,128)S(1)}, f32[8,3584]{1,0:T(8,128)S(1)}, u32[]{:S(2)}, u32[]{:S(2)}) collective-permute-start(f32[8,3584]{1,0:T(8,128)S(1)} %add_multiply_fusion.s0), channel_id=1, source_target_pairs={{0,12},{4,8},{8,4},{12,0},{16,28},{20,24},{24,20},{28,16},{1,13},{... | collective-permute-start | bytes 344072 | tf_op jit(solution)/shard_map/ppermute | solution.py:316
  34.6 1.1 %collective-permute-start.13 = (f32[8,3584]{1,0:T(8,128)S(1)}, f32[8,3584]{1,0:T(8,128)S(1)}, u32[]{:S(2)}, u32[]{:S(2)}) collective-permute-start(f32[8,3584]{1,0:T(8,128)S(1)} %add_multiply_fusion.s0), channel_id=1, source_target_pairs={{0,4},{4,0},{8,12},{12,8},{16,20},{20,16},{24,28},{28,24},{1,5},{5... | collective-permute-start | bytes 344072 | tf_op jit(solution)/shard_map/ppermute | solution.py:316
  36.9 1.3 %shard_map.80 = (f32[32,3584]{1,0:T(8,128)S(1)}, f32[32,256]{1,0:T(8,128)S(1)}, f32[32,128]{1,0:T(8,128)S(1)}) custom-call(f32[8,3584]{1,0:T(8,128)S(1)} %add_multiply_fusion.1.s0, f32[8,3584]{1,0:T(8,128)S(1)} %collective-permute-done.7.s1, f32[8,3584]{1,0:T(8,128)S(1)} %collective-permute-done.8.s2, f32[8,3584]{1,0:T(8,128)S(1)} %collective-permute-done.9.s3, ...), custom_call_target="tpu_custom_call" | custom-call | flops 117440512 | bytes 2293760 | tf_op jit(solution)/shard_map/pallas_call | solution.py:381
  41.3 1.3 %collective-permute-start.15 = (f32[16,512]{1,0:T(8,128)S(1)}, f32[16,512]{1,0:T(8,128)S(1)}, u32[]{:S(2)}, u32[]{:S(2)}) collective-permute-start(f32[16,512]{1,0:T(8,128)S(1)} %pad_add_fusion.mine_ref), channel_id=1, source_target_pairs={{0,3},{1,2},{2,1},{3,0},{4,7},{5,6},{6,5},{7,4},{8,11},{9,10},{10,... | collective-permute-start | bytes 98312 | tf_op jit(solution)/shard_map/ppermute | solution.py:327
  42.6 2.0 %collective-permute-done.15.got_ref = f32[16,512]{1,0:T(8,128)S(1)} collective-permute-done((f32[16,512]{1,0:T(8,128)S(1)}, f32[16,512]{1,0:T(8,128)S(1)}, u32[]{:S(2)}, u32[]{:S(2)}) %collective-permute-start.15) | collective-permute-done | bytes 32800 | tf_op jit(solution)/shard_map/ppermute | solution.py:327
  45.1 1.9 %collective-permute-start.17 = (f32[2,16,512]{2,1,0:T(8,128)S(1)}, f32[2,16,512]{2,1,0:T(8,128)S(1)}, u32[]{:S(2)}, u32[]{:S(2)}) collective-permute-start(f32[2,16,512]{2,1,0:T(8,128)S(1)} %get-tuple-element.64), channel_id=1, source_target_pairs={{0,12},{4,8},{8,4},{12,0},{16,28},{20,24},{24,20},{28,16},{1,13},{... | collective-permute-start | bytes 196616 | tf_op jit(solution)/shard_map/ppermute | solution.py:316
  47.6 1.0 %collective-permute-start.19 = (f32[2,16,512]{2,1,0:T(8,128)S(1)}, f32[2,16,512]{2,1,0:T(8,128)S(1)}, u32[]{:S(2)}, u32[]{:S(2)}) collective-permute-start(f32[2,16,512]{2,1,0:T(8,128)S(1)} %get-tuple-element.66), channel_id=1, source_target_pairs={{0,4},{4,0},{8,12},{12,8},{16,20},{20,16},{24,28},{28,24},{1,5},{5... | collective-permute-start | bytes 196616 | tf_op jit(solution)/shard_map/ppermute | solution.py:316
  48.6 1.2 %collective-permute-done.16.got_ref = f32[16,256]{1,0:T(8,128)S(1)} collective-permute-done((f32[16,256]{1,0:T(8,128)S(1)}, f32[16,256]{1,0:T(8,128)S(1)}, u32[]{:S(2)}, u32[]{:S(2)}) %collective-permute-start.16) | collective-permute-done | bytes 16416 | tf_op jit(solution)/shard_map/ppermute | solution.py:321
  52.4 2.3 %collective-permute-start.21 = (f32[16,512]{1,0:T(8,128)S(1)}, f32[16,512]{1,0:T(8,128)S(1)}, u32[]{:S(2)}, u32[]{:S(2)}) collective-permute-start(f32[16,512]{1,0:T(8,128)S(1)} %get-tuple-element.67), channel_id=1, source_target_pairs={{0,16},{1,17},{2,18},{3,19},{4,20},{5,21},{6,22},{7,23},{8,24},{9,... | collective-permute-start | bytes 98312 | tf_op jit(solution)/shard_map/ppermute | solution.py:327
  54.7 1.1 %collective-permute-start.22 = (f32[16,512]{1,0:T(8,128)S(1)}, f32[16,512]{1,0:T(8,128)S(1)}, u32[]{:S(2)}, u32[]{:S(2)}) collective-permute-start(f32[16,512]{1,0:T(8,128)S(1)} %get-tuple-element.68.near_ref), channel_id=1, source_target_pairs={{0,3},{1,2},{2,1},{3,0},{4,7},{5,6},{6,5},{7,4},{8,11},{9,10},{10,... | collective-permute-start | bytes 98312 | tf_op jit(solution)/shard_map/ppermute | solution.py:327
  55.8 1.6 %shard_map.84 = (f32[32,7168]{1,0:T(8,128)}, f32[32,1024]{1,0:T(8,128)S(1)}) custom-call(f32[32,3584]{1,0:T(8,128)S(1)} %get-tuple-element.54.p_ref, f32[32,3584]{1,0:T(8,128)S(1)} %get-tuple-element.57.p_ref.r_ref, f32[32,128]{1,0:T(8,128)S(1)} %shard_map.83.l_ref.after_ref, f32[32,8192]{1,0:T(8,128)S(1)} %bitcast.6), custom_call_target="tpu_custom_call" | custom-call | flops 14680064 | bytes 1835008 | tf_op jit(solution)/shard_map/pallas_call | solution.py:426
  59.1 0.9 %collective-permute-done.23.u_ref = f32[16,1024]{1,0:T(8,128)S(1)} collective-permute-done((f32[16,1024]{1,0:T(8,128)S(1)}, f32[16,1024]{1,0:T(8,128)S(1)}, u32[]{:S(2)}, u32[]{:S(2)}) %collective-permute-start.23) | collective-permute-done | bytes 65568 | tf_op jit(solution)/shard_map/ppermute | solution.py:321
  60.0 0.9 %shard_map.88 = f32[32,1024]{1,0:T(8,128)} custom-call(f32[16,1024]{1,0:T(8,128)S(1)} %shard_map.87.t_ref, f32[16,1024]{1,0:T(8,128)S(1)} %collective-permute-done.23.u_ref, f32[32,128]{1,0:T(8,128)S(1)} %shard_map.83.l_ref.after_ref, f32[32,1024]{1,0:T(8,128)S(1)} %get-tuple-element.69.after_ref.fix_ref), custom_call_target="tpu_custom_call" | custom-call | flops 2097152 | bytes 393216 | tf_op jit(solution)/shard_map/pallas_call | solution.py:443
  (46 shorter events, 12.8 us)
Async XLA Ops:
  5.6 6.6 %collective-permute-start.1 = (f32[8,3584]{1,0:T(8,128)S(1)}, f32[8,3584]{1,0:T(8,128)S(1)}, u32[]{:S(2)}, u32[]{:S(2)}) collective-permute-start(f32[8,3584]{1,0:T(8,128)S(1)} %get-tuple-element.38), channel_id=1, source_target_pairs={{0,8},{4,12},{8,0},{12,4},{16,24},{20,28},{24,16},{28,20},{1,9},{5... | collective-permute-start | bytes 344072 | tf_op jit(solution)/shard_map/ppermute | solution.py:316
  8.7 8.9 %collective-permute-start.2 = (f32[8,3584]{1,0:T(8,128)S(1)}, f32[8,3584]{1,0:T(8,128)S(1)}, u32[]{:S(2)}, u32[]{:S(2)}) collective-permute-start(f32[8,3584]{1,0:T(8,128)S(1)} %get-tuple-element.46), channel_id=1, source_target_pairs={{0,4},{4,0},{8,12},{12,8},{16,20},{20,16},{24,28},{28,24},{1,5},{5... | collective-permute-start | bytes 344072 | tf_op jit(solution)/shard_map/ppermute | solution.py:316
  10.2 7.4 %collective-permute-start = (f32[8,3584]{1,0:T(8,128)S(1)}, f32[8,3584]{1,0:T(8,128)S(1)}, u32[]{:S(2)}, u32[]{:S(2)}) collective-permute-start(f32[8,3584]{1,0:T(8,128)S(1)} %get-tuple-element.37), channel_id=1, source_target_pairs={{0,12},{4,8},{8,4},{12,0},{16,28},{20,24},{24,20},{28,16},{1,13},{... | collective-permute-start | bytes 344072 | tf_op jit(solution)/shard_map/ppermute | solution.py:316
  12.2 8.0 %collective-permute-start.6 = (f32[8,3584]{1,0:T(8,128)S(1)}, f32[8,3584]{1,0:T(8,128)S(1)}, u32[]{:S(2)}, u32[]{:S(2)}) collective-permute-start(f32[8,3584]{1,0:T(8,128)S(1)} %get-tuple-element.50), channel_id=1, source_target_pairs={{0,4},{4,0},{8,12},{12,8},{16,20},{20,16},{24,28},{28,24},{1,5},{5... | collective-permute-start | bytes 344072 | tf_op jit(solution)/shard_map/ppermute | solution.py:316
  13.7 7.2 %collective-permute-start.4 = (f32[8,3584]{1,0:T(8,128)S(1)}, f32[8,3584]{1,0:T(8,128)S(1)}, u32[]{:S(2)}, u32[]{:S(2)}) collective-permute-start(f32[8,3584]{1,0:T(8,128)S(1)} %get-tuple-element.48), channel_id=1, source_target_pairs={{0,12},{4,8},{8,4},{12,0},{16,28},{20,24},{24,20},{28,16},{1,13},{... | collective-permute-start | bytes 344072 | tf_op jit(solution)/shard_map/ppermute | solution.py:316
  16.2 5.2 %collective-permute-start.5 = (f32[8,3584]{1,0:T(8,128)S(1)}, f32[8,3584]{1,0:T(8,128)S(1)}, u32[]{:S(2)}, u32[]{:S(2)}) collective-permute-start(f32[8,3584]{1,0:T(8,128)S(1)} %get-tuple-element.49), channel_id=1, source_target_pairs={{0,8},{4,12},{8,0},{12,4},{16,24},{20,28},{24,16},{28,20},{1,9},{5... | collective-permute-start | bytes 344072 | tf_op jit(solution)/shard_map/ppermute | solution.py:316
  17.6 8.8 %collective-permute-start.3 = (f32[8,3584]{1,0:T(8,128)S(1)}, f32[8,3584]{1,0:T(8,128)S(1)}, u32[]{:S(2)}, u32[]{:S(2)}) collective-permute-start(f32[8,3584]{1,0:T(8,128)S(1)} %add_add_fusion.1), channel_id=1, source_target_pairs={{0,16},{4,20},{8,24},{12,28},{16,0},{20,4},{24,8},{28,12},{1,17},{... | collective-permute-start | bytes 344072 | tf_op jit(solution)/shard_map/ppermute | solution.py:316
  21.5 9.6 %collective-permute-start.10 = (f32[8,3584]{1,0:T(8,128)S(1)}, f32[8,3584]{1,0:T(8,128)S(1)}, u32[]{:S(2)}, u32[]{:S(2)}) collective-permute-start(f32[8,3584]{1,0:T(8,128)S(1)} %add_add_fusion.after_ref), channel_id=1, source_target_pairs={{0,16},{4,20},{8,24},{12,28},{16,0},{20,4},{24,8},{28,12},{1,17},{... | collective-permute-start | bytes 344072 | tf_op jit(solution)/shard_map/ppermute | solution.py:316
  26.4 8.1 %collective-permute-start.7 = (f32[8,3584]{1,0:T(8,128)S(1)}, f32[8,3584]{1,0:T(8,128)S(1)}, u32[]{:S(2)}, u32[]{:S(2)}) collective-permute-start(f32[8,3584]{1,0:T(8,128)S(1)} %add_multiply_fusion.1.s0), channel_id=1, source_target_pairs={{0,12},{4,8},{8,4},{12,0},{16,28},{20,24},{24,20},{28,16},{1,13},{... | collective-permute-start | bytes 344072 | tf_op jit(solution)/shard_map/ppermute | solution.py:316
  30.4 5.7 %collective-permute-start.8 = (f32[8,3584]{1,0:T(8,128)S(1)}, f32[8,3584]{1,0:T(8,128)S(1)}, u32[]{:S(2)}, u32[]{:S(2)}) collective-permute-start(f32[8,3584]{1,0:T(8,128)S(1)} %add_multiply_fusion.1.s0), channel_id=1, source_target_pairs={{0,8},{4,12},{8,0},{12,4},{16,24},{20,28},{24,16},{28,20},{1,9},{5... | collective-permute-start | bytes 344072 | tf_op jit(solution)/shard_map/ppermute | solution.py:316
  30.4 6.5 %collective-permute-start.9 = (f32[8,3584]{1,0:T(8,128)S(1)}, f32[8,3584]{1,0:T(8,128)S(1)}, u32[]{:S(2)}, u32[]{:S(2)}) collective-permute-start(f32[8,3584]{1,0:T(8,128)S(1)} %add_multiply_fusion.1.s0), channel_id=1, source_target_pairs={{0,4},{4,0},{8,12},{12,8},{16,20},{20,16},{24,28},{28,24},{1,5},{5... | collective-permute-start | bytes 344072 | tf_op jit(solution)/shard_map/ppermute | solution.py:316
  31.1 7.1 %collective-permute-start.11 = (f32[8,3584]{1,0:T(8,128)S(1)}, f32[8,3584]{1,0:T(8,128)S(1)}, u32[]{:S(2)}, u32[]{:S(2)}) collective-permute-start(f32[8,3584]{1,0:T(8,128)S(1)} %add_multiply_fusion.s0), channel_id=1, source_target_pairs={{0,12},{4,8},{8,4},{12,0},{16,28},{20,24},{24,20},{28,16},{1,13},{... | collective-permute-start | bytes 344072 | tf_op jit(solution)/shard_map/ppermute | solution.py:316
  34.0 4.8 %collective-permute-start.12 = (f32[8,3584]{1,0:T(8,128)S(1)}, f32[8,3584]{1,0:T(8,128)S(1)}, u32[]{:S(2)}, u32[]{:S(2)}) collective-permute-start(f32[8,3584]{1,0:T(8,128)S(1)} %add_multiply_fusion.s0), channel_id=1, source_target_pairs={{0,8},{4,12},{8,0},{12,4},{16,24},{20,28},{24,16},{28,20},{1,9},{5... | collective-permute-start | bytes 344072 | tf_op jit(solution)/shard_map/ppermute | solution.py:316
  34.6 4.8 %collective-permute-start.13 = (f32[8,3584]{1,0:T(8,128)S(1)}, f32[8,3584]{1,0:T(8,128)S(1)}, u32[]{:S(2)}, u32[]{:S(2)}) collective-permute-start(f32[8,3584]{1,0:T(8,128)S(1)} %add_multiply_fusion.s0), channel_id=1, source_target_pairs={{0,4},{4,0},{8,12},{12,8},{16,20},{20,16},{24,28},{28,24},{1,5},{5... | collective-permute-start | bytes 344072 | tf_op jit(solution)/shard_map/ppermute | solution.py:316
  40.1 1.2 %collective-permute-start.14 = (f32[16,256]{1,0:T(8,128)S(1)}, f32[16,256]{1,0:T(8,128)S(1)}, u32[]{:S(2)}, u32[]{:S(2)}) collective-permute-start(f32[16,256]{1,0:T(8,128)S(1)} %get-tuple-element.60), channel_id=1, source_target_pairs={{0,1},{1,0},{2,3},{3,2},{4,5},{5,4},{6,7},{7,6},{8,9},{9,8},{10,11... | collective-permute-start | bytes 49160 | tf_op jit(solution)/shard_map/ppermute | solution.py:321
  41.3 3.3 %collective-permute-start.15 = (f32[16,512]{1,0:T(8,128)S(1)}, f32[16,512]{1,0:T(8,128)S(1)}, u32[]{:S(2)}, u32[]{:S(2)}) collective-permute-start(f32[16,512]{1,0:T(8,128)S(1)} %pad_add_fusion.mine_ref), channel_id=1, source_target_pairs={{0,3},{1,2},{2,1},{3,0},{4,7},{5,6},{6,5},{7,4},{8,11},{9,10},{10,... | collective-permute-start | bytes 98312 | tf_op jit(solution)/shard_map/ppermute | solution.py:327
  45.1 5.6 %collective-permute-start.17 = (f32[2,16,512]{2,1,0:T(8,128)S(1)}, f32[2,16,512]{2,1,0:T(8,128)S(1)}, u32[]{:S(2)}, u32[]{:S(2)}) collective-permute-start(f32[2,16,512]{2,1,0:T(8,128)S(1)} %get-tuple-element.64), channel_id=1, source_target_pairs={{0,12},{4,8},{8,4},{12,0},{16,28},{20,24},{24,20},{28,16},{1,13},{... | collective-permute-start | bytes 196616 | tf_op jit(solution)/shard_map/ppermute | solution.py:316
  47.0 4.3 %collective-permute-start.18 = (f32[2,16,512]{2,1,0:T(8,128)S(1)}, f32[2,16,512]{2,1,0:T(8,128)S(1)}, u32[]{:S(2)}, u32[]{:S(2)}) collective-permute-start(f32[2,16,512]{2,1,0:T(8,128)S(1)} %get-tuple-element.65), channel_id=1, source_target_pairs={{0,8},{4,12},{8,0},{12,4},{16,24},{20,28},{24,16},{28,20},{1,9},{5... | collective-permute-start | bytes 196616 | tf_op jit(solution)/shard_map/ppermute | solution.py:316
  47.6 4.3 %collective-permute-start.19 = (f32[2,16,512]{2,1,0:T(8,128)S(1)}, f32[2,16,512]{2,1,0:T(8,128)S(1)}, u32[]{:S(2)}, u32[]{:S(2)}) collective-permute-start(f32[2,16,512]{2,1,0:T(8,128)S(1)} %get-tuple-element.66), channel_id=1, source_target_pairs={{0,4},{4,0},{8,12},{12,8},{16,20},{20,16},{24,28},{28,24},{1,5},{5... | collective-permute-start | bytes 196616 | tf_op jit(solution)/shard_map/ppermute | solution.py:316
  48.6 1.2 %collective-permute-start.16 = (f32[16,256]{1,0:T(8,128)S(1)}, f32[16,256]{1,0:T(8,128)S(1)}, u32[]{:S(2)}, u32[]{:S(2)}) collective-permute-start(f32[16,256]{1,0:T(8,128)S(1)} %slice_add_fusion.mine_ref), channel_id=1, source_target_pairs={{0,1},{1,0},{2,3},{3,2},{4,5},{5,4},{6,7},{7,6},{8,9},{9,8},{10,11... | collective-permute-start | bytes 49160 | tf_op jit(solution)/shard_map/ppermute | solution.py:321
  51.9 5.5 %collective-permute-start.20 = (f32[16,512]{1,0:T(8,128)S(1)}, f32[16,512]{1,0:T(8,128)S(1)}, u32[]{:S(2)}, u32[]{:S(2)}) collective-permute-start(f32[16,512]{1,0:T(8,128)S(1)} %get-tuple-element.67), channel_id=1, source_target_pairs={{0,19},{1,18},{2,17},{3,16},{4,23},{5,22},{6,21},{7,20},{8,27},{9,... | collective-permute-start | bytes 98312 | tf_op jit(solution)/shard_map/ppermute | solution.py:327
  52.4 5.9 %collective-permute-start.21 = (f32[16,512]{1,0:T(8,128)S(1)}, f32[16,512]{1,0:T(8,128)S(1)}, u32[]{:S(2)}, u32[]{:S(2)}) collective-permute-start(f32[16,512]{1,0:T(8,128)S(1)} %get-tuple-element.67), channel_id=1, source_target_pairs={{0,16},{1,17},{2,18},{3,19},{4,20},{5,21},{6,22},{7,23},{8,24},{9,... | collective-permute-start | bytes 98312 | tf_op jit(solution)/shard_map/ppermute | solution.py:327
  54.7 3.6 %collective-permute-start.22 = (f32[16,512]{1,0:T(8,128)S(1)}, f32[16,512]{1,0:T(8,128)S(1)}, u32[]{:S(2)}, u32[]{:S(2)}) collective-permute-start(f32[16,512]{1,0:T(8,128)S(1)} %get-tuple-element.68.near_ref), channel_id=1, source_target_pairs={{0,3},{1,2},{2,1},{3,0},{4,7},{5,6},{6,5},{7,4},{8,11},{9,10},{10,... | collective-permute-start | bytes 98312 | tf_op jit(solution)/shard_map/ppermute | solution.py:327
  58.3 1.7 %collective-permute-start.23 = (f32[16,1024]{1,0:T(8,128)S(1)}, f32[16,1024]{1,0:T(8,128)S(1)}, u32[]{:S(2)}, u32[]{:S(2)}) collective-permute-start(f32[16,1024]{1,0:T(8,128)S(1)} %shard_map.87.t_ref), channel_id=1, source_target_pairs={{0,1},{1,0},{2,3},{3,2},{4,5},{5,4},{6,7},{7,6},{8,9},{9,8},{10,11... | collective-permute-start | bytes 196616 | tf_op jit(solution)/shard_map/ppermute | solution.py:321
  (2 other events, 28.5 us)
